TPU v7x, 32 devices: a whole 2x2x4 slice. The times are simulated.
32 devices in a mesh: orb: 8 (over y, x, core), grid: 4 (over z).
Axes of the slice: x: 2, y: 2, z: 4, core: 2. Of those that a mesh axis runs over, the one named last changes fastest.
Arguments:
- wavefunctions: float32 [64, 24, 1024], P('orb', 'grid'), may hold values from -2 to 2
- potential: float32 [24, 1024], P('grid'), may hold values from -3 to 0
Outputs:
- orbitals: float32 [64, 24, 1024], P('orb', 'grid')
All inputs are finite; a program needn't handle non-finite values.
Results may differ from a plain program's by a relative error of at most 0.0003.
Values sent between devices are 32-bit elements; how exact they have to be, the bound alone decides.
No kernel may reach another device: no remote copies, remote signals or barrier semaphores. Data moves between devices by JAX's collectives and lax.ppermute only.
A program may use at most 64 MiB of HBM per device.

v0:
```python
import jax
import jax.numpy as jnp
from jax import lax
from jax.sharding import PartitionSpec as P

PANEL = 32
NPANEL = 2
NY = 32


COEFFS = (
    -5369.0 / 1800.0,
    12.0 / 7.0,
    -15.0 / 56.0,
    10.0 / 189.0,
    -1.0 / 112.0,
    2.0 / 1925.0,
    -1.0 / 16632.0,
)
HIGH = lax.Precision.HIGHEST
RIM = 6


def from_root(shard, axis, root):
    mine = lax.axis_index(axis) == root
    return lax.psum(jnp.where(mine, shard, jnp.zeros_like(shard)), axis)


def extended_2(shard, sides, width):
    for axis, dim in sides:
        peers, length = (lax.axis_size(axis), shard.shape[dim])
        up = [(i, (i + 1) % peers) for i in range(peers)]
        down = [(j, i) for i, j in up]
        last = lax.slice_in_dim(shard, length - width, length, axis=dim)
        first = lax.slice_in_dim(shard, 0, width, axis=dim)
        before = lax.ppermute(last, axis, up)
        after = lax.ppermute(first, axis, down)
        shard = jnp.concatenate([before, shard, after], axis=dim)
    return shard


def inner(left, right, scale):
    return jnp.einsum("ic,jc->ij", left, right, precision=HIGH) * scale


def orthonormalize(block, gram):
    lower = jnp.linalg.cholesky(gram)
    return lax.linalg.triangular_solve(lower, block, left_side=True, lower=True)


def fetch_panel(work, first, members):
    pieces = []
    for member in range(members):
        pieces.append(from_root(work, "orb", first + member))
    return jnp.concatenate(pieces, 0)


def first_gram_sum(block, scale):
    return lax.psum(inner(block, block, scale), "grid")


def coefficient_sum(local):
    return lax.psum(local, "grid")


def joint_sum(local, ahead, whole):
    return lax.psum((local, ahead, whole), "grid")


def remove(block, coeff, ortho):
    return block - jnp.einsum("ij,ic->jc", coeff, ortho, precision=HIGH)


def update(work, moved, ortho, rank, first, members):
    count = work.shape[0]
    offset = jnp.clip(rank - first, 0, members - 1) * count
    owned = lax.dynamic_slice_in_dim(ortho, offset, count, 0)
    member = (rank >= first) & (rank < first + members)
    later = rank >= first + members
    return jnp.where(later, moved, jnp.where(member, owned, work))


def per_device(wavefunctions, potential):
    count, depth, plane = wavefunctions.shape
    cells = depth * plane
    members = PANEL // count
    scale = 1.0 / (depth * plane * lax.axis_size("grid"))
    extended = extended_2(wavefunctions, (("grid", 1),), RIM)
    margin = RIM * NY
    padded = jnp.pad(wavefunctions, ((0, 0), (0, 0), (margin, margin)))
    column = lax.broadcasted_iota(jnp.int32, (plane,), 0) % NY
    total = 3.0 * COEFFS[0] * wavefunctions
    for k in range(1, RIM + 1):
        along_z = extended[:, RIM + k : RIM + k + depth] + extended[:, RIM - k : RIM - k + depth]
        along_x = (
            padded[:, :, margin + k * NY : margin + k * NY + plane]
            + padded[:, :, margin - k * NY : margin - k * NY + plane]
        )
        y_plus = jnp.where(column + k < NY, padded[:, :, margin + k : margin + k + plane], 0.0)
        y_minus = jnp.where(column - k >= 0, padded[:, :, margin - k : margin - k + plane], 0.0)
        total = total + COEFFS[k] * (along_z + along_x + y_plus + y_minus)
    work = -0.5 * total.reshape(count, cells) + (potential[None] * wavefunctions).reshape(
        count, cells
    )
    rank = lax.axis_index("orb")
    panel = fetch_panel(work, 0, members)
    gram = first_gram_sum(panel, scale)
    for p in range(NPANEL):
        ortho = orthonormalize(panel, gram)
        if p + 1 < NPANEL:
            upcoming = fetch_panel(work, (p + 1) * members, members)
            coeff, ahead, whole = joint_sum(
                inner(ortho, work, scale),
                inner(ortho, upcoming, scale),
                inner(upcoming, upcoming, scale),
            )
            next_panel = remove(upcoming, ahead, ortho)
            gram = whole - jnp.einsum("ki,kj->ij", ahead, ahead, precision=HIGH)
        else:
            coeff = coefficient_sum(inner(ortho, work, scale))
        work = update(work, remove(work, coeff, ortho), ortho, rank, p * members, members)
        if p + 1 < NPANEL:
            panel = next_panel
    return work.reshape(count, depth, plane)


def solution(mesh):
    return jax.shard_map(
        per_device,
        mesh=mesh,
        in_specs=(P("orb", "grid", None), P("grid", None)),
        out_specs=P("orb", "grid", None),
        check_vma=False,
    )
```

profile of v0, /device:TPU:0, one launch (start us, length us, event | category | flops | bytes accessed | tf_op | source)
XLA Modules:
  0.0 170.6 jit_solution(10125674970479276462)
XLA Ops:
  6.5 3.0 %collective-permute-start.1 = (f32[8,6,1024]{2,0,1:T(8,128)}, f32[8,6,1024]{2,0,1:T(8,128)S(1)}, u32[]{:S(2)}, u32[]{:S(2)}) collective-permute-start(f32[8,6,1024]{2,0,1:T(8,128)} %param.5), channel_id=1, source_target_pairs={{0,1},{1,2},{2,3},{3,0},{4,5},{5,6},{6,7},{7,4},{8,9},{9,10},{10,1... | collective-permute-start | bytes 589832 | tf_op jit(solution)/shard_map/ppermute | solution.py:36
  9.6 2.0 %collective-permute-start = (f32[8,6,1024]{2,0,1:T(8,128)}, f32[8,6,1024]{2,0,1:T(8,128)S(1)}, u32[]{:S(2)}, u32[]{:S(2)}) collective-permute-start(f32[8,6,1024]{2,0,1:T(8,128)} %param.5), channel_id=1, source_target_pairs={{1,0},{2,1},{3,2},{0,3},{5,4},{6,5},{7,6},{4,7},{9,8},{10,9},{11,1... | collective-permute-start | bytes 589832 | tf_op jit(solution)/shard_map/ppermute | solution.py:37
  11.7 5.9 %collective-permute-done.1 = f32[8,6,1024]{2,0,1:T(8,128)S(1)} collective-permute-done((f32[8,6,1024]{2,0,1:T(8,128)}, f32[8,6,1024]{2,0,1:T(8,128)S(1)}, u32[]{:S(2)}, u32[]{:S(2)}) %collective-permute-start.1) | collective-permute-done | bytes 196640 | tf_op jit(solution)/shard_map/ppermute | solution.py:36
  17.6 2.7 %collective-permute-done = f32[8,6,1024]{2,0,1:T(8,128)S(1)} collective-permute-done((f32[8,6,1024]{2,0,1:T(8,128)}, f32[8,6,1024]{2,0,1:T(8,128)S(1)}, u32[]{:S(2)}, u32[]{:S(2)}) %collective-permute-start) | collective-permute-done | bytes 196640 | tf_op jit(solution)/shard_map/ppermute | solution.py:37
  20.4 0.7 copy-done.8
  21.1 1.2 fusion.14
  22.3 1.2 broadcast_select_fusion
  23.5 60.6 %all-reduce.5.cloned.1.call-done = (f32[8,6144]{1,0:T(8,128)}, f32[8,6144]{1,0:T(8,128)}, f32[8,6144]{1,0:T(8,128)}, f32[8,6144]{1,0:T(8,128)}, f32[8,6144]{1,0:...) async-done(((f32[8,6144]{1,0:T(8,128)}, f32[8,6144]{1,0:T(8,128)}, f32[8,6144]{1,0:T(8,128)}, f32[8,6144]{1,0:T(8,128)}, f32[8,6144]{1,0:T(8,128)}, ...) | async-done | bytes 1572880 | tf_op jit(solution)/shard_map/psum | solution.py:26
  84.1 1.0 constant_dynamic-update-slice_fusion.11
  85.1 0.9 copy-done.6
  86.1 0.9 copy-done.5
  87.0 0.9 copy-done.4
  87.9 0.8 convolution_multiply_fusion.2
  88.7 18.7 %psum.95 = f32[32,32]{0,1:T(8,128)S(1)} all-reduce(f32[32,32]{0,1:T(8,128)S(1)} %convolution_multiply_fusion.2), channel_id=1, replica_groups=mesh['orb'=8,'grid'=4] {'grid'}, use_global_device_ids=true, to_apply=%region_4.5 | all-reduce | flops 1024 | bytes 8192 | tf_op jit(solution)/shard_map/psum | solution.py:59
  107.5 2.9 %cholesky.44 = f32[32,32]{1,0:T(8,128)S(1)} custom-call(f32[32,32]{1,0:T(8,128)S(1)} %fusion.59), custom_call_target="Cholesky" | custom-call | tf_op jit(solution)/shard_map/jit(cholesky)/cholesky | solution.py:47
  111.1 0.7 fusion.52
  111.7 2.4 %custom-call.6 = f32[1,32,32]{1,2,0:T(8,128)S(1)} custom-call(f32[1,32,32]{2,1,0:T(8,128)S(1)} %fusion.52), custom_call_target="InvertDiagBlocksLowerTriangular" | custom-call | tf_op jit(solution)/shard_map/triangular_solve/custom-call.0 | solution.py:48
  114.2 0.8 fusion.57
  115.1 0.9 copy-done.2
  116.1 0.9 copy-done.1
  117.0 0.8 convolution_multiply_fusion.1
  117.8 0.8 convolution_multiply_fusion
  118.5 0.8 convolution_multiply_fusion.4
  119.3 16.4 %all-reduce.2 = (f32[32,8]{1,0:T(8,128)S(1)}, f32[32,32]{0,1:T(8,128)S(1)}, f32[32,32]{0,1:T(8,128)S(1)}) all-reduce(f32[32,8]{1,0:T(8,128)S(1)} %convolution_multiply_fusion.4, f32[32,32]{0,1:T(8,128)S(1)} %convolution_multiply_fusion, f32[32,32]{0,1:T(8,128)S(1)} %convolution_multiply_fusion.1), channel_id=1, replica_groups=mesh['orb'=8,'grid'=4] {'grid'}, use_global_device_ids=true, to_apply=%region_7.10 | all-reduce | flops 2304 | bytes 18432 | tf_op jit(solution)/shard_map/psum | solution.py:67
  135.7 0.8 convolution_subtract_fusion
  136.7 2.9 %cholesky.55 = f32[32,32]{1,0:T(8,128)S(1)} custom-call(f32[32,32]{1,0:T(8,128)S(1)} %fusion.56), custom_call_target="Cholesky" | custom-call | tf_op jit(solution)/shard_map/jit(cholesky)/cholesky | solution.py:47
  140.3 0.7 fusion.53
  141.0 2.4 %custom-call.7 = f32[1,32,32]{1,2,0:T(8,128)S(1)} custom-call(f32[1,32,32]{2,1,0:T(8,128)S(1)} %fusion.53), custom_call_target="InvertDiagBlocksLowerTriangular" | custom-call | tf_op jit(solution)/shard_map/triangular_solve/custom-call.0 | solution.py:48
  143.4 0.8 fusion.54
  144.8 0.7 convolution_multiply_fusion.3
  145.5 17.1 %psum.103 = f32[32,8]{1,0:T(8,128)S(1)} all-reduce(f32[32,8]{1,0:T(8,128)S(1)} %convolution_multiply_fusion.3), channel_id=1, replica_groups=mesh['orb'=8,'grid'=4] {'grid'}, use_global_device_ids=true, to_apply=%region_14.17 | all-reduce | flops 256 | bytes 2048 | tf_op jit(solution)/shard_map/psum | solution.py:63
  162.6 1.2 fusion.1
  (40 shorter events, 2.5 us)
Async XLA Ops:
  6.5 77.6 %all-reduce.5.cloned.1.call-start = ((), (), s32[]{:S(2)}) async-start(), calls=%async_computation | async-start | bytes 3145728 | tf_op jit(solution)/shard_map/psum | solution.py:26
  6.5 11.0 %collective-permute-start.1 = (f32[8,6,1024]{2,0,1:T(8,128)}, f32[8,6,1024]{2,0,1:T(8,128)S(1)}, u32[]{:S(2)}, u32[]{:S(2)}) collective-permute-start(f32[8,6,1024]{2,0,1:T(8,128)} %param.5), channel_id=1, source_target_pairs={{0,1},{1,2},{2,3},{3,0},{4,5},{5,6},{6,7},{7,4},{8,9},{9,10},{10,1... | collective-permute-start | bytes 589832 | tf_op jit(solution)/shard_map/ppermute | solution.py:36
  9.6 10.8 %collective-permute-start = (f32[8,6,1024]{2,0,1:T(8,128)}, f32[8,6,1024]{2,0,1:T(8,128)S(1)}, u32[]{:S(2)}, u32[]{:S(2)}) collective-permute-start(f32[8,6,1024]{2,0,1:T(8,128)} %param.5), channel_id=1, source_target_pairs={{1,0},{2,1},{3,2},{0,3},{5,4},{6,5},{7,6},{4,7},{9,8},{10,9},{11,1... | collective-permute-start | bytes 589832 | tf_op jit(solution)/shard_map/ppermute | solution.py:37
  11.7 5.9 %copy-start = (f32[8,6,1024]{2,0,1:T(8,128)S(1)}, f32[8,6,1024]{2,0,1:T(8,128)}, u32[]{:S(2)}) copy-start(f32[8,6,1024]{2,0,1:T(8,128)} %param.5) | copy-start | bytes 589828
  20.3 0.8 copy-start.8
  84.1 1.0 copy-start.7
  85.1 0.9 copy-start.6
  86.0 0.9 copy-start.5
  87.0 0.9 copy-start.4
  114.2 1.0 copy-start.3
  115.1 0.9 copy-start.2
  116.1 0.9 copy-start.1
Sparse Core Ops, SparseCore 0:
  23.6 60.4 all-reduce.4
where the time goes:
time: 171 us
  waiting for transfers between devices  69.2 us (40%)
  blocking collectives  52.1 us (30%)
  other arithmetic  15.7 us (9%)
  between operations  13.6 us (8%)
  matrix products  8.11 us (5%)
  local copies, waits for them, and re-layouts  6.71 us (4%)
  starting transfers between devices  5.05 us (3%)
    psum x1, waiting for transfers between devices, from_root(): return lax.psum(jnp.where(mine, shard, jnp.zeros_like(shard)), axis)  60.6 us
    psum x1, blocking collectives, first_gram_sum(): return lax.psum(inner(block, block, scale), 'grid')  18.7 us
    psum x1, blocking collectives, coefficient_sum(): return lax.psum(local, 'grid')  17.1 us
    psum x1, blocking collectives, joint_sum(): return lax.psum((local, ahead, whole), 'grid')  16.4 us
    another operation x6, other arithmetic, orthonormalize(): lower = jnp.linalg.cholesky(gram)  7.19 us
    unnamed x26, local copies, waits for them, and re-layouts  6.52 us
    another operation x4, other arithmetic, orthonormalize(): return lax.linalg.triangular_solve(lower, block, left_side=True, lower=True)  6.17 us
    ppermute x1, waiting for transfers between devices, extended_2(): before = lax.ppermute(last, axis, up)  5.88 us
  transfers between devices with their start and end apart: 3, of which 3 were waited for; matrix products, arithmetic and copies ran while one was open for 0% of the time, Pallas kernels for 0%

commit v1 on v0

v1 whole, which is shorter than its diff:
```python
import functools

import jax
import jax.numpy as jnp
from jax import lax
from jax.experimental import pallas as pl
from jax.experimental.pallas import tpu as pltpu
from jax.sharding import PartitionSpec as P

PANEL = 32
NPANEL = 2
NY = 32

COEFFS = (
    -5369.0 / 1800.0,
    12.0 / 7.0,
    -15.0 / 56.0,
    10.0 / 189.0,
    -1.0 / 112.0,
    2.0 / 1925.0,
    -1.0 / 16632.0,
)
HIGH = lax.Precision.HIGHEST
RIM = 6
LANES = 128


def local_kernel(v_ref, pot_ref, out_ref):
    depth, count, plane = v_ref.shape
    lane = lax.broadcasted_iota(jnp.int32, (count, plane), 1)
    column = lane % NY
    for p in range(depth):
        here = v_ref[p]
        acc = (-1.5 * COEFFS[0] + pot_ref[p : p + 1, :]) * here
        for k in range(1, RIM + 1):
            up, down = NY * k, plane - NY * k
            near = jnp.where(lane < down, pltpu.roll(here, down, 1), 0.0)
            near += jnp.where(lane >= up, pltpu.roll(here, up, 1), 0.0)
            near += jnp.where(column + k < NY, pltpu.roll(here, plane - k, 1), 0.0)
            near += jnp.where(column >= k, pltpu.roll(here, k, 1), 0.0)
            if p + k < depth:
                near += v_ref[p + k]
            if p >= k:
                near += v_ref[p - k]
            acc += (-0.5 * COEFFS[k]) * near
        out_ref[:, p * plane : (p + 1) * plane] = acc


def couple_kernel(local_ref, before_ref, after_ref, out_ref):
    rim, count, plane = before_ref.shape
    depth = out_ref.shape[1] // plane
    for p in range(depth):
        acc = local_ref[:, p * plane : (p + 1) * plane]
        for q in range(rim):
            if p + rim - q <= rim:
                acc += (-0.5 * COEFFS[p + rim - q]) * before_ref[q]
            if depth + q - p <= rim:
                acc += (-0.5 * COEFFS[depth + q - p]) * after_ref[q]
        out_ref[:, p * plane : (p + 1) * plane] = acc


def gram_kernel(scale, rank_ref, *refs):
    blocks, (gram_ref, stack_ref) = refs[:-2], refs[-2:]
    count = blocks[0].shape[0]
    total = count * len(blocks)
    rank = rank_ref[0]
    odd = rank % 2 == 1
    for k in range(0, len(blocks), 2):
        one, two = blocks[k][...], blocks[k + 1][...]
        pair = jnp.concatenate([jnp.where(odd, two, one), jnp.where(odd, one, two)], 0)
        high = pair.astype(jnp.bfloat16)
        low = (pair - high.astype(jnp.float32)).astype(jnp.bfloat16)
        first = pl.multiple_of((rank // 2 ^ k // 2) * (2 * count), 2 * count)
        stack_ref[pl.ds(first, 2 * count), :] = high
        stack_ref[pl.ds(total + first, 2 * count), :] = low
    whole = stack_ref[...]
    products = lax.dot_general(
        whole, whole, (((1,), (1,)), ((), ())), preferred_element_type=jnp.float32
    )
    gram = products[:total] + products[total:]
    gram_ref[...] = (gram[:, :total] + gram[:, total:]) * scale


def invert_factor(gram):
    size = gram.shape[0]
    rows = 8
    ident = (
        lax.broadcasted_iota(jnp.int32, (size, size), 0)
        == lax.broadcasted_iota(jnp.int32, (size, size), 1)
    ).astype(jnp.float32)
    whole = jnp.concatenate([gram, ident], 1)
    tiles = [whole[i : i + rows] for i in range(0, size, rows)]
    sub = lax.broadcasted_iota(jnp.int32, (rows, 1), 0)
    pivots = []
    for j in range(size):
        t, s = divmod(j, rows)
        pivot = tiles[t][s : s + 1, j : j + 1]
        pivots.append(pivot)
        row = tiles[t][s : s + 1] / pivot
        for i in range(t, len(tiles)):
            column = tiles[i][:, j : j + 1]
            if i == t:
                column = jnp.where(sub > s, column, 0.0)
            tiles[i] = tiles[i] - column * row
    norm = lax.rsqrt(jnp.concatenate(pivots, 0))
    return jnp.concatenate(tiles, 0)[:, size:] * norm


def finish_kernel(rank_ref, *refs):
    parts, (stack_ref, out_ref, factor_ref) = refs[:-3], refs[-3:]
    depth, count, plane = out_ref.shape
    gram = parts[0][...]
    for part in parts[1:]:
        gram = gram + part[...]
    factor_ref[...] = invert_factor(gram)
    rows = factor_ref[pl.ds(pl.multiple_of(rank_ref[0] * count, count), count), :]
    high = rows.astype(jnp.bfloat16).astype(jnp.float32)
    low = rows - high
    left = jnp.concatenate(
        [jnp.concatenate([high, high], 1), jnp.concatenate([low, low], 1)], 0
    ).astype(jnp.bfloat16)
    for p in range(depth):
        both = jnp.dot(
            left, stack_ref[:, p * plane : (p + 1) * plane], preferred_element_type=jnp.float32
        )
        out_ref[p] = both[:count] + both[count:]


def call(kernel, out_shape, inputs, scratch=(), flops=0):
    in_specs = [
        pl.BlockSpec(memory_space=pltpu.SMEM if a.dtype == jnp.int32 else pltpu.VMEM)
        for a in inputs
    ]
    out_specs = jax.tree.map(lambda s: pl.BlockSpec(memory_space=pltpu.VMEM), out_shape)
    return pl.pallas_call(
        kernel,
        out_shape=out_shape,
        in_specs=in_specs,
        out_specs=out_specs,
        scratch_shapes=scratch,
        compiler_params=pltpu.CompilerParams(vmem_limit_bytes=32 * 2**20),
        cost_estimate=pl.CostEstimate(flops=flops, bytes_accessed=10**6, transcendentals=0),
    )(*inputs)


def rotation(peers, step):
    return [(i, (i + step) % peers) for i in range(peers)]


def exchange(peers, mask):
    return [(i, i ^ mask) for i in range(peers)]


def shape(*dims, dtype=jnp.float32):
    return jax.ShapeDtypeStruct(dims, dtype)


def grid_sum(part, grid):
    if grid > 4:
        return [lax.psum(part, "grid")]
    return [part] + [lax.ppermute(part, "grid", rotation(grid, k)) for k in range(1, grid)]


def gather_all(work, orb):
    blocks = []
    for chip in range(0, orb, 2):
        block = work if chip == 0 else lax.ppermute(work, "orb", exchange(orb, chip))
        blocks += [block, lax.ppermute(block, "orb", exchange(orb, 1))]
    return blocks


def gather_leading(work, rank, members):
    kept = [jnp.where(rank == m, work, jnp.zeros_like(work)) for m in range(members)]
    return lax.psum(kept, "orb")


def finish_leading(work, blocks, gram, rank, scale):
    count = work.shape[0]
    leading = jnp.concatenate(blocks, 0)
    total = leading.shape[0]
    inner = functools.partial(jnp.einsum, "ic,jc->ij", precision=HIGH)
    coeff = lax.psum(inner(work, leading) * scale, "grid")
    inverse = lax.linalg.triangular_solve(
        jnp.linalg.cholesky(gram), jnp.eye(total, dtype=gram.dtype), left_side=True, lower=True
    )
    first = jnp.minimum(rank * count, total - count)
    owned = lax.dynamic_slice_in_dim(inverse, first, count, 0)
    taken = jnp.dot(inner(coeff, inverse), inverse, precision=HIGH)
    member = rank * count < total
    rows = jnp.where(member, owned, -taken)
    return jnp.where(member, 0.0, work) + jnp.dot(rows, leading, precision=HIGH)


def per_device(wavefunctions, potential):
    planes = jnp.transpose(wavefunctions, (1, 0, 2))
    depth, count, plane = planes.shape
    cells = depth * plane
    orb, grid = lax.axis_size("orb"), lax.axis_size("grid")
    members = min(PANEL * NPANEL // count, orb)
    total = members * count
    scale = 1.0 / (cells * grid)
    before = lax.ppermute(planes[depth - RIM :], "grid", rotation(grid, 1))
    after = lax.ppermute(planes[:RIM], "grid", rotation(grid, -1))
    local = call(local_kernel, shape(count, cells), [planes, potential], flops=10**9)
    work = call(couple_kernel, shape(count, cells), [local, before, after])
    rank = lax.axis_index("orb").astype(jnp.int32)
    everyone = members == orb and orb & (orb - 1) == 0
    blocks = gather_all(work, orb) if everyone else gather_leading(work, rank, members)
    gram, stack = call(
        functools.partial(gram_kernel, scale),
        (shape(total, total), shape(2 * total, cells, dtype=jnp.bfloat16)),
        [rank.reshape(1) if everyone else jnp.zeros((1,), jnp.int32), *blocks],
    )
    parts = grid_sum(gram, grid)
    if not everyone:
        rest = finish_leading(work, blocks, sum(parts), rank, scale)
        return rest.reshape(count, depth, plane)
    done = call(
        finish_kernel,
        shape(depth, count, plane),
        [rank.reshape(1), *parts, stack],
        scratch=[pltpu.VMEM((total, total), jnp.float32)],
    )
    return jnp.transpose(done, (1, 0, 2))


def solution(mesh):
    return jax.shard_map(
        per_device,
        mesh=mesh,
        in_specs=(P("orb", "grid", None), P("grid", None)),
        out_specs=P("orb", "grid", None),
        check_vma=False,
    )
```

time: 171 us -> 44.1 us (0.26)
  blocking collectives: 52.1 us -> 0 us
  waiting for transfers between devices: 69.2 us -> 21.3 us
  other arithmetic: 15.7 us -> 0 us
  between operations: 13.6 us -> 0.03 us
  Pallas kernels: 0 us -> 8.67 us
  matrix products: 8.11 us -> 0 us
  starting transfers between devices: 5.05 us -> 12.1 us
  local copies, waits for them, and re-layouts: 6.71 us -> 1.75 us
    psum x1 -> x0, waiting for transfers between devices: 60.6 us -> none  [from_root(): return lax.psum(jnp.where(mine, shard, jnp.zeros_like(shard)), axis)]
    psum x3 -> x0, blocking collectives: 52.1 us -> none  [the longest x1 18.7 us: first_gram_sum(): return lax.psum(inner(block, block, scale), 'grid')]
    another operation x10 -> x0, other arithmetic: 13.4 us -> none  [the longest x6 7.19 us: orthonormalize(): lower = jnp.linalg.cholesky(gram)]
    ppermute x2 -> x12, waiting for transfers between devices: 8.59 us -> 21.3 us  [the longest x3 7.58 us: gather_all(): lax.ppermute(work, 'orb', exchange(orb, chip))]
    pallas_call x0 -> x4, Pallas kernels: none -> 8.67 us  [call(): pl.pallas_call(kernel, out_shape=out_shape, in_specs=in_specs, out_specs=...]
    ppermute x2 -> x12, starting transfers between devices: 5.05 us -> 12.1 us  [the longest x1 5.05 us: per_device(): after = lax.ppermute(planes[:RIM], 'grid', rotation(grid, -1))]
    dot_general x9 -> x0, matrix products: 6.41 us -> none  [the longest x5 3.79 us: inner(): return jnp.einsum('ic,jc->ij', left, right, precision=HIGH) * scale]
    unnamed x26 -> x4, local copies, waits for them, and re-layouts: 6.52 us -> 1.75 us
  transfers between devices with their start and end apart: 3 -> 12, of which waited for: 3 -> 10; matrix products, arithmetic and copies ran while one was open for 0% -> 0% of each run, Pallas kernels for 0% -> 2%
where the time goes in v1:
time: 44.1 us; the launch traced here: 43.9 us
  waiting for transfers between devices  21.3 us (48%)
  starting transfers between devices  12.1 us (27%)
  Pallas kernels  8.67 us (20%)
  local copies, waits for them, and re-layouts  1.75 us (4%)
    pallas_call x4, Pallas kernels, call(): pl.pallas_call(kernel, out_shape=out_shape, in_specs=in_specs, out_specs=...  8.67 us
    ppermute x3, waiting for transfers between devices, gather_all(): lax.ppermute(work, 'orb', exchange(orb, chip))  7.58 us
    ppermute x3, waiting for transfers between devices, grid_sum(): lax.ppermute(part, 'grid', rotation(grid, k))  5.71 us
    ppermute x1, starting transfers between devices, per_device(): after = lax.ppermute(planes[:RIM], 'grid', rotation(grid, -1))  5.05 us
    ppermute x1, waiting for transfers between devices, per_device(): before = lax.ppermute(planes[depth - RIM:], 'grid', rotation(grid, 1))  3.86 us
    ppermute x3, starting transfers between devices, gather_all(): lax.ppermute(work, 'orb', exchange(orb, chip))  3.55 us
    ppermute x3, starting transfers between devices, grid_sum(): lax.ppermute(part, 'grid', rotation(grid, k))  3.08 us
    ppermute x1, waiting for transfers between devices, per_device(): after = lax.ppermute(planes[:RIM], 'grid', rotation(grid, -1))  2.93 us
  transfers between devices with their start and end apart: 12, of which 10 were waited for; matrix products, arithmetic and copies ran while one was open for 0% of the time, Pallas kernels for 2%

profile of v1, /device:TPU:0, one launch (start us, length us, event | category | flops | bytes accessed | tf_op | source)
XLA Modules:
  0.0 43.9 jit_solution(11713392429779069573)
XLA Ops:
  0.0 5.0 %collective-permute-start.1 = (f32[6,8,1024]{2,1,0:T(8,128)}, f32[6,8,1024]{2,1,0:T(8,128)S(1)}, u32[]{:S(2)}, u32[]{:S(2)}) collective-permute-start(f32[6,8,1024]{2,1,0:T(8,128)} %bitcast.3), channel_id=1, source_target_pairs={{0,3},{1,0},{2,1},{3,2},{4,7},{5,4},{6,5},{7,6},{8,11},{9,8},{10,9... | collective-permute-start | bytes 589832 | tf_op jit(solution)/shard_map/ppermute | solution.py:203
  5.0 0.0 collective-permute-start
  5.1 0.0 copy-start
  5.1 1.0 %copy-done = f32[8,6,1024]{2,0,1:T(8,128)S(1)} copy-done((f32[8,6,1024]{2,0,1:T(8,128)S(1)}, f32[8,6,1024]{2,0,1:T(8,128)}, u32[]{:S(2)}) %copy-start) | copy-done | bytes 196632
  6.0 0.0 copy-start.1
  6.0 0.8 %copy-done.1 = f32[6,1024]{1,0:T(8,128)S(1)} copy-done((f32[6,1024]{1,0:T(8,128)S(1)}, f32[6,1024]{1,0:T(8,128)}, u32[]{:S(2)}) %copy-start.1) | copy-done | bytes 24600
  6.8 0.9 %shard_map.28.local_ref = f32[8,6144]{1,0:T(8,128)S(1)} custom-call(f32[6,8,1024]{2,1,0:T(8,128)S(1)} %bitcast.5, f32[6,1024]{1,0:T(8,128)S(1)} %copy-done.1), custom_call_target="tpu_custom_call" | custom-call | flops 1000000000 | bytes 1000000 | tf_op jit(solution)/shard_map/pallas_call | solution.py:135
  7.7 2.9 %collective-permute-done.1.after_ref = f32[6,8,1024]{2,1,0:T(8,128)S(1)} collective-permute-done((f32[6,8,1024]{2,1,0:T(8,128)}, f32[6,8,1024]{2,1,0:T(8,128)S(1)}, u32[]{:S(2)}, u32[]{:S(2)}) %collective-permute-start.1) | collective-permute-done | bytes 196640 | tf_op jit(solution)/shard_map/ppermute | solution.py:203
  10.7 3.9 %collective-permute-done.before_ref = f32[6,8,1024]{2,1,0:T(8,128)S(1)} collective-permute-done((f32[6,8,1024]{2,1,0:T(8,128)}, f32[6,8,1024]{2,1,0:T(8,128)S(1)}, u32[]{:S(2)}, u32[]{:S(2)}) %collective-permute-start) | collective-permute-done | bytes 196640 | tf_op jit(solution)/shard_map/ppermute | solution.py:202
  14.5 0.1 shard_map.29.refs_0_
  14.6 2.5 %collective-permute-start.7 = (f32[8,6144]{1,0:T(8,128)S(1)}, f32[8,6144]{1,0:T(8,128)S(1)}, u32[]{:S(2)}, u32[]{:S(2)}) collective-permute-start(f32[8,6144]{1,0:T(8,128)S(1)} %shard_map.29.refs_0_), channel_id=1, source_target_pairs={{0,24},{4,28},{8,16},{12,20},{16,8},{20,12},{24,0},{28,4},{1,25},{... | collective-permute-start | bytes 589832 | tf_op jit(solution)/shard_map/ppermute | solution.py:167
  17.2 0.5 %collective-permute-start.5 = (f32[8,6144]{1,0:T(8,128)S(1)}, f32[8,6144]{1,0:T(8,128)S(1)}, u32[]{:S(2)}, u32[]{:S(2)}) collective-permute-start(f32[8,6144]{1,0:T(8,128)S(1)} %shard_map.29.refs_0_), channel_id=1, source_target_pairs={{0,16},{4,20},{8,24},{12,28},{16,0},{20,4},{24,8},{28,12},{1,17},{... | collective-permute-start | bytes 589832 | tf_op jit(solution)/shard_map/ppermute | solution.py:167
  17.7 0.5 %collective-permute-start.3 = (f32[8,6144]{1,0:T(8,128)S(1)}, f32[8,6144]{1,0:T(8,128)S(1)}, u32[]{:S(2)}, u32[]{:S(2)}) collective-permute-start(f32[8,6144]{1,0:T(8,128)S(1)} %shard_map.29.refs_0_), channel_id=1, source_target_pairs={{0,8},{4,12},{8,0},{12,4},{16,24},{20,28},{24,16},{28,20},{1,9},{5... | collective-permute-start | bytes 589832 | tf_op jit(solution)/shard_map/ppermute | solution.py:167
  18.2 0.0 collective-permute-start.2
  18.2 5.0 %collective-permute-done.7.refs_6_ = f32[8,6144]{1,0:T(8,128)S(1)} collective-permute-done((f32[8,6144]{1,0:T(8,128)S(1)}, f32[8,6144]{1,0:T(8,128)S(1)}, u32[]{:S(2)}, u32[]{:S(2)}) %collective-permute-start.7) | collective-permute-done | bytes 196640 | tf_op jit(solution)/shard_map/ppermute | solution.py:167
  23.2 0.0 collective-permute-start.8
  23.2 2.4 %collective-permute-done.5.refs_4_ = f32[8,6144]{1,0:T(8,128)S(1)} collective-permute-done((f32[8,6144]{1,0:T(8,128)S(1)}, f32[8,6144]{1,0:T(8,128)S(1)}, u32[]{:S(2)}, u32[]{:S(2)}) %collective-permute-start.5) | collective-permute-done | bytes 196640 | tf_op jit(solution)/shard_map/ppermute | solution.py:167
  25.7 0.0 collective-permute-start.6
  25.7 0.1 collective-permute-done.3.refs_2_
  25.8 0.4 collective-permute-start.4
  26.2 0.0 collective-permute-done.2.refs_1_
  26.2 0.0 collective-permute-done.8.refs_7_
  26.2 0.9 %collective-permute-done.6.refs_5_ = f32[8,6144]{1,0:T(8,128)S(1)} collective-permute-done((f32[8,6144]{1,0:T(8,128)S(1)}, f32[8,6144]{1,0:T(8,128)S(1)}, u32[]{:S(2)}, u32[]{:S(2)}) %collective-permute-start.6) | collective-permute-done | bytes 196640 | tf_op jit(solution)/shard_map/ppermute | solution.py:168
  27.1 0.3 collective-permute-done.4.refs_3_
  27.4 1.1 %shard_map.30 = (f32[64,64]{1,0:T(8,128)S(1)}, bf16[128,6144]{1,0:T(8,128)(2,1)S(1)}) custom-call(s32[1]{0:T(128)} %bitcast.rank_ref, f32[8,6144]{1,0:T(8,128)S(1)} %shard_map.29.refs_0_, f32[8,6144]{1,0:T(8,128)S(1)} %collective-permute-done.2.refs_1_, f32[8,6144]{1,0:T(8,128)S(1)} %collective-permute-done.3.refs_2_, ...), custom_call_target="tpu_custom_call" | custom-call | bytes 1000000 | tf_op jit(solution)/shard_map/pallas_call | solution.py:135
  28.5 1.3 %collective-permute-start.11 = (f32[64,64]{1,0:T(8,128)S(1)}, f32[64,64]{1,0:T(8,128)S(1)}, u32[]{:S(2)}, u32[]{:S(2)}) collective-permute-start(f32[64,64]{1,0:T(8,128)S(1)} %get-tuple-element.7.refs_0_), channel_id=1, source_target_pairs={{0,3},{1,0},{2,1},{3,2},{4,7},{5,4},{6,5},{7,6},{8,11},{9,8},{10,9... | collective-permute-start | bytes 49160 | tf_op jit(solution)/shard_map/ppermute | solution.py:161
  29.8 1.7 %collective-permute-start.10 = (f32[64,64]{1,0:T(8,128)S(1)}, f32[64,64]{1,0:T(8,128)S(1)}, u32[]{:S(2)}, u32[]{:S(2)}) collective-permute-start(f32[64,64]{1,0:T(8,128)S(1)} %get-tuple-element.7.refs_0_), channel_id=1, source_target_pairs={{0,2},{1,3},{2,0},{3,1},{4,6},{5,7},{6,4},{7,5},{8,10},{9,11},{10,... | collective-permute-start | bytes 49160 | tf_op jit(solution)/shard_map/ppermute | solution.py:161
  31.6 0.0 collective-permute-start.9
  31.6 0.9 %collective-permute-done.11.refs_3_ = f32[64,64]{1,0:T(8,128)S(1)} collective-permute-done((f32[64,64]{1,0:T(8,128)S(1)}, f32[64,64]{1,0:T(8,128)S(1)}, u32[]{:S(2)}, u32[]{:S(2)}) %collective-permute-start.11) | collective-permute-done | bytes 16416 | tf_op jit(solution)/shard_map/ppermute | solution.py:161
  32.5 2.5 %collective-permute-done.10.refs_2_ = f32[64,64]{1,0:T(8,128)S(1)} collective-permute-done((f32[64,64]{1,0:T(8,128)S(1)}, f32[64,64]{1,0:T(8,128)S(1)}, u32[]{:S(2)}, u32[]{:S(2)}) %collective-permute-start.10) | collective-permute-done | bytes 16416 | tf_op jit(solution)/shard_map/ppermute | solution.py:161
  35.0 2.3 %collective-permute-done.9.refs_1_ = f32[64,64]{1,0:T(8,128)S(1)} collective-permute-done((f32[64,64]{1,0:T(8,128)S(1)}, f32[64,64]{1,0:T(8,128)S(1)}, u32[]{:S(2)}, u32[]{:S(2)}) %collective-permute-start.9) | collective-permute-done | bytes 16416 | tf_op jit(solution)/shard_map/ppermute | solution.py:161
  37.3 6.6 %shard_map.31 = f32[6,8,1024]{2,1,0:T(8,128)} custom-call(s32[1]{0:T(128)} %bitcast.rank_ref, f32[64,64]{1,0:T(8,128)S(1)} %get-tuple-element.7.refs_0_, f32[64,64]{1,0:T(8,128)S(1)} %collective-permute-done.9.refs_1_, f32[64,64]{1,0:T(8,128)S(1)} %collective-permute-done.10.refs_2_, f32[64,64]{1,0:T(8,128)S(1)} %collective-permute-done.11.refs_3_, ...), custom_call_target="tpu_custom_call" | custom-call | bytes 1000000 | tf_op jit(solution)/shard_map/pallas_call | solution.py:135
Async XLA Ops:
  0.0 10.7 %collective-permute-start.1 = (f32[6,8,1024]{2,1,0:T(8,128)}, f32[6,8,1024]{2,1,0:T(8,128)S(1)}, u32[]{:S(2)}, u32[]{:S(2)}) collective-permute-start(f32[6,8,1024]{2,1,0:T(8,128)} %bitcast.3), channel_id=1, source_target_pairs={{0,3},{1,0},{2,1},{3,2},{4,7},{5,4},{6,5},{7,6},{8,11},{9,8},{10,9... | collective-permute-start | bytes 589832 | tf_op jit(solution)/shard_map/ppermute | solution.py:203
  5.0 9.5 %collective-permute-start = (f32[6,8,1024]{2,1,0:T(8,128)}, f32[6,8,1024]{2,1,0:T(8,128)S(1)}, u32[]{:S(2)}, u32[]{:S(2)}) collective-permute-start(f32[6,8,1024]{2,1,0:T(8,128)} %bitcast.4), channel_id=1, source_target_pairs={{0,1},{1,2},{2,3},{3,0},{4,5},{5,6},{6,7},{7,4},{8,9},{9,10},{10,1... | collective-permute-start | bytes 589832 | tf_op jit(solution)/shard_map/ppermute | solution.py:202
  5.1 1.0 %copy-start = (f32[8,6,1024]{2,0,1:T(8,128)S(1)}, f32[8,6,1024]{2,0,1:T(8,128)}, u32[]{:S(2)}) copy-start(f32[8,6,1024]{2,0,1:T(8,128)} %param.2) | copy-start | bytes 589828
  6.0 0.8 %copy-start.1 = (f32[6,1024]{1,0:T(8,128)S(1)}, f32[6,1024]{1,0:T(8,128)}, u32[]{:S(2)}) copy-start(f32[6,1024]{1,0:T(8,128)} %pot_ref.1) | copy-start | bytes 73732
  14.6 8.6 %collective-permute-start.7 = (f32[8,6144]{1,0:T(8,128)S(1)}, f32[8,6144]{1,0:T(8,128)S(1)}, u32[]{:S(2)}, u32[]{:S(2)}) collective-permute-start(f32[8,6144]{1,0:T(8,128)S(1)} %shard_map.29.refs_0_), channel_id=1, source_target_pairs={{0,24},{4,28},{8,16},{12,20},{16,8},{20,12},{24,0},{28,4},{1,25},{... | collective-permute-start | bytes 589832 | tf_op jit(solution)/shard_map/ppermute | solution.py:167
  17.2 8.5 %collective-permute-start.5 = (f32[8,6144]{1,0:T(8,128)S(1)}, f32[8,6144]{1,0:T(8,128)S(1)}, u32[]{:S(2)}, u32[]{:S(2)}) collective-permute-start(f32[8,6144]{1,0:T(8,128)S(1)} %shard_map.29.refs_0_), channel_id=1, source_target_pairs={{0,16},{4,20},{8,24},{12,28},{16,0},{20,4},{24,8},{28,12},{1,17},{... | collective-permute-start | bytes 589832 | tf_op jit(solution)/shard_map/ppermute | solution.py:167
  17.7 8.1 %collective-permute-start.3 = (f32[8,6144]{1,0:T(8,128)S(1)}, f32[8,6144]{1,0:T(8,128)S(1)}, u32[]{:S(2)}, u32[]{:S(2)}) collective-permute-start(f32[8,6144]{1,0:T(8,128)S(1)} %shard_map.29.refs_0_), channel_id=1, source_target_pairs={{0,8},{4,12},{8,0},{12,4},{16,24},{20,28},{24,16},{28,20},{1,9},{5... | collective-permute-start | bytes 589832 | tf_op jit(solution)/shard_map/ppermute | solution.py:167
  18.2 8.0 %collective-permute-start.2 = (f32[8,6144]{1,0:T(8,128)S(1)}, f32[8,6144]{1,0:T(8,128)S(1)}, u32[]{:S(2)}, u32[]{:S(2)}) collective-permute-start(f32[8,6144]{1,0:T(8,128)S(1)} %shard_map.29.refs_0_), channel_id=1, source_target_pairs={{0,4},{4,0},{8,12},{12,8},{16,20},{20,16},{24,28},{28,24},{1,5},{5... | collective-permute-start | bytes 589832 | tf_op jit(solution)/shard_map/ppermute | solution.py:168
  23.2 3.0 %collective-permute-start.8 = (f32[8,6144]{1,0:T(8,128)S(1)}, f32[8,6144]{1,0:T(8,128)S(1)}, u32[]{:S(2)}, u32[]{:S(2)}) collective-permute-start(f32[8,6144]{1,0:T(8,128)S(1)} %collective-permute-done.7.refs_6_), channel_id=1, source_target_pairs={{0,4},{4,0},{8,12},{12,8},{16,20},{20,16},{24,28},{28,24},{1,5},{5... | collective-permute-start | bytes 589832 | tf_op jit(solution)/shard_map/ppermute | solution.py:168
  25.7 1.4 %collective-permute-start.6 = (f32[8,6144]{1,0:T(8,128)S(1)}, f32[8,6144]{1,0:T(8,128)S(1)}, u32[]{:S(2)}, u32[]{:S(2)}) collective-permute-start(f32[8,6144]{1,0:T(8,128)S(1)} %collective-permute-done.5.refs_4_), channel_id=1, source_target_pairs={{0,4},{4,0},{8,12},{12,8},{16,20},{20,16},{24,28},{28,24},{1,5},{5... | collective-permute-start | bytes 589832 | tf_op jit(solution)/shard_map/ppermute | solution.py:168
  25.8 1.6 %collective-permute-start.4 = (f32[8,6144]{1,0:T(8,128)S(1)}, f32[8,6144]{1,0:T(8,128)S(1)}, u32[]{:S(2)}, u32[]{:S(2)}) collective-permute-start(f32[8,6144]{1,0:T(8,128)S(1)} %collective-permute-done.3.refs_2_), channel_id=1, source_target_pairs={{0,4},{4,0},{8,12},{12,8},{16,20},{20,16},{24,28},{28,24},{1,5},{5... | collective-permute-start | bytes 589832 | tf_op jit(solution)/shard_map/ppermute | solution.py:168
  28.5 4.0 %collective-permute-start.11 = (f32[64,64]{1,0:T(8,128)S(1)}, f32[64,64]{1,0:T(8,128)S(1)}, u32[]{:S(2)}, u32[]{:S(2)}) collective-permute-start(f32[64,64]{1,0:T(8,128)S(1)} %get-tuple-element.7.refs_0_), channel_id=1, source_target_pairs={{0,3},{1,0},{2,1},{3,2},{4,7},{5,4},{6,5},{7,6},{8,11},{9,8},{10,9... | collective-permute-start | bytes 49160 | tf_op jit(solution)/shard_map/ppermute | solution.py:161
  29.8 5.2 %collective-permute-start.10 = (f32[64,64]{1,0:T(8,128)S(1)}, f32[64,64]{1,0:T(8,128)S(1)}, u32[]{:S(2)}, u32[]{:S(2)}) collective-permute-start(f32[64,64]{1,0:T(8,128)S(1)} %get-tuple-element.7.refs_0_), channel_id=1, source_target_pairs={{0,2},{1,3},{2,0},{3,1},{4,6},{5,7},{6,4},{7,5},{8,10},{9,11},{10,... | collective-permute-start | bytes 49160 | tf_op jit(solution)/shard_map/ppermute | solution.py:161
  31.6 5.7 %collective-permute-start.9 = (f32[64,64]{1,0:T(8,128)S(1)}, f32[64,64]{1,0:T(8,128)S(1)}, u32[]{:S(2)}, u32[]{:S(2)}) collective-permute-start(f32[64,64]{1,0:T(8,128)S(1)} %get-tuple-element.7.refs_0_), channel_id=1, source_target_pairs={{0,1},{1,2},{2,3},{3,0},{4,5},{5,6},{6,7},{7,4},{8,9},{9,10},{10,1... | collective-permute-start | bytes 49160 | tf_op jit(solution)/shard_map/ppermute | solution.py:161

commit v2 on v1

--- a/solution.py
+++ b/solution.py
@@ -84,26 +84,48 @@
 def invert_factor(gram):
     size = gram.shape[0]
     rows = 8
+    full = (rows, 2 * size)
     ident = (
         lax.broadcasted_iota(jnp.int32, (size, size), 0)
         == lax.broadcasted_iota(jnp.int32, (size, size), 1)
     ).astype(jnp.float32)
     whole = jnp.concatenate([gram, ident], 1)
     tiles = [whole[i : i + rows] for i in range(0, size, rows)]
-    sub = lax.broadcasted_iota(jnp.int32, (rows, 1), 0)
-    pivots = []
-    for j in range(size):
-        t, s = divmod(j, rows)
-        pivot = tiles[t][s : s + 1, j : j + 1]
-        pivots.append(pivot)
-        row = tiles[t][s : s + 1] / pivot
-        for i in range(t, len(tiles)):
-            column = tiles[i][:, j : j + 1]
-            if i == t:
-                column = jnp.where(sub > s, column, 0.0)
-            tiles[i] = tiles[i] - column * row
-    norm = lax.rsqrt(jnp.concatenate(pivots, 0))
-    return jnp.concatenate(tiles, 0)[:, size:] * norm
+    done = []
+    for t in range(len(tiles)):
+        later = range(t + 1, len(tiles))
+        columns = {
+            i: [
+                jnp.broadcast_to(tiles[i][:, t * rows + a : t * rows + a + 1], full)
+                for a in range(rows)
+            ]
+            for i in (t, *later)
+        }
+        line = [jnp.broadcast_to(tiles[t][a : a + 1], full) for a in range(rows)]
+        pivot = [
+            [jnp.broadcast_to(columns[t][b][a : a + 1], full) for b in range(a + 1)]
+            for a in range(rows)
+        ]
+        factor = [[None] * rows for _ in range(rows)]
+        inverse = []
+        for a in range(rows):
+            inverse.append(1.0 / pivot[a][a])
+            for b in range(a + 1, rows):
+                factor[b][a] = pivot[b][a] * inverse[a]
+                line[b] = line[b] - factor[b][a] * line[a]
+                for c in range(a + 1, b + 1):
+                    pivot[b][c] = pivot[b][c] - factor[b][a] * pivot[c][a]
+        done += [(line[a] * lax.rsqrt(pivot[a][a]))[:1] for a in range(rows)]
+        solved = [line[a] * inverse[a] for a in range(rows)]
+        for a in range(rows - 1, -1, -1):
+            for b in range(a):
+                solved[b] = solved[b] - factor[a][b] * solved[a]
+        for i in later:
+            terms = [columns[i][a] * solved[a] for a in range(rows)]
+            while len(terms) > 1:
+                terms = [terms[k] + terms[k + 1] for k in range(0, len(terms), 2)]
+            tiles[i] = tiles[i] - terms[0]
+    return jnp.concatenate(done, 0)[:, size:]
 
 
 def finish_kernel(rank_ref, *refs):

time: 44.1 us -> 40.9 us (0.927)
  Pallas kernels: 8.67 us -> 5.47 us
    pallas_call x4, Pallas kernels: 8.67 us -> 5.47 us  [call(): pl.pallas_call(kernel, out_shape=out_shape, in_specs=in_specs, out_specs=...]
where the time goes in v2:
time: 40.9 us; the launch traced here: 40.7 us
  waiting for transfers between devices  21.3 us (52%)
  starting transfers between devices  12.1 us (30%)
  Pallas kernels  5.47 us (13%)
  local copies, waits for them, and re-layouts  1.75 us (4%)
    ppermute x3, waiting for transfers between devices, gather_all(): lax.ppermute(work, 'orb', exchange(orb, chip))  7.58 us
    ppermute x3, waiting for transfers between devices, grid_sum(): lax.ppermute(part, 'grid', rotation(grid, k))  5.71 us
    pallas_call x4, Pallas kernels, call(): pl.pallas_call(kernel, out_shape=out_shape, in_specs=in_specs, out_specs=...  5.47 us
    ppermute x1, starting transfers between devices, per_device(): after = lax.ppermute(planes[:RIM], 'grid', rotation(grid, -1))  5.05 us
    ppermute x1, waiting for transfers between devices, per_device(): before = lax.ppermute(planes[depth - RIM:], 'grid', rotation(grid, 1))  3.86 us
    ppermute x3, starting transfers between devices, gather_all(): lax.ppermute(work, 'orb', exchange(orb, chip))  3.55 us
    ppermute x3, starting transfers between devices, grid_sum(): lax.ppermute(part, 'grid', rotation(grid, k))  3.08 us
    ppermute x1, waiting for transfers between devices, per_device(): after = lax.ppermute(planes[:RIM], 'grid', rotation(grid, -1))  2.93 us
  transfers between devices with their start and end apart: 12, of which 10 were waited for; matrix products, arithmetic and copies ran while one was open for 0% of the time, Pallas kernels for 2%

profile of v2, /device:TPU:0, one launch (start us, length us, event | category | flops | bytes accessed | tf_op | source)
XLA Modules:
  0.0 40.7 jit_solution(4146291857908882307)
XLA Ops:
  0.0 5.0 %collective-permute-start.1 = (f32[6,8,1024]{2,1,0:T(8,128)}, f32[6,8,1024]{2,1,0:T(8,128)S(1)}, u32[]{:S(2)}, u32[]{:S(2)}) collective-permute-start(f32[6,8,1024]{2,1,0:T(8,128)} %bitcast.3), channel_id=1, source_target_pairs={{0,3},{1,0},{2,1},{3,2},{4,7},{5,4},{6,5},{7,6},{8,11},{9,8},{10,9... | collective-permute-start | bytes 589832 | tf_op jit(solution)/shard_map/ppermute | solution.py:225
  5.0 0.0 collective-permute-start
  5.1 0.0 copy-start
  5.1 1.0 %copy-done = f32[8,6,1024]{2,0,1:T(8,128)S(1)} copy-done((f32[8,6,1024]{2,0,1:T(8,128)S(1)}, f32[8,6,1024]{2,0,1:T(8,128)}, u32[]{:S(2)}) %copy-start) | copy-done | bytes 196632
  6.0 0.0 copy-start.1
  6.0 0.8 %copy-done.1 = f32[6,1024]{1,0:T(8,128)S(1)} copy-done((f32[6,1024]{1,0:T(8,128)S(1)}, f32[6,1024]{1,0:T(8,128)}, u32[]{:S(2)}) %copy-start.1) | copy-done | bytes 24600
  6.8 0.9 %shard_map.28.local_ref = f32[8,6144]{1,0:T(8,128)S(1)} custom-call(f32[6,8,1024]{2,1,0:T(8,128)S(1)} %bitcast.5, f32[6,1024]{1,0:T(8,128)S(1)} %copy-done.1), custom_call_target="tpu_custom_call" | custom-call | flops 1000000000 | bytes 1000000 | tf_op jit(solution)/shard_map/pallas_call | solution.py:157
  7.7 2.9 %collective-permute-done.1.after_ref = f32[6,8,1024]{2,1,0:T(8,128)S(1)} collective-permute-done((f32[6,8,1024]{2,1,0:T(8,128)}, f32[6,8,1024]{2,1,0:T(8,128)S(1)}, u32[]{:S(2)}, u32[]{:S(2)}) %collective-permute-start.1) | collective-permute-done | bytes 196640 | tf_op jit(solution)/shard_map/ppermute | solution.py:225
  10.7 3.9 %collective-permute-done.before_ref = f32[6,8,1024]{2,1,0:T(8,128)S(1)} collective-permute-done((f32[6,8,1024]{2,1,0:T(8,128)}, f32[6,8,1024]{2,1,0:T(8,128)S(1)}, u32[]{:S(2)}, u32[]{:S(2)}) %collective-permute-start) | collective-permute-done | bytes 196640 | tf_op jit(solution)/shard_map/ppermute | solution.py:224
  14.5 0.1 shard_map.29.refs_0_
  14.6 2.5 %collective-permute-start.7 = (f32[8,6144]{1,0:T(8,128)S(1)}, f32[8,6144]{1,0:T(8,128)S(1)}, u32[]{:S(2)}, u32[]{:S(2)}) collective-permute-start(f32[8,6144]{1,0:T(8,128)S(1)} %shard_map.29.refs_0_), channel_id=1, source_target_pairs={{0,24},{4,28},{8,16},{12,20},{16,8},{20,12},{24,0},{28,4},{1,25},{... | collective-permute-start | bytes 589832 | tf_op jit(solution)/shard_map/ppermute | solution.py:189
  17.2 0.5 %collective-permute-start.5 = (f32[8,6144]{1,0:T(8,128)S(1)}, f32[8,6144]{1,0:T(8,128)S(1)}, u32[]{:S(2)}, u32[]{:S(2)}) collective-permute-start(f32[8,6144]{1,0:T(8,128)S(1)} %shard_map.29.refs_0_), channel_id=1, source_target_pairs={{0,16},{4,20},{8,24},{12,28},{16,0},{20,4},{24,8},{28,12},{1,17},{... | collective-permute-start | bytes 589832 | tf_op jit(solution)/shard_map/ppermute | solution.py:189
  17.7 0.5 %collective-permute-start.3 = (f32[8,6144]{1,0:T(8,128)S(1)}, f32[8,6144]{1,0:T(8,128)S(1)}, u32[]{:S(2)}, u32[]{:S(2)}) collective-permute-start(f32[8,6144]{1,0:T(8,128)S(1)} %shard_map.29.refs_0_), channel_id=1, source_target_pairs={{0,8},{4,12},{8,0},{12,4},{16,24},{20,28},{24,16},{28,20},{1,9},{5... | collective-permute-start | bytes 589832 | tf_op jit(solution)/shard_map/ppermute | solution.py:189
  18.2 0.0 collective-permute-start.2
  18.2 5.0 %collective-permute-done.7.refs_6_ = f32[8,6144]{1,0:T(8,128)S(1)} collective-permute-done((f32[8,6144]{1,0:T(8,128)S(1)}, f32[8,6144]{1,0:T(8,128)S(1)}, u32[]{:S(2)}, u32[]{:S(2)}) %collective-permute-start.7) | collective-permute-done | bytes 196640 | tf_op jit(solution)/shard_map/ppermute | solution.py:189
  23.2 0.0 collective-permute-start.8
  23.2 2.4 %collective-permute-done.5.refs_4_ = f32[8,6144]{1,0:T(8,128)S(1)} collective-permute-done((f32[8,6144]{1,0:T(8,128)S(1)}, f32[8,6144]{1,0:T(8,128)S(1)}, u32[]{:S(2)}, u32[]{:S(2)}) %collective-permute-start.5) | collective-permute-done | bytes 196640 | tf_op jit(solution)/shard_map/ppermute | solution.py:189
  25.7 0.0 collective-permute-start.6
  25.7 0.1 collective-permute-done.3.refs_2_
  25.8 0.4 %collective-permute-start.4 = (f32[8,6144]{1,0:T(8,128)S(1)}, f32[8,6144]{1,0:T(8,128)S(1)}, u32[]{:S(2)}, u32[]{:S(2)}) collective-permute-start(f32[8,6144]{1,0:T(8,128)S(1)} %collective-permute-done.3.refs_2_), channel_id=1, source_target_pairs={{0,4},{4,0},{8,12},{12,8},{16,20},{20,16},{24,28},{28,24},{1,5},{5... | collective-permute-start | bytes 589832 | tf_op jit(solution)/shard_map/ppermute | solution.py:190
  26.2 0.0 collective-permute-done.2.refs_1_
  26.2 0.0 collective-permute-done.8.refs_7_
  26.2 0.9 %collective-permute-done.6.refs_5_ = f32[8,6144]{1,0:T(8,128)S(1)} collective-permute-done((f32[8,6144]{1,0:T(8,128)S(1)}, f32[8,6144]{1,0:T(8,128)S(1)}, u32[]{:S(2)}, u32[]{:S(2)}) %collective-permute-start.6) | collective-permute-done | bytes 196640 | tf_op jit(solution)/shard_map/ppermute | solution.py:190
  27.1 0.3 collective-permute-done.4.refs_3_
  27.4 1.1 %shard_map.30 = (f32[64,64]{1,0:T(8,128)S(1)}, bf16[128,6144]{1,0:T(8,128)(2,1)S(1)}) custom-call(s32[1]{0:T(128)} %bitcast.rank_ref, f32[8,6144]{1,0:T(8,128)S(1)} %shard_map.29.refs_0_, f32[8,6144]{1,0:T(8,128)S(1)} %collective-permute-done.2.refs_1_, f32[8,6144]{1,0:T(8,128)S(1)} %collective-permute-done.3.refs_2_, ...), custom_call_target="tpu_custom_call" | custom-call | bytes 1000000 | tf_op jit(solution)/shard_map/pallas_call | solution.py:157
  28.5 1.3 %collective-permute-start.11 = (f32[64,64]{1,0:T(8,128)S(1)}, f32[64,64]{1,0:T(8,128)S(1)}, u32[]{:S(2)}, u32[]{:S(2)}) collective-permute-start(f32[64,64]{1,0:T(8,128)S(1)} %get-tuple-element.7.refs_0_), channel_id=1, source_target_pairs={{0,3},{1,0},{2,1},{3,2},{4,7},{5,4},{6,5},{7,6},{8,11},{9,8},{10,9... | collective-permute-start | bytes 49160 | tf_op jit(solution)/shard_map/ppermute | solution.py:183
  29.8 1.7 %collective-permute-start.10 = (f32[64,64]{1,0:T(8,128)S(1)}, f32[64,64]{1,0:T(8,128)S(1)}, u32[]{:S(2)}, u32[]{:S(2)}) collective-permute-start(f32[64,64]{1,0:T(8,128)S(1)} %get-tuple-element.7.refs_0_), channel_id=1, source_target_pairs={{0,2},{1,3},{2,0},{3,1},{4,6},{5,7},{6,4},{7,5},{8,10},{9,11},{10,... | collective-permute-start | bytes 49160 | tf_op jit(solution)/shard_map/ppermute | solution.py:183
  31.6 0.0 collective-permute-start.9
  31.6 0.9 %collective-permute-done.11.refs_3_ = f32[64,64]{1,0:T(8,128)S(1)} collective-permute-done((f32[64,64]{1,0:T(8,128)S(1)}, f32[64,64]{1,0:T(8,128)S(1)}, u32[]{:S(2)}, u32[]{:S(2)}) %collective-permute-start.11) | collective-permute-done | bytes 16416 | tf_op jit(solution)/shard_map/ppermute | solution.py:183
  32.5 2.5 %collective-permute-done.10.refs_2_ = f32[64,64]{1,0:T(8,128)S(1)} collective-permute-done((f32[64,64]{1,0:T(8,128)S(1)}, f32[64,64]{1,0:T(8,128)S(1)}, u32[]{:S(2)}, u32[]{:S(2)}) %collective-permute-start.10) | collective-permute-done | bytes 16416 | tf_op jit(solution)/shard_map/ppermute | solution.py:183
  35.0 2.3 %collective-permute-done.9.refs_1_ = f32[64,64]{1,0:T(8,128)S(1)} collective-permute-done((f32[64,64]{1,0:T(8,128)S(1)}, f32[64,64]{1,0:T(8,128)S(1)}, u32[]{:S(2)}, u32[]{:S(2)}) %collective-permute-start.9) | collective-permute-done | bytes 16416 | tf_op jit(solution)/shard_map/ppermute | solution.py:183
  37.3 3.4 %shard_map.31 = f32[6,8,1024]{2,1,0:T(8,128)} custom-call(s32[1]{0:T(128)} %bitcast.rank_ref, f32[64,64]{1,0:T(8,128)S(1)} %get-tuple-element.7.refs_0_, f32[64,64]{1,0:T(8,128)S(1)} %collective-permute-done.9.refs_1_, f32[64,64]{1,0:T(8,128)S(1)} %collective-permute-done.10.refs_2_, f32[64,64]{1,0:T(8,128)S(1)} %collective-permute-done.11.refs_3_, ...), custom_call_target="tpu_custom_call" | custom-call | bytes 1000000 | tf_op jit(solution)/shard_map/pallas_call | solution.py:157
Async XLA Ops:
  0.0 10.7 %collective-permute-start.1 = (f32[6,8,1024]{2,1,0:T(8,128)}, f32[6,8,1024]{2,1,0:T(8,128)S(1)}, u32[]{:S(2)}, u32[]{:S(2)}) collective-permute-start(f32[6,8,1024]{2,1,0:T(8,128)} %bitcast.3), channel_id=1, source_target_pairs={{0,3},{1,0},{2,1},{3,2},{4,7},{5,4},{6,5},{7,6},{8,11},{9,8},{10,9... | collective-permute-start | bytes 589832 | tf_op jit(solution)/shard_map/ppermute | solution.py:225
  5.0 9.5 %collective-permute-start = (f32[6,8,1024]{2,1,0:T(8,128)}, f32[6,8,1024]{2,1,0:T(8,128)S(1)}, u32[]{:S(2)}, u32[]{:S(2)}) collective-permute-start(f32[6,8,1024]{2,1,0:T(8,128)} %bitcast.4), channel_id=1, source_target_pairs={{0,1},{1,2},{2,3},{3,0},{4,5},{5,6},{6,7},{7,4},{8,9},{9,10},{10,1... | collective-permute-start | bytes 589832 | tf_op jit(solution)/shard_map/ppermute | solution.py:224
  5.1 1.0 %copy-start = (f32[8,6,1024]{2,0,1:T(8,128)S(1)}, f32[8,6,1024]{2,0,1:T(8,128)}, u32[]{:S(2)}) copy-start(f32[8,6,1024]{2,0,1:T(8,128)} %param.2) | copy-start | bytes 589828
  6.0 0.8 %copy-start.1 = (f32[6,1024]{1,0:T(8,128)S(1)}, f32[6,1024]{1,0:T(8,128)}, u32[]{:S(2)}) copy-start(f32[6,1024]{1,0:T(8,128)} %pot_ref.1) | copy-start | bytes 73732
  14.6 8.6 %collective-permute-start.7 = (f32[8,6144]{1,0:T(8,128)S(1)}, f32[8,6144]{1,0:T(8,128)S(1)}, u32[]{:S(2)}, u32[]{:S(2)}) collective-permute-start(f32[8,6144]{1,0:T(8,128)S(1)} %shard_map.29.refs_0_), channel_id=1, source_target_pairs={{0,24},{4,28},{8,16},{12,20},{16,8},{20,12},{24,0},{28,4},{1,25},{... | collective-permute-start | bytes 589832 | tf_op jit(solution)/shard_map/ppermute | solution.py:189
  17.2 8.5 %collective-permute-start.5 = (f32[8,6144]{1,0:T(8,128)S(1)}, f32[8,6144]{1,0:T(8,128)S(1)}, u32[]{:S(2)}, u32[]{:S(2)}) collective-permute-start(f32[8,6144]{1,0:T(8,128)S(1)} %shard_map.29.refs_0_), channel_id=1, source_target_pairs={{0,16},{4,20},{8,24},{12,28},{16,0},{20,4},{24,8},{28,12},{1,17},{... | collective-permute-start | bytes 589832 | tf_op jit(solution)/shard_map/ppermute | solution.py:189
  17.7 8.1 %collective-permute-start.3 = (f32[8,6144]{1,0:T(8,128)S(1)}, f32[8,6144]{1,0:T(8,128)S(1)}, u32[]{:S(2)}, u32[]{:S(2)}) collective-permute-start(f32[8,6144]{1,0:T(8,128)S(1)} %shard_map.29.refs_0_), channel_id=1, source_target_pairs={{0,8},{4,12},{8,0},{12,4},{16,24},{20,28},{24,16},{28,20},{1,9},{5... | collective-permute-start | bytes 589832 | tf_op jit(solution)/shard_map/ppermute | solution.py:189
  18.2 8.0 %collective-permute-start.2 = (f32[8,6144]{1,0:T(8,128)S(1)}, f32[8,6144]{1,0:T(8,128)S(1)}, u32[]{:S(2)}, u32[]{:S(2)}) collective-permute-start(f32[8,6144]{1,0:T(8,128)S(1)} %shard_map.29.refs_0_), channel_id=1, source_target_pairs={{0,4},{4,0},{8,12},{12,8},{16,20},{20,16},{24,28},{28,24},{1,5},{5... | collective-permute-start | bytes 589832 | tf_op jit(solution)/shard_map/ppermute | solution.py:190
  23.2 3.0 %collective-permute-start.8 = (f32[8,6144]{1,0:T(8,128)S(1)}, f32[8,6144]{1,0:T(8,128)S(1)}, u32[]{:S(2)}, u32[]{:S(2)}) collective-permute-start(f32[8,6144]{1,0:T(8,128)S(1)} %collective-permute-done.7.refs_6_), channel_id=1, source_target_pairs={{0,4},{4,0},{8,12},{12,8},{16,20},{20,16},{24,28},{28,24},{1,5},{5... | collective-permute-start | bytes 589832 | tf_op jit(solution)/shard_map/ppermute | solution.py:190
  25.7 1.4 %collective-permute-start.6 = (f32[8,6144]{1,0:T(8,128)S(1)}, f32[8,6144]{1,0:T(8,128)S(1)}, u32[]{:S(2)}, u32[]{:S(2)}) collective-permute-start(f32[8,6144]{1,0:T(8,128)S(1)} %collective-permute-done.5.refs_4_), channel_id=1, source_target_pairs={{0,4},{4,0},{8,12},{12,8},{16,20},{20,16},{24,28},{28,24},{1,5},{5... | collective-permute-start | bytes 589832 | tf_op jit(solution)/shard_map/ppermute | solution.py:190
  25.8 1.6 %collective-permute-start.4 = (f32[8,6144]{1,0:T(8,128)S(1)}, f32[8,6144]{1,0:T(8,128)S(1)}, u32[]{:S(2)}, u32[]{:S(2)}) collective-permute-start(f32[8,6144]{1,0:T(8,128)S(1)} %collective-permute-done.3.refs_2_), channel_id=1, source_target_pairs={{0,4},{4,0},{8,12},{12,8},{16,20},{20,16},{24,28},{28,24},{1,5},{5... | collective-permute-start | bytes 589832 | tf_op jit(solution)/shard_map/ppermute | solution.py:190
  28.5 4.0 %collective-permute-start.11 = (f32[64,64]{1,0:T(8,128)S(1)}, f32[64,64]{1,0:T(8,128)S(1)}, u32[]{:S(2)}, u32[]{:S(2)}) collective-permute-start(f32[64,64]{1,0:T(8,128)S(1)} %get-tuple-element.7.refs_0_), channel_id=1, source_target_pairs={{0,3},{1,0},{2,1},{3,2},{4,7},{5,4},{6,5},{7,6},{8,11},{9,8},{10,9... | collective-permute-start | bytes 49160 | tf_op jit(solution)/shard_map/ppermute | solution.py:183
  29.8 5.2 %collective-permute-start.10 = (f32[64,64]{1,0:T(8,128)S(1)}, f32[64,64]{1,0:T(8,128)S(1)}, u32[]{:S(2)}, u32[]{:S(2)}) collective-permute-start(f32[64,64]{1,0:T(8,128)S(1)} %get-tuple-element.7.refs_0_), channel_id=1, source_target_pairs={{0,2},{1,3},{2,0},{3,1},{4,6},{5,7},{6,4},{7,5},{8,10},{9,11},{10,... | collective-permute-start | bytes 49160 | tf_op jit(solution)/shard_map/ppermute | solution.py:183
  31.6 5.7 %collective-permute-start.9 = (f32[64,64]{1,0:T(8,128)S(1)}, f32[64,64]{1,0:T(8,128)S(1)}, u32[]{:S(2)}, u32[]{:S(2)}) collective-permute-start(f32[64,64]{1,0:T(8,128)S(1)} %get-tuple-element.7.refs_0_), channel_id=1, source_target_pairs={{0,1},{1,2},{2,3},{3,0},{4,5},{5,6},{6,7},{7,4},{8,9},{9,10},{10,1... | collective-permute-start | bytes 49160 | tf_op jit(solution)/shard_map/ppermute | solution.py:183

commit v3 on v2

--- a/solution.py
+++ b/solution.py
@@ -46,7 +46,17 @@
         out_ref[:, p * plane : (p + 1) * plane] = acc
 
 
-def couple_kernel(local_ref, before_ref, after_ref, out_ref):
+def couple_kernel(swap_ref, local_ref, one_ref, two_ref, out_ref):
+    @pl.when(swap_ref[0] == 0)
+    def _():
+        couple(local_ref, one_ref, two_ref, out_ref)
+
+    @pl.when(swap_ref[0] == 1)
+    def _():
+        couple(local_ref, two_ref, one_ref, out_ref)
+
+
+def couple(local_ref, before_ref, after_ref, out_ref):
     rim, count, plane = before_ref.shape
     depth = out_ref.shape[1] // plane
     for p in range(depth):
@@ -177,10 +187,24 @@
     return jax.ShapeDtypeStruct(dims, dtype)
 
 
+def halo(planes, grid):
+    depth = planes.shape[0]
+    if grid == 4 and depth == RIM:
+        one = lax.ppermute(planes, "grid", exchange(grid, 3))
+        two = lax.ppermute(planes, "grid", exchange(grid, 1))
+        return one, two, (lax.axis_index("grid") % 2).astype(jnp.int32).reshape(1)
+    before = lax.ppermute(planes[depth - RIM :], "grid", rotation(grid, 1))
+    after = lax.ppermute(planes[:RIM], "grid", rotation(grid, -1))
+    return before, after, jnp.zeros((1,), jnp.int32)
+
+
 def grid_sum(part, grid):
     if grid > 4:
         return [lax.psum(part, "grid")]
-    return [part] + [lax.ppermute(part, "grid", rotation(grid, k)) for k in range(1, grid)]
+    masks = (1, 3, 2) if grid == 4 else range(1, grid)
+    paired = grid & (grid - 1) == 0
+    pairs = [exchange(grid, k) if paired else rotation(grid, k) for k in masks]
+    return [part] + [lax.ppermute(part, "grid", pair) for pair in pairs]
 
 
 def gather_all(work, orb):
@@ -221,10 +245,9 @@
     members = min(PANEL * NPANEL // count, orb)
     total = members * count
     scale = 1.0 / (cells * grid)
-    before = lax.ppermute(planes[depth - RIM :], "grid", rotation(grid, 1))
-    after = lax.ppermute(planes[:RIM], "grid", rotation(grid, -1))
+    one, two, swap = halo(planes, grid)
     local = call(local_kernel, shape(count, cells), [planes, potential], flops=10**9)
-    work = call(couple_kernel, shape(count, cells), [local, before, after])
+    work = call(couple_kernel, shape(count, cells), [swap, local, one, two])
     rank = lax.axis_index("orb").astype(jnp.int32)
     everyone = members == orb and orb & (orb - 1) == 0
     blocks = gather_all(work, orb) if everyone else gather_leading(work, rank, members)

time: 40.9 us -> 38 us (0.929)
  waiting for transfers between devices: 21.3 us -> 17.5 us
  starting transfers between devices: 12.1 us -> 13 us
    ppermute x5, waiting for transfers between devices: 12.5 us -> 8.87 us  [the longest x1 6 us: halo(): one = lax.ppermute(planes, 'grid', exchange(grid, 3))]
    ppermute x5, starting transfers between devices: 8.14 us -> 9.04 us  [the longest x3 3.55 us: grid_sum(): return [part] + [lax.ppermute(part, 'grid', pair) for pair in pairs]]
  transfers between devices with their start and end apart: 12 -> 12, of which waited for: 10 -> 9; matrix products, arithmetic and copies ran while one was open for 0% -> 0% of each run, Pallas kernels for 2% -> 2%
where the time goes in v3:
time: 38 us; the launch traced here: 37.8 us
  waiting for transfers between devices  17.5 us (46%)
  starting transfers between devices  13 us (34%)
  Pallas kernels  5.48 us (14%)
  local copies, waits for them, and re-layouts  1.72 us (5%)
    ppermute x3, waiting for transfers between devices, gather_all(): lax.ppermute(work, 'orb', exchange(orb, chip))  7.42 us
    ppermute x1, waiting for transfers between devices, halo(): one = lax.ppermute(planes, 'grid', exchange(grid, 3))  6 us
    pallas_call x4, Pallas kernels, call(): pl.pallas_call(kernel, out_shape=out_shape, in_specs=in_specs, out_specs=...  5.48 us
    ppermute x3, starting transfers between devices, gather_all(): lax.ppermute(work, 'orb', exchange(orb, chip))  3.55 us
    ppermute x3, starting transfers between devices, grid_sum(): return [part] + [lax.ppermute(part, 'grid', pair) for pair in pairs]  3.55 us
    ppermute x1, starting transfers between devices, halo(): two = lax.ppermute(planes, 'grid', exchange(grid, 1))  3.02 us
    ppermute x1, starting transfers between devices, halo(): one = lax.ppermute(planes, 'grid', exchange(grid, 3))  2.47 us
    ppermute x3, waiting for transfers between devices, grid_sum(): return [part] + [lax.ppermute(part, 'grid', pair) for pair in pairs]  2.38 us
  transfers between devices with their start and end apart: 12, of which 9 were waited for; matrix products, arithmetic and copies ran while one was open for 0% of the time, Pallas kernels for 2%

profile of v3, /device:TPU:0, one launch (start us, length us, event | category | flops | bytes accessed | tf_op | source)
XLA Modules:
  0.0 37.8 jit_solution(3384083460764687589)
XLA Ops:
  0.0 3.0 %collective-permute-start.1 = (f32[6,8,1024]{2,1,0:T(8,128)}, f32[6,8,1024]{2,1,0:T(8,128)S(1)}, u32[]{:S(2)}, u32[]{:S(2)}) collective-permute-start(f32[6,8,1024]{2,1,0:T(8,128)} %bitcast.4), channel_id=1, source_target_pairs={{0,1},{1,0},{2,3},{3,2},{4,5},{5,4},{6,7},{7,6},{8,9},{9,8},{10,11... | collective-permute-start | bytes 589832 | tf_op jit(solution)/shard_map/ppermute | solution.py:194
  3.0 2.5 %collective-permute-start = (f32[6,8,1024]{2,1,0:T(8,128)}, f32[6,8,1024]{2,1,0:T(8,128)S(1)}, u32[]{:S(2)}, u32[]{:S(2)}) collective-permute-start(f32[6,8,1024]{2,1,0:T(8,128)} %bitcast.5), channel_id=1, source_target_pairs={{0,3},{1,2},{2,1},{3,0},{4,7},{5,6},{6,5},{7,4},{8,11},{9,10},{10,... | collective-permute-start | bytes 589832 | tf_op jit(solution)/shard_map/ppermute | solution.py:193
  5.5 0.0 copy-start
  5.5 1.0 %copy-done = f32[8,6,1024]{2,0,1:T(8,128)S(1)} copy-done((f32[8,6,1024]{2,0,1:T(8,128)S(1)}, f32[8,6,1024]{2,0,1:T(8,128)}, u32[]{:S(2)}) %copy-start) | copy-done | bytes 196632
  6.5 0.0 copy-start.1
  6.5 0.8 %copy-done.1 = f32[6,1024]{1,0:T(8,128)S(1)} copy-done((f32[6,1024]{1,0:T(8,128)S(1)}, f32[6,1024]{1,0:T(8,128)}, u32[]{:S(2)}) %copy-start.1) | copy-done | bytes 24600
  7.2 0.9 %shard_map.28.local_ref = f32[8,6144]{1,0:T(8,128)S(1)} custom-call(f32[6,8,1024]{2,1,0:T(8,128)S(1)} %bitcast.6, f32[6,1024]{1,0:T(8,128)S(1)} %copy-done.1), custom_call_target="tpu_custom_call" | custom-call | flops 1000000000 | bytes 1000000 | tf_op jit(solution)/shard_map/pallas_call | solution.py:167
  8.2 0.5 %collective-permute-done.1.two_ref = f32[6,8,1024]{2,1,0:T(8,128)S(1)} collective-permute-done((f32[6,8,1024]{2,1,0:T(8,128)}, f32[6,8,1024]{2,1,0:T(8,128)S(1)}, u32[]{:S(2)}, u32[]{:S(2)}) %collective-permute-start.1) | collective-permute-done | bytes 196640 | tf_op jit(solution)/shard_map/ppermute | solution.py:194
  8.6 6.0 %collective-permute-done.one_ref = f32[6,8,1024]{2,1,0:T(8,128)S(1)} collective-permute-done((f32[6,8,1024]{2,1,0:T(8,128)}, f32[6,8,1024]{2,1,0:T(8,128)S(1)}, u32[]{:S(2)}, u32[]{:S(2)}) %collective-permute-start) | collective-permute-done | bytes 196640 | tf_op jit(solution)/shard_map/ppermute | solution.py:193
  14.6 0.1 shard_map.29.refs_0_
  14.8 2.5 %collective-permute-start.7 = (f32[8,6144]{1,0:T(8,128)S(1)}, f32[8,6144]{1,0:T(8,128)S(1)}, u32[]{:S(2)}, u32[]{:S(2)}) collective-permute-start(f32[8,6144]{1,0:T(8,128)S(1)} %shard_map.29.refs_0_), channel_id=1, source_target_pairs={{0,24},{4,28},{8,16},{12,20},{16,8},{20,12},{24,0},{28,4},{1,25},{... | collective-permute-start | bytes 589832 | tf_op jit(solution)/shard_map/ppermute | solution.py:213
  17.3 0.5 %collective-permute-start.5 = (f32[8,6144]{1,0:T(8,128)S(1)}, f32[8,6144]{1,0:T(8,128)S(1)}, u32[]{:S(2)}, u32[]{:S(2)}) collective-permute-start(f32[8,6144]{1,0:T(8,128)S(1)} %shard_map.29.refs_0_), channel_id=1, source_target_pairs={{0,16},{4,20},{8,24},{12,28},{16,0},{20,4},{24,8},{28,12},{1,17},{... | collective-permute-start | bytes 589832 | tf_op jit(solution)/shard_map/ppermute | solution.py:213
  17.8 0.5 %collective-permute-start.3 = (f32[8,6144]{1,0:T(8,128)S(1)}, f32[8,6144]{1,0:T(8,128)S(1)}, u32[]{:S(2)}, u32[]{:S(2)}) collective-permute-start(f32[8,6144]{1,0:T(8,128)S(1)} %shard_map.29.refs_0_), channel_id=1, source_target_pairs={{0,8},{4,12},{8,0},{12,4},{16,24},{20,28},{24,16},{28,20},{1,9},{5... | collective-permute-start | bytes 589832 | tf_op jit(solution)/shard_map/ppermute | solution.py:213
  18.3 0.0 collective-permute-start.2
  18.3 4.9 %collective-permute-done.7.refs_6_ = f32[8,6144]{1,0:T(8,128)S(1)} collective-permute-done((f32[8,6144]{1,0:T(8,128)S(1)}, f32[8,6144]{1,0:T(8,128)S(1)}, u32[]{:S(2)}, u32[]{:S(2)}) %collective-permute-start.7) | collective-permute-done | bytes 196640 | tf_op jit(solution)/shard_map/ppermute | solution.py:213
  23.2 0.0 collective-permute-start.8
  23.2 2.4 %collective-permute-done.5.refs_4_ = f32[8,6144]{1,0:T(8,128)S(1)} collective-permute-done((f32[8,6144]{1,0:T(8,128)S(1)}, f32[8,6144]{1,0:T(8,128)S(1)}, u32[]{:S(2)}, u32[]{:S(2)}) %collective-permute-start.5) | collective-permute-done | bytes 196640 | tf_op jit(solution)/shard_map/ppermute | solution.py:213
  25.6 0.0 collective-permute-start.6
  25.6 0.1 collective-permute-done.3.refs_2_
  25.7 0.4 %collective-permute-start.4 = (f32[8,6144]{1,0:T(8,128)S(1)}, f32[8,6144]{1,0:T(8,128)S(1)}, u32[]{:S(2)}, u32[]{:S(2)}) collective-permute-start(f32[8,6144]{1,0:T(8,128)S(1)} %collective-permute-done.3.refs_2_), channel_id=1, source_target_pairs={{0,4},{4,0},{8,12},{12,8},{16,20},{20,16},{24,28},{28,24},{1,5},{5... | collective-permute-start | bytes 589832 | tf_op jit(solution)/shard_map/ppermute | solution.py:214
  26.2 0.0 collective-permute-done.2.refs_1_
  26.2 0.0 collective-permute-done.8.refs_7_
  26.2 0.9 %collective-permute-done.6.refs_5_ = f32[8,6144]{1,0:T(8,128)S(1)} collective-permute-done((f32[8,6144]{1,0:T(8,128)S(1)}, f32[8,6144]{1,0:T(8,128)S(1)}, u32[]{:S(2)}, u32[]{:S(2)}) %collective-permute-start.6) | collective-permute-done | bytes 196640 | tf_op jit(solution)/shard_map/ppermute | solution.py:214
  27.1 0.3 collective-permute-done.4.refs_3_
  27.4 1.1 %shard_map.30 = (f32[64,64]{1,0:T(8,128)S(1)}, bf16[128,6144]{1,0:T(8,128)(2,1)S(1)}) custom-call(s32[1]{0:T(128)} %bitcast.rank_ref, f32[8,6144]{1,0:T(8,128)S(1)} %shard_map.29.refs_0_, f32[8,6144]{1,0:T(8,128)S(1)} %collective-permute-done.2.refs_1_, f32[8,6144]{1,0:T(8,128)S(1)} %collective-permute-done.3.refs_2_, ...), custom_call_target="tpu_custom_call" | custom-call | bytes 1000000 | tf_op jit(solution)/shard_map/pallas_call | solution.py:167
  28.5 0.1 collective-permute-start.11
  28.5 1.4 %collective-permute-start.10 = (f32[64,64]{1,0:T(8,128)S(1)}, f32[64,64]{1,0:T(8,128)S(1)}, u32[]{:S(2)}, u32[]{:S(2)}) collective-permute-start(f32[64,64]{1,0:T(8,128)S(1)} %get-tuple-element.7.refs_0_), channel_id=1, source_target_pairs={{0,3},{1,2},{2,1},{3,0},{4,7},{5,6},{6,5},{7,4},{8,11},{9,10},{10,... | collective-permute-start | bytes 49160 | tf_op jit(solution)/shard_map/ppermute | solution.py:207
  29.9 2.1 %collective-permute-start.9 = (f32[64,64]{1,0:T(8,128)S(1)}, f32[64,64]{1,0:T(8,128)S(1)}, u32[]{:S(2)}, u32[]{:S(2)}) collective-permute-start(f32[64,64]{1,0:T(8,128)S(1)} %get-tuple-element.7.refs_0_), channel_id=1, source_target_pairs={{0,1},{1,0},{2,3},{3,2},{4,5},{5,4},{6,7},{7,6},{8,9},{9,8},{10,11... | collective-permute-start | bytes 49160 | tf_op jit(solution)/shard_map/ppermute | solution.py:207
  32.0 1.7 %collective-permute-done.11.refs_3_ = f32[64,64]{1,0:T(8,128)S(1)} collective-permute-done((f32[64,64]{1,0:T(8,128)S(1)}, f32[64,64]{1,0:T(8,128)S(1)}, u32[]{:S(2)}, u32[]{:S(2)}) %collective-permute-start.11) | collective-permute-done | bytes 16416 | tf_op jit(solution)/shard_map/ppermute | solution.py:207
  33.7 0.7 %collective-permute-done.10.refs_2_ = f32[64,64]{1,0:T(8,128)S(1)} collective-permute-done((f32[64,64]{1,0:T(8,128)S(1)}, f32[64,64]{1,0:T(8,128)S(1)}, u32[]{:S(2)}, u32[]{:S(2)}) %collective-permute-start.10) | collective-permute-done | bytes 16416 | tf_op jit(solution)/shard_map/ppermute | solution.py:207
  34.4 0.0 collective-permute-done.9.refs_1_
  34.4 3.4 %shard_map.31 = f32[6,8,1024]{2,1,0:T(8,128)} custom-call(s32[1]{0:T(128)} %bitcast.rank_ref, f32[64,64]{1,0:T(8,128)S(1)} %get-tuple-element.7.refs_0_, f32[64,64]{1,0:T(8,128)S(1)} %collective-permute-done.9.refs_1_, f32[64,64]{1,0:T(8,128)S(1)} %collective-permute-done.10.refs_2_, f32[64,64]{1,0:T(8,128)S(1)} %collective-permute-done.11.refs_3_, ...), custom_call_target="tpu_custom_call" | custom-call | bytes 1000000 | tf_op jit(solution)/shard_map/pallas_call | solution.py:167
Async XLA Ops:
  0.0 8.6 %collective-permute-start.1 = (f32[6,8,1024]{2,1,0:T(8,128)}, f32[6,8,1024]{2,1,0:T(8,128)S(1)}, u32[]{:S(2)}, u32[]{:S(2)}) collective-permute-start(f32[6,8,1024]{2,1,0:T(8,128)} %bitcast.4), channel_id=1, source_target_pairs={{0,1},{1,0},{2,3},{3,2},{4,5},{5,4},{6,7},{7,6},{8,9},{9,8},{10,11... | collective-permute-start | bytes 589832 | tf_op jit(solution)/shard_map/ppermute | solution.py:194
  3.0 11.6 %collective-permute-start = (f32[6,8,1024]{2,1,0:T(8,128)}, f32[6,8,1024]{2,1,0:T(8,128)S(1)}, u32[]{:S(2)}, u32[]{:S(2)}) collective-permute-start(f32[6,8,1024]{2,1,0:T(8,128)} %bitcast.5), channel_id=1, source_target_pairs={{0,3},{1,2},{2,1},{3,0},{4,7},{5,6},{6,5},{7,4},{8,11},{9,10},{10,... | collective-permute-start | bytes 589832 | tf_op jit(solution)/shard_map/ppermute | solution.py:193
  5.5 1.0 %copy-start = (f32[8,6,1024]{2,0,1:T(8,128)S(1)}, f32[8,6,1024]{2,0,1:T(8,128)}, u32[]{:S(2)}) copy-start(f32[8,6,1024]{2,0,1:T(8,128)} %param.2) | copy-start | bytes 589828
  6.5 0.8 %copy-start.1 = (f32[6,1024]{1,0:T(8,128)S(1)}, f32[6,1024]{1,0:T(8,128)}, u32[]{:S(2)}) copy-start(f32[6,1024]{1,0:T(8,128)} %pot_ref.1) | copy-start | bytes 73732
  14.8 8.4 %collective-permute-start.7 = (f32[8,6144]{1,0:T(8,128)S(1)}, f32[8,6144]{1,0:T(8,128)S(1)}, u32[]{:S(2)}, u32[]{:S(2)}) collective-permute-start(f32[8,6144]{1,0:T(8,128)S(1)} %shard_map.29.refs_0_), channel_id=1, source_target_pairs={{0,24},{4,28},{8,16},{12,20},{16,8},{20,12},{24,0},{28,4},{1,25},{... | collective-permute-start | bytes 589832 | tf_op jit(solution)/shard_map/ppermute | solution.py:213
  17.3 8.4 %collective-permute-start.5 = (f32[8,6144]{1,0:T(8,128)S(1)}, f32[8,6144]{1,0:T(8,128)S(1)}, u32[]{:S(2)}, u32[]{:S(2)}) collective-permute-start(f32[8,6144]{1,0:T(8,128)S(1)} %shard_map.29.refs_0_), channel_id=1, source_target_pairs={{0,16},{4,20},{8,24},{12,28},{16,0},{20,4},{24,8},{28,12},{1,17},{... | collective-permute-start | bytes 589832 | tf_op jit(solution)/shard_map/ppermute | solution.py:213
  17.8 8.0 %collective-permute-start.3 = (f32[8,6144]{1,0:T(8,128)S(1)}, f32[8,6144]{1,0:T(8,128)S(1)}, u32[]{:S(2)}, u32[]{:S(2)}) collective-permute-start(f32[8,6144]{1,0:T(8,128)S(1)} %shard_map.29.refs_0_), channel_id=1, source_target_pairs={{0,8},{4,12},{8,0},{12,4},{16,24},{20,28},{24,16},{28,20},{1,9},{5... | collective-permute-start | bytes 589832 | tf_op jit(solution)/shard_map/ppermute | solution.py:213
  18.3 7.8 %collective-permute-start.2 = (f32[8,6144]{1,0:T(8,128)S(1)}, f32[8,6144]{1,0:T(8,128)S(1)}, u32[]{:S(2)}, u32[]{:S(2)}) collective-permute-start(f32[8,6144]{1,0:T(8,128)S(1)} %shard_map.29.refs_0_), channel_id=1, source_target_pairs={{0,4},{4,0},{8,12},{12,8},{16,20},{20,16},{24,28},{28,24},{1,5},{5... | collective-permute-start | bytes 589832 | tf_op jit(solution)/shard_map/ppermute | solution.py:214
  23.2 3.0 %collective-permute-start.8 = (f32[8,6144]{1,0:T(8,128)S(1)}, f32[8,6144]{1,0:T(8,128)S(1)}, u32[]{:S(2)}, u32[]{:S(2)}) collective-permute-start(f32[8,6144]{1,0:T(8,128)S(1)} %collective-permute-done.7.refs_6_), channel_id=1, source_target_pairs={{0,4},{4,0},{8,12},{12,8},{16,20},{20,16},{24,28},{28,24},{1,5},{5... | collective-permute-start | bytes 589832 | tf_op jit(solution)/shard_map/ppermute | solution.py:214
  25.6 1.4 %collective-permute-start.6 = (f32[8,6144]{1,0:T(8,128)S(1)}, f32[8,6144]{1,0:T(8,128)S(1)}, u32[]{:S(2)}, u32[]{:S(2)}) collective-permute-start(f32[8,6144]{1,0:T(8,128)S(1)} %collective-permute-done.5.refs_4_), channel_id=1, source_target_pairs={{0,4},{4,0},{8,12},{12,8},{16,20},{20,16},{24,28},{28,24},{1,5},{5... | collective-permute-start | bytes 589832 | tf_op jit(solution)/shard_map/ppermute | solution.py:214
  25.7 1.6 %collective-permute-start.4 = (f32[8,6144]{1,0:T(8,128)S(1)}, f32[8,6144]{1,0:T(8,128)S(1)}, u32[]{:S(2)}, u32[]{:S(2)}) collective-permute-start(f32[8,6144]{1,0:T(8,128)S(1)} %collective-permute-done.3.refs_2_), channel_id=1, source_target_pairs={{0,4},{4,0},{8,12},{12,8},{16,20},{20,16},{24,28},{28,24},{1,5},{5... | collective-permute-start | bytes 589832 | tf_op jit(solution)/shard_map/ppermute | solution.py:214
  28.5 5.2 %collective-permute-start.11 = (f32[64,64]{1,0:T(8,128)S(1)}, f32[64,64]{1,0:T(8,128)S(1)}, u32[]{:S(2)}, u32[]{:S(2)}) collective-permute-start(f32[64,64]{1,0:T(8,128)S(1)} %get-tuple-element.7.refs_0_), channel_id=1, source_target_pairs={{0,2},{1,3},{2,0},{3,1},{4,6},{5,7},{6,4},{7,5},{8,10},{9,11},{10,... | collective-permute-start | bytes 49160 | tf_op jit(solution)/shard_map/ppermute | solution.py:207
  28.5 5.8 %collective-permute-start.10 = (f32[64,64]{1,0:T(8,128)S(1)}, f32[64,64]{1,0:T(8,128)S(1)}, u32[]{:S(2)}, u32[]{:S(2)}) collective-permute-start(f32[64,64]{1,0:T(8,128)S(1)} %get-tuple-element.7.refs_0_), channel_id=1, source_target_pairs={{0,3},{1,2},{2,1},{3,0},{4,7},{5,6},{6,5},{7,4},{8,11},{9,10},{10,... | collective-permute-start | bytes 49160 | tf_op jit(solution)/shard_map/ppermute | solution.py:207
  29.9 4.4 %collective-permute-start.9 = (f32[64,64]{1,0:T(8,128)S(1)}, f32[64,64]{1,0:T(8,128)S(1)}, u32[]{:S(2)}, u32[]{:S(2)}) collective-permute-start(f32[64,64]{1,0:T(8,128)S(1)} %get-tuple-element.7.refs_0_), channel_id=1, source_target_pairs={{0,1},{1,0},{2,3},{3,2},{4,5},{5,4},{6,7},{7,6},{8,9},{9,8},{10,11... | collective-permute-start | bytes 49160 | tf_op jit(solution)/shard_map/ppermute | solution.py:207

commit v4 on v3

--- a/solution.py
+++ b/solution.py
@@ -22,7 +22,8 @@
 )
 HIGH = lax.Precision.HIGHEST
 RIM = 6
-LANES = 128
+LAST = 6
+BOTH = ("orb", "grid")
 
 
 def local_kernel(v_ref, pot_ref, out_ref):
@@ -69,26 +70,61 @@
         out_ref[:, p * plane : (p + 1) * plane] = acc
 
 
-def gram_kernel(scale, rank_ref, *refs):
+def place(rank, mask, rows):
+    return pl.multiple_of((rank // 2 ^ mask // 2) * rows, rows)
+
+
+def store_pair(rank, mask, one_ref, two_ref, stack_ref):
+    odd = rank % 2 == 1
+    one, two = one_ref[...], two_ref[...]
+    pair = jnp.concatenate([jnp.where(odd, two, one), jnp.where(odd, one, two)], 0)
+    high = pair.astype(jnp.bfloat16)
+    low = (pair - high.astype(jnp.float32)).astype(jnp.bfloat16)
+    rows, half = pair.shape[0], stack_ref.shape[0] // 2
+    first = place(rank, mask, rows)
+    stack_ref[pl.ds(first, rows), :] = high
+    stack_ref[pl.ds(half + first, rows), :] = low
+    return jnp.concatenate([high, low], 0)
+
+
+def products(left, right, scale):
+    every = lax.dot_general(
+        left, right, (((1,), (1,)), ((), ())), preferred_element_type=jnp.float32
+    )
+    rows, columns = left.shape[0] // 2, right.shape[0] // 2
+    both = every[:rows] + every[rows:]
+    return (both[:, :columns] + both[:, columns:]) * scale
+
+
+def gram_kernel(scale, masks, rank_ref, *refs):
     blocks, (gram_ref, stack_ref) = refs[:-2], refs[-2:]
-    count = blocks[0].shape[0]
-    total = count * len(blocks)
+    rows = 2 * blocks[0].shape[0]
+    half = stack_ref.shape[0] // 2
     rank = rank_ref[0]
-    odd = rank % 2 == 1
-    for k in range(0, len(blocks), 2):
-        one, two = blocks[k][...], blocks[k + 1][...]
-        pair = jnp.concatenate([jnp.where(odd, two, one), jnp.where(odd, one, two)], 0)
-        high = pair.astype(jnp.bfloat16)
-        low = (pair - high.astype(jnp.float32)).astype(jnp.bfloat16)
-        first = pl.multiple_of((rank // 2 ^ k // 2) * (2 * count), 2 * count)
-        stack_ref[pl.ds(first, 2 * count), :] = high
-        stack_ref[pl.ds(total + first, 2 * count), :] = low
+    missing = place(rank, LAST, rows)
+    blank = jnp.zeros((rows, stack_ref.shape[1]), jnp.bfloat16)
+    stack_ref[pl.ds(missing, rows), :] = blank
+    stack_ref[pl.ds(half + missing, rows), :] = blank
+    for k, mask in enumerate(masks):
+        store_pair(rank, mask, blocks[2 * k], blocks[2 * k + 1], stack_ref)
     whole = stack_ref[...]
-    products = lax.dot_general(
-        whole, whole, (((1,), (1,)), ((), ())), preferred_element_type=jnp.float32
-    )
-    gram = products[:total] + products[total:]
-    gram_ref[...] = (gram[:, :total] + gram[:, total:]) * scale
+    gram_ref[...] = products(whole, whole, scale)
+
+
+def last_kernel(scale, rank_ref, one_ref, two_ref, early_ref, before_ref, gram_ref, stack_ref):
+    rank = rank_ref[0]
+    rows = 2 * one_ref.shape[0]
+    total = gram_ref.shape[0]
+    pair = store_pair(rank, LAST, one_ref, two_ref, stack_ref)
+    lines = products(pair, stack_ref[...], scale)
+    repeated = jnp.concatenate([lines] * (total // rows), 0)
+    first = place(rank, LAST, rows)
+    row = lax.broadcasted_iota(jnp.int32, (total, total), 0)
+    column = lax.broadcasted_iota(jnp.int32, (total, total), 1)
+    gram = jnp.where(
+        (column >= first) & (column < first + rows), repeated.T, early_ref[...]
+    )
+    gram_ref[...] = jnp.where((row >= first) & (row < first + rows), repeated, gram)
 
 
 def invert_factor(gram):
@@ -99,39 +135,44 @@
         lax.broadcasted_iota(jnp.int32, (size, size), 0)
         == lax.broadcasted_iota(jnp.int32, (size, size), 1)
     ).astype(jnp.float32)
+    zero = lax.broadcasted_iota(jnp.int32, full, 1).astype(jnp.float32) * 0.0
     whole = jnp.concatenate([gram, ident], 1)
     tiles = [whole[i : i + rows] for i in range(0, size, rows)]
     done = []
     for t in range(len(tiles)):
-        later = range(t + 1, len(tiles))
-        columns = {
-            i: [
-                jnp.broadcast_to(tiles[i][:, t * rows + a : t * rows + a + 1], full)
-                for a in range(rows)
+
+        def columns(i):
+            first = t * rows
+            return [
+                jnp.broadcast_to(tiles[i][:, first + a : first + a + 1], full) for a in range(rows)
             ]
-            for i in (t, *later)
-        }
+
+        own = [column + zero for column in columns(t)]
+        after = columns(t + 1) if t + 1 < len(tiles) else None
         line = [jnp.broadcast_to(tiles[t][a : a + 1], full) for a in range(rows)]
         pivot = [
-            [jnp.broadcast_to(columns[t][b][a : a + 1], full) for b in range(a + 1)]
-            for a in range(rows)
+            [jnp.broadcast_to(own[b][a : a + 1], full) for b in range(a + 1)] for a in range(rows)
         ]
         factor = [[None] * rows for _ in range(rows)]
-        inverse = []
+        scaled = []
         for a in range(rows):
-            inverse.append(1.0 / pivot[a][a])
+            inverse = 1.0 / pivot[a][a]
+            scaled.append(line[a] * inverse)
             for b in range(a + 1, rows):
-                factor[b][a] = pivot[b][a] * inverse[a]
+                factor[b][a] = pivot[b][a] * inverse
                 line[b] = line[b] - factor[b][a] * line[a]
                 for c in range(a + 1, b + 1):
                     pivot[b][c] = pivot[b][c] - factor[b][a] * pivot[c][a]
+            if after is not None:
+                tiles[t + 1] = tiles[t + 1] - after[a] * scaled[a]
+                for b in range(a + 1, rows):
+                    after[b] = after[b] - factor[b][a] * after[a]
         done += [(line[a] * lax.rsqrt(pivot[a][a]))[:1] for a in range(rows)]
-        solved = [line[a] * inverse[a] for a in range(rows)]
         for a in range(rows - 1, -1, -1):
             for b in range(a):
-                solved[b] = solved[b] - factor[a][b] * solved[a]
-        for i in later:
-            terms = [columns[i][a] * solved[a] for a in range(rows)]
+                scaled[b] = scaled[b] - factor[a][b] * scaled[a]
+        for i in range(t + 2, len(tiles)):
+            terms = [column * scaled[a] for a, column in enumerate(columns(i))]
             while len(terms) > 1:
                 terms = [terms[k] + terms[k + 1] for k in range(0, len(terms), 2)]
             tiles[i] = tiles[i] - terms[0]
@@ -158,7 +199,7 @@
         out_ref[p] = both[:count] + both[count:]
 
 
-def call(kernel, out_shape, inputs, scratch=(), flops=0):
+def call(kernel, out_shape, inputs, scratch=(), flops=0, aliases=None):
     in_specs = [
         pl.BlockSpec(memory_space=pltpu.SMEM if a.dtype == jnp.int32 else pltpu.VMEM)
         for a in inputs
@@ -170,6 +211,7 @@
         in_specs=in_specs,
         out_specs=out_specs,
         scratch_shapes=scratch,
+        input_output_aliases=aliases or {},
         compiler_params=pltpu.CompilerParams(vmem_limit_bytes=32 * 2**20),
         cost_estimate=pl.CostEstimate(flops=flops, bytes_accessed=10**6, transcendentals=0),
     )(*inputs)
@@ -179,6 +221,14 @@
     return [(i, (i + step) % peers) for i in range(peers)]
 
 
+def partners(orb, grid, masks, core=0):
+    return [
+        (o * grid + g, (o ^ core) * grid + (g ^ masks[o % 2]))
+        for o in range(orb)
+        for g in range(grid)
+    ]
+
+
 def exchange(peers, mask):
     return [(i, i ^ mask) for i in range(peers)]
 
@@ -187,32 +237,43 @@
     return jax.ShapeDtypeStruct(dims, dtype)
 
 
-def halo(planes, grid):
+def halo(planes, orb, grid):
     depth = planes.shape[0]
     if grid == 4 and depth == RIM:
-        one = lax.ppermute(planes, "grid", exchange(grid, 3))
-        two = lax.ppermute(planes, "grid", exchange(grid, 1))
-        return one, two, (lax.axis_index("grid") % 2).astype(jnp.int32).reshape(1)
+        one = lax.ppermute(planes, BOTH, partners(orb, grid, (3, 1)))
+        two = lax.ppermute(planes, BOTH, partners(orb, grid, (1, 3)))
+        swap = (lax.axis_index("grid") + lax.axis_index("orb")) % 2
+        return one, two, swap.astype(jnp.int32).reshape(1)
     before = lax.ppermute(planes[depth - RIM :], "grid", rotation(grid, 1))
     after = lax.ppermute(planes[:RIM], "grid", rotation(grid, -1))
     return before, after, jnp.zeros((1,), jnp.int32)
 
 
-def grid_sum(part, grid):
-    if grid > 4:
+def grid_sum(part, orb, grid):
+    if grid != 4:
         return [lax.psum(part, "grid")]
-    masks = (1, 3, 2) if grid == 4 else range(1, grid)
-    paired = grid & (grid - 1) == 0
-    pairs = [exchange(grid, k) if paired else rotation(grid, k) for k in masks]
-    return [part] + [lax.ppermute(part, "grid", pair) for pair in pairs]
-
-
-def gather_all(work, orb):
-    blocks = []
-    for chip in range(0, orb, 2):
-        block = work if chip == 0 else lax.ppermute(work, "orb", exchange(orb, chip))
-        blocks += [block, lax.ppermute(block, "orb", exchange(orb, 1))]
-    return blocks
+    sets = [partners(orb, grid, (k, k), 1) for k in (2, 1, 3)]
+    return [part] + [lax.ppermute(part, BOTH, pairs) for pairs in sets]
+
+
+def gather_all(work, orb, scale, rank):
+    count, cells = work.shape
+    total = orb * count
+    pairs = []
+    masks = (0, 2, 4, LAST)
+    for mask in masks:
+        block = work if mask == 0 else lax.ppermute(work, "orb", exchange(orb, mask))
+        pairs.append([block, lax.ppermute(block, "orb", exchange(orb, 1))])
+    outs = (shape(total, total), shape(2 * total, cells, dtype=jnp.bfloat16))
+    early, before = call(
+        functools.partial(gram_kernel, scale, masks[:-1]), outs, [rank, *sum(pairs[:-1], [])]
+    )
+    return call(
+        functools.partial(last_kernel, scale),
+        outs,
+        [rank, *pairs[-1], early, before],
+        aliases={4: 1},
+    )
 
 
 def gather_leading(work, rank, members):
@@ -245,18 +306,18 @@
     members = min(PANEL * NPANEL // count, orb)
     total = members * count
     scale = 1.0 / (cells * grid)
-    one, two, swap = halo(planes, grid)
+    one, two, swap = halo(planes, orb, grid)
     local = call(local_kernel, shape(count, cells), [planes, potential], flops=10**9)
     work = call(couple_kernel, shape(count, cells), [swap, local, one, two])
     rank = lax.axis_index("orb").astype(jnp.int32)
-    everyone = members == orb and orb & (orb - 1) == 0
-    blocks = gather_all(work, orb) if everyone else gather_leading(work, rank, members)
-    gram, stack = call(
-        functools.partial(gram_kernel, scale),
-        (shape(total, total), shape(2 * total, cells, dtype=jnp.bfloat16)),
-        [rank.reshape(1) if everyone else jnp.zeros((1,), jnp.int32), *blocks],
-    )
-    parts = grid_sum(gram, grid)
+    everyone = members == orb == 8
+    if everyone:
+        gram, stack = gather_all(work, orb, scale, rank.reshape(1))
+    else:
+        blocks = gather_leading(work, rank, members)
+        leading = jnp.concatenate(blocks, 0)
+        gram = jnp.einsum("ic,jc->ij", leading, leading, precision=HIGH) * scale
+    parts = grid_sum(gram, orb, grid)
     if not everyone:
         rest = finish_leading(work, blocks, sum(parts), rank, scale)
         return rest.reshape(count, depth, plane)

time: 38 us -> 36.7 us (0.966)
  waiting for transfers between devices: 17.5 us -> 16.1 us
    ppermute x12, waiting for transfers between devices: 17.5 us -> 16.1 us  [the longest x3 7.3 us: gather_all(): lax.ppermute(work, 'orb', exchange(orb, mask))]
    pallas_call x4 -> x5, Pallas kernels: 5.48 us -> 5.66 us  [call(): pl.pallas_call(kernel, out_shape=out_shape, in_specs=in_specs, out_specs=...]
  transfers between devices with their start and end apart: 12 -> 12, of which waited for: 9 -> 8; matrix products, arithmetic and copies ran while one was open for 0% -> 0% of each run, Pallas kernels for 2% -> 5%
where the time goes in v4:
time: 36.7 us; the launch traced here: 36.5 us
  waiting for transfers between devices  16.1 us (44%)
  starting transfers between devices  13 us (35%)
  Pallas kernels  5.66 us (15%)
  local copies, waits for them, and re-layouts  1.72 us (5%)
    ppermute x3, waiting for transfers between devices, gather_all(): lax.ppermute(work, 'orb', exchange(orb, mask))  7.3 us
    pallas_call x5, Pallas kernels, call(): pl.pallas_call(kernel, out_shape=out_shape, in_specs=in_specs, out_specs=...  5.66 us
    ppermute x1, waiting for transfers between devices, halo(): one = lax.ppermute(planes, BOTH, partners(orb, grid, (3, 1)))  4.72 us
    ppermute x3, starting transfers between devices, grid_sum(): return [part] + [lax.ppermute(part, BOTH, pairs) for pairs in sets]  3.93 us
    ppermute x3, starting transfers between devices, gather_all(): lax.ppermute(work, 'orb', exchange(orb, mask))  3.55 us
    ppermute x1, starting transfers between devices, halo(): two = lax.ppermute(planes, BOTH, partners(orb, grid, (1, 3)))  3.02 us
    ppermute x1, starting transfers between devices, halo(): one = lax.ppermute(planes, BOTH, partners(orb, grid, (3, 1)))  2.47 us
    ppermute x3, waiting for transfers between devices, grid_sum(): return [part] + [lax.ppermute(part, BOTH, pairs) for pairs in sets]  2.08 us
  transfers between devices with their start and end apart: 12, of which 8 were waited for; matrix products, arithmetic and copies ran while one was open for 0% of the time, Pallas kernels for 5%

profile of v4, /device:TPU:0, one launch (start us, length us, event | category | flops | bytes accessed | tf_op | source)
XLA Modules:
  0.0 36.5 jit_solution(2430838839545774263)
XLA Ops:
  0.0 3.0 %collective-permute-start.1 = (f32[6,8,1024]{2,1,0:T(8,128)}, f32[6,8,1024]{2,1,0:T(8,128)S(1)}, u32[]{:S(2)}, u32[]{:S(2)}) collective-permute-start(f32[6,8,1024]{2,1,0:T(8,128)} %bitcast.4), channel_id=1, source_target_pairs={{0,1},{1,0},{2,3},{3,2},{4,7},{5,6},{6,5},{7,4},{8,9},{9,8},{10,11... | collective-permute-start | bytes 589832 | tf_op jit(solution)/shard_map/ppermute | solution.py:244
  3.0 2.5 %collective-permute-start = (f32[6,8,1024]{2,1,0:T(8,128)}, f32[6,8,1024]{2,1,0:T(8,128)S(1)}, u32[]{:S(2)}, u32[]{:S(2)}) collective-permute-start(f32[6,8,1024]{2,1,0:T(8,128)} %bitcast.5), channel_id=1, source_target_pairs={{0,3},{1,2},{2,1},{3,0},{4,5},{5,4},{6,7},{7,6},{8,11},{9,10},{10,... | collective-permute-start | bytes 589832 | tf_op jit(solution)/shard_map/ppermute | solution.py:243
  5.5 0.0 copy-start
  5.5 1.0 %copy-done = f32[8,6,1024]{2,0,1:T(8,128)S(1)} copy-done((f32[8,6,1024]{2,0,1:T(8,128)S(1)}, f32[8,6,1024]{2,0,1:T(8,128)}, u32[]{:S(2)}) %copy-start) | copy-done | bytes 196632
  6.5 0.8 %copy-done.1 = f32[6,1024]{1,0:T(8,128)S(1)} copy-done((f32[6,1024]{1,0:T(8,128)S(1)}, f32[6,1024]{1,0:T(8,128)}, u32[]{:S(2)}) %copy-start.1) | copy-done | bytes 24600
  7.2 0.9 %shard_map.28.local_ref = f32[8,6144]{1,0:T(8,128)S(1)} custom-call(f32[6,8,1024]{2,1,0:T(8,128)S(1)} %bitcast.6, f32[6,1024]{1,0:T(8,128)S(1)} %copy-done.1), custom_call_target="tpu_custom_call" | custom-call | flops 1000000000 | bytes 1000000 | tf_op jit(solution)/shard_map/pallas_call | solution.py:208
  8.2 1.5 %collective-permute-done.1.two_ref = f32[6,8,1024]{2,1,0:T(8,128)S(1)} collective-permute-done((f32[6,8,1024]{2,1,0:T(8,128)}, f32[6,8,1024]{2,1,0:T(8,128)S(1)}, u32[]{:S(2)}, u32[]{:S(2)}) %collective-permute-start.1) | collective-permute-done | bytes 196640 | tf_op jit(solution)/shard_map/ppermute | solution.py:244
  9.7 4.7 %collective-permute-done.one_ref = f32[6,8,1024]{2,1,0:T(8,128)S(1)} collective-permute-done((f32[6,8,1024]{2,1,0:T(8,128)}, f32[6,8,1024]{2,1,0:T(8,128)S(1)}, u32[]{:S(2)}, u32[]{:S(2)}) %collective-permute-start) | collective-permute-done | bytes 196640 | tf_op jit(solution)/shard_map/ppermute | solution.py:243
  14.4 0.1 shard_map.29.refs_0_
  14.5 1.6 %collective-permute-start.7 = (f32[8,6144]{1,0:T(8,128)S(1)}, f32[8,6144]{1,0:T(8,128)S(1)}, u32[]{:S(2)}, u32[]{:S(2)}) collective-permute-start(f32[8,6144]{1,0:T(8,128)S(1)} %shard_map.29.refs_0_), channel_id=1, source_target_pairs={{0,16},{4,20},{8,24},{12,28},{16,0},{20,4},{24,8},{28,12},{1,17},{... | collective-permute-start | bytes 589832 | tf_op jit(solution)/shard_map/ppermute | solution.py:265
  16.1 1.5 %collective-permute-start.5 = (f32[8,6144]{1,0:T(8,128)S(1)}, f32[8,6144]{1,0:T(8,128)S(1)}, u32[]{:S(2)}, u32[]{:S(2)}) collective-permute-start(f32[8,6144]{1,0:T(8,128)S(1)} %shard_map.29.refs_0_), channel_id=1, source_target_pairs={{0,8},{4,12},{8,0},{12,4},{16,24},{20,28},{24,16},{28,20},{1,9},{5... | collective-permute-start | bytes 589832 | tf_op jit(solution)/shard_map/ppermute | solution.py:265
  17.6 0.5 %collective-permute-start.2 = (f32[8,6144]{1,0:T(8,128)S(1)}, f32[8,6144]{1,0:T(8,128)S(1)}, u32[]{:S(2)}, u32[]{:S(2)}) collective-permute-start(f32[8,6144]{1,0:T(8,128)S(1)} %shard_map.29.refs_0_), channel_id=1, source_target_pairs={{0,24},{4,28},{8,16},{12,20},{16,8},{20,12},{24,0},{28,4},{1,25},{... | collective-permute-start | bytes 589832 | tf_op jit(solution)/shard_map/ppermute | solution.py:265
  18.1 0.0 collective-permute-start.4
  18.1 3.8 %collective-permute-done.7.refs_4_ = f32[8,6144]{1,0:T(8,128)S(1)} collective-permute-done((f32[8,6144]{1,0:T(8,128)S(1)}, f32[8,6144]{1,0:T(8,128)S(1)}, u32[]{:S(2)}, u32[]{:S(2)}) %collective-permute-start.7) | collective-permute-done | bytes 196640 | tf_op jit(solution)/shard_map/ppermute | solution.py:265
  21.9 0.0 collective-permute-start.8
  21.9 1.4 %collective-permute-done.5.refs_2_ = f32[8,6144]{1,0:T(8,128)S(1)} collective-permute-done((f32[8,6144]{1,0:T(8,128)S(1)}, f32[8,6144]{1,0:T(8,128)S(1)}, u32[]{:S(2)}, u32[]{:S(2)}) %collective-permute-start.5) | collective-permute-done | bytes 196640 | tf_op jit(solution)/shard_map/ppermute | solution.py:265
  23.3 0.0 collective-permute-start.6
  23.3 2.1 %collective-permute-done.2.one_ref = f32[8,6144]{1,0:T(8,128)S(1)} collective-permute-done((f32[8,6144]{1,0:T(8,128)S(1)}, f32[8,6144]{1,0:T(8,128)S(1)}, u32[]{:S(2)}, u32[]{:S(2)}) %collective-permute-start.2) | collective-permute-done | bytes 196640 | tf_op jit(solution)/shard_map/ppermute | solution.py:265
  25.4 0.0 collective-permute-start.3
  25.4 0.0 collective-permute-done.4.refs_1_
  25.4 0.0 collective-permute-done.8.refs_5_
  25.4 0.0 collective-permute-done.6.refs_3_
  25.4 1.0 %shard_map.30 = (f32[64,64]{1,0:T(8,128)S(1)}, bf16[128,6144]{1,0:T(8,128)(2,1)S(1)}) custom-call(s32[1]{0:T(128)} %bitcast.rank_ref, f32[8,6144]{1,0:T(8,128)S(1)} %shard_map.29.refs_0_, f32[8,6144]{1,0:T(8,128)S(1)} %collective-permute-done.4.refs_1_, f32[8,6144]{1,0:T(8,128)S(1)} %collective-permute-done.5.refs_2_, ...), custom_call_target="tpu_custom_call" | custom-call | bytes 1000000 | tf_op jit(solution)/shard_map/pallas_call | solution.py:208
  26.4 0.4 %collective-permute-done.3.two_ref = f32[8,6144]{1,0:T(8,128)S(1)} collective-permute-done((f32[8,6144]{1,0:T(8,128)S(1)}, f32[8,6144]{1,0:T(8,128)S(1)}, u32[]{:S(2)}, u32[]{:S(2)}) %collective-permute-start.3) | collective-permute-done | bytes 196640 | tf_op jit(solution)/shard_map/ppermute | solution.py:266
  26.8 0.9 %shard_map.31 = (f32[64,64]{1,0:T(8,128)S(1)}, bf16[128,6144]{1,0:T(8,128)(2,1)S(1)}) custom-call(s32[1]{0:T(128)} %bitcast.rank_ref, f32[8,6144]{1,0:T(8,128)S(1)} %collective-permute-done.2.one_ref, f32[8,6144]{1,0:T(8,128)S(1)} %collective-permute-done.3.two_ref, f32[64,64]{1,0:T(8,128)S(1)} %get-tuple-element.9.early_ref, ...), custom_call_target="tpu_custom_call", output_to_operand_aliasing={{1}: (4, {})} | custom-call | bytes 1000000 | tf_op jit(solution)/shard_map/pallas_call | solution.py:208
  27.7 0.7 %collective-permute-start.11 = (f32[64,64]{1,0:T(8,128)S(1)}, f32[64,64]{1,0:T(8,128)S(1)}, u32[]{:S(2)}, u32[]{:S(2)}) collective-permute-start(f32[64,64]{1,0:T(8,128)S(1)} %get-tuple-element.11.refs_0_), channel_id=1, source_target_pairs={{0,7},{1,6},{2,5},{3,4},{4,3},{5,2},{6,1},{7,0},{8,15},{9,14},{10,... | collective-permute-start | bytes 49160 | tf_op jit(solution)/shard_map/ppermute | solution.py:256
  28.4 0.5 %collective-permute-start.10 = (f32[64,64]{1,0:T(8,128)S(1)}, f32[64,64]{1,0:T(8,128)S(1)}, u32[]{:S(2)}, u32[]{:S(2)}) collective-permute-start(f32[64,64]{1,0:T(8,128)S(1)} %get-tuple-element.11.refs_0_), channel_id=1, source_target_pairs={{0,5},{1,4},{2,7},{3,6},{4,1},{5,0},{6,3},{7,2},{8,13},{9,12},{10,... | collective-permute-start | bytes 49160 | tf_op jit(solution)/shard_map/ppermute | solution.py:256
  28.9 2.7 %collective-permute-start.9 = (f32[64,64]{1,0:T(8,128)S(1)}, f32[64,64]{1,0:T(8,128)S(1)}, u32[]{:S(2)}, u32[]{:S(2)}) collective-permute-start(f32[64,64]{1,0:T(8,128)S(1)} %get-tuple-element.11.refs_0_), channel_id=1, source_target_pairs={{0,6},{1,7},{2,4},{3,5},{4,2},{5,3},{6,0},{7,1},{8,14},{9,15},{10,... | collective-permute-start | bytes 49160 | tf_op jit(solution)/shard_map/ppermute | solution.py:256
  31.7 1.3 %collective-permute-done.11.refs_3_ = f32[64,64]{1,0:T(8,128)S(1)} collective-permute-done((f32[64,64]{1,0:T(8,128)S(1)}, f32[64,64]{1,0:T(8,128)S(1)}, u32[]{:S(2)}, u32[]{:S(2)}) %collective-permute-start.11) | collective-permute-done | bytes 16416 | tf_op jit(solution)/shard_map/ppermute | solution.py:256
  33.0 0.0 collective-permute-done.10.refs_2_
  33.0 0.8 %collective-permute-done.9.refs_1_ = f32[64,64]{1,0:T(8,128)S(1)} collective-permute-done((f32[64,64]{1,0:T(8,128)S(1)}, f32[64,64]{1,0:T(8,128)S(1)}, u32[]{:S(2)}, u32[]{:S(2)}) %collective-permute-start.9) | collective-permute-done | bytes 16416 | tf_op jit(solution)/shard_map/ppermute | solution.py:256
  33.7 2.7 %shard_map.32 = f32[6,8,1024]{2,1,0:T(8,128)} custom-call(s32[1]{0:T(128)} %bitcast.rank_ref, f32[64,64]{1,0:T(8,128)S(1)} %get-tuple-element.11.refs_0_, f32[64,64]{1,0:T(8,128)S(1)} %collective-permute-done.9.refs_1_, f32[64,64]{1,0:T(8,128)S(1)} %collective-permute-done.10.refs_2_, f32[64,64]{1,0:T(8,128)S(1)} %collective-permute-done.11.refs_3_, ...), custom_call_target="tpu_custom_call" | custom-call | bytes 1000000 | tf_op jit(solution)/shard_map/pallas_call | solution.py:208
  (1 shorter events, 0.0 us)
Async XLA Ops:
  0.0 9.7 %collective-permute-start.1 = (f32[6,8,1024]{2,1,0:T(8,128)}, f32[6,8,1024]{2,1,0:T(8,128)S(1)}, u32[]{:S(2)}, u32[]{:S(2)}) collective-permute-start(f32[6,8,1024]{2,1,0:T(8,128)} %bitcast.4), channel_id=1, source_target_pairs={{0,1},{1,0},{2,3},{3,2},{4,7},{5,6},{6,5},{7,4},{8,9},{9,8},{10,11... | collective-permute-start | bytes 589832 | tf_op jit(solution)/shard_map/ppermute | solution.py:244
  3.0 11.4 %collective-permute-start = (f32[6,8,1024]{2,1,0:T(8,128)}, f32[6,8,1024]{2,1,0:T(8,128)S(1)}, u32[]{:S(2)}, u32[]{:S(2)}) collective-permute-start(f32[6,8,1024]{2,1,0:T(8,128)} %bitcast.5), channel_id=1, source_target_pairs={{0,3},{1,2},{2,1},{3,0},{4,5},{5,4},{6,7},{7,6},{8,11},{9,10},{10,... | collective-permute-start | bytes 589832 | tf_op jit(solution)/shard_map/ppermute | solution.py:243
  5.5 1.0 %copy-start = (f32[8,6,1024]{2,0,1:T(8,128)S(1)}, f32[8,6,1024]{2,0,1:T(8,128)}, u32[]{:S(2)}) copy-start(f32[8,6,1024]{2,0,1:T(8,128)} %param.2) | copy-start | bytes 589828
  6.5 0.8 %copy-start.1 = (f32[6,1024]{1,0:T(8,128)S(1)}, f32[6,1024]{1,0:T(8,128)}, u32[]{:S(2)}) copy-start(f32[6,1024]{1,0:T(8,128)} %pot_ref.1) | copy-start | bytes 73732
  14.5 7.4 %collective-permute-start.7 = (f32[8,6144]{1,0:T(8,128)S(1)}, f32[8,6144]{1,0:T(8,128)S(1)}, u32[]{:S(2)}, u32[]{:S(2)}) collective-permute-start(f32[8,6144]{1,0:T(8,128)S(1)} %shard_map.29.refs_0_), channel_id=1, source_target_pairs={{0,16},{4,20},{8,24},{12,28},{16,0},{20,4},{24,8},{28,12},{1,17},{... | collective-permute-start | bytes 589832 | tf_op jit(solution)/shard_map/ppermute | solution.py:265
  16.1 7.2 %collective-permute-start.5 = (f32[8,6144]{1,0:T(8,128)S(1)}, f32[8,6144]{1,0:T(8,128)S(1)}, u32[]{:S(2)}, u32[]{:S(2)}) collective-permute-start(f32[8,6144]{1,0:T(8,128)S(1)} %shard_map.29.refs_0_), channel_id=1, source_target_pairs={{0,8},{4,12},{8,0},{12,4},{16,24},{20,28},{24,16},{28,20},{1,9},{5... | collective-permute-start | bytes 589832 | tf_op jit(solution)/shard_map/ppermute | solution.py:265
  17.6 7.8 %collective-permute-start.2 = (f32[8,6144]{1,0:T(8,128)S(1)}, f32[8,6144]{1,0:T(8,128)S(1)}, u32[]{:S(2)}, u32[]{:S(2)}) collective-permute-start(f32[8,6144]{1,0:T(8,128)S(1)} %shard_map.29.refs_0_), channel_id=1, source_target_pairs={{0,24},{4,28},{8,16},{12,20},{16,8},{20,12},{24,0},{28,4},{1,25},{... | collective-permute-start | bytes 589832 | tf_op jit(solution)/shard_map/ppermute | solution.py:265
  18.1 7.3 %collective-permute-start.4 = (f32[8,6144]{1,0:T(8,128)S(1)}, f32[8,6144]{1,0:T(8,128)S(1)}, u32[]{:S(2)}, u32[]{:S(2)}) collective-permute-start(f32[8,6144]{1,0:T(8,128)S(1)} %shard_map.29.refs_0_), channel_id=1, source_target_pairs={{0,4},{4,0},{8,12},{12,8},{16,20},{20,16},{24,28},{28,24},{1,5},{5... | collective-permute-start | bytes 589832 | tf_op jit(solution)/shard_map/ppermute | solution.py:266
  21.9 3.5 %collective-permute-start.8 = (f32[8,6144]{1,0:T(8,128)S(1)}, f32[8,6144]{1,0:T(8,128)S(1)}, u32[]{:S(2)}, u32[]{:S(2)}) collective-permute-start(f32[8,6144]{1,0:T(8,128)S(1)} %collective-permute-done.7.refs_4_), channel_id=1, source_target_pairs={{0,4},{4,0},{8,12},{12,8},{16,20},{20,16},{24,28},{28,24},{1,5},{5... | collective-permute-start | bytes 589832 | tf_op jit(solution)/shard_map/ppermute | solution.py:266
  23.3 2.1 %collective-permute-start.6 = (f32[8,6144]{1,0:T(8,128)S(1)}, f32[8,6144]{1,0:T(8,128)S(1)}, u32[]{:S(2)}, u32[]{:S(2)}) collective-permute-start(f32[8,6144]{1,0:T(8,128)S(1)} %collective-permute-done.5.refs_2_), channel_id=1, source_target_pairs={{0,4},{4,0},{8,12},{12,8},{16,20},{20,16},{24,28},{28,24},{1,5},{5... | collective-permute-start | bytes 589832 | tf_op jit(solution)/shard_map/ppermute | solution.py:266
  25.4 1.4 %collective-permute-start.3 = (f32[8,6144]{1,0:T(8,128)S(1)}, f32[8,6144]{1,0:T(8,128)S(1)}, u32[]{:S(2)}, u32[]{:S(2)}) collective-permute-start(f32[8,6144]{1,0:T(8,128)S(1)} %collective-permute-done.2.one_ref), channel_id=1, source_target_pairs={{0,4},{4,0},{8,12},{12,8},{16,20},{20,16},{24,28},{28,24},{1,5},{5... | collective-permute-start | bytes 589832 | tf_op jit(solution)/shard_map/ppermute | solution.py:266
  27.7 5.2 %collective-permute-start.11 = (f32[64,64]{1,0:T(8,128)S(1)}, f32[64,64]{1,0:T(8,128)S(1)}, u32[]{:S(2)}, u32[]{:S(2)}) collective-permute-start(f32[64,64]{1,0:T(8,128)S(1)} %get-tuple-element.11.refs_0_), channel_id=1, source_target_pairs={{0,7},{1,6},{2,5},{3,4},{4,3},{5,2},{6,1},{7,0},{8,15},{9,14},{10,... | collective-permute-start | bytes 49160 | tf_op jit(solution)/shard_map/ppermute | solution.py:256
  28.4 4.5 %collective-permute-start.10 = (f32[64,64]{1,0:T(8,128)S(1)}, f32[64,64]{1,0:T(8,128)S(1)}, u32[]{:S(2)}, u32[]{:S(2)}) collective-permute-start(f32[64,64]{1,0:T(8,128)S(1)} %get-tuple-element.11.refs_0_), channel_id=1, source_target_pairs={{0,5},{1,4},{2,7},{3,6},{4,1},{5,0},{6,3},{7,2},{8,13},{9,12},{10,... | collective-permute-start | bytes 49160 | tf_op jit(solution)/shard_map/ppermute | solution.py:256
  28.9 4.8 %collective-permute-start.9 = (f32[64,64]{1,0:T(8,128)S(1)}, f32[64,64]{1,0:T(8,128)S(1)}, u32[]{:S(2)}, u32[]{:S(2)}) collective-permute-start(f32[64,64]{1,0:T(8,128)S(1)} %get-tuple-element.11.refs_0_), channel_id=1, source_target_pairs={{0,6},{1,7},{2,4},{3,5},{4,2},{5,3},{6,0},{7,1},{8,14},{9,15},{10,... | collective-permute-start | bytes 49160 | tf_op jit(solution)/shard_map/ppermute | solution.py:256

commit v5 on v4

--- a/solution.py
+++ b/solution.py
@@ -138,44 +138,50 @@
     zero = lax.broadcasted_iota(jnp.int32, full, 1).astype(jnp.float32) * 0.0
     whole = jnp.concatenate([gram, ident], 1)
     tiles = [whole[i : i + rows] for i in range(0, size, rows)]
+
+    def columns(i, first):
+        return [jnp.broadcast_to(tiles[i][:, k : k + 1], full) for k in range(first, first + rows)]
+
+    def spread(value, a):
+        return jnp.broadcast_to(value[a : a + 1], full)
+
+    own = [column + zero for column in columns(0, 0)]
     done = []
     for t in range(len(tiles)):
-
-        def columns(i):
-            first = t * rows
-            return [
-                jnp.broadcast_to(tiles[i][:, first + a : first + a + 1], full) for a in range(rows)
-            ]
-
-        own = [column + zero for column in columns(t)]
-        after = columns(t + 1) if t + 1 < len(tiles) else None
-        line = [jnp.broadcast_to(tiles[t][a : a + 1], full) for a in range(rows)]
-        pivot = [
-            [jnp.broadcast_to(own[b][a : a + 1], full) for b in range(a + 1)] for a in range(rows)
-        ]
+        last = t + 1 == len(tiles)
+        if not last:
+            after = [column + zero for column in columns(t + 1, t * rows)]
+            following = [column + zero for column in columns(t + 1, (t + 1) * rows)]
+        line = [spread(tiles[t], a) for a in range(rows)]
+        pivot = [[spread(own[b], a) for b in range(a + 1)] for a in range(rows)]
         factor = [[None] * rows for _ in range(rows)]
-        scaled = []
+        inverse = []
         for a in range(rows):
-            inverse = 1.0 / pivot[a][a]
-            scaled.append(line[a] * inverse)
+            inverse.append(1.0 / pivot[a][a])
             for b in range(a + 1, rows):
-                factor[b][a] = pivot[b][a] * inverse
+                factor[b][a] = pivot[b][a] * inverse[a]
                 line[b] = line[b] - factor[b][a] * line[a]
                 for c in range(a + 1, b + 1):
                     pivot[b][c] = pivot[b][c] - factor[b][a] * pivot[c][a]
-            if after is not None:
-                tiles[t + 1] = tiles[t + 1] - after[a] * scaled[a]
-                for b in range(a + 1, rows):
-                    after[b] = after[b] - factor[b][a] * after[a]
         done += [(line[a] * lax.rsqrt(pivot[a][a]))[:1] for a in range(rows)]
+        if last:
+            break
+        scaled = [line[a] * inverse[a] for a in range(rows)]
+        for a in range(rows):
+            tiles[t + 1] = tiles[t + 1] - after[a] * scaled[a]
+            weight = after[a] * inverse[a]
+            following = [f - weight * spread(after[a], c) for c, f in enumerate(following)]
+            for b in range(a + 1, rows):
+                after[b] = after[b] - factor[b][a] * after[a]
         for a in range(rows - 1, -1, -1):
             for b in range(a):
                 scaled[b] = scaled[b] - factor[a][b] * scaled[a]
         for i in range(t + 2, len(tiles)):
-            terms = [column * scaled[a] for a, column in enumerate(columns(i))]
+            terms = [column * scaled[a] for a, column in enumerate(columns(i, t * rows))]
             while len(terms) > 1:
                 terms = [terms[k] + terms[k + 1] for k in range(0, len(terms), 2)]
             tiles[i] = tiles[i] - terms[0]
+        own = following
     return jnp.concatenate(done, 0)[:, size:]
 
 

time: 36.7 us -> 36.2 us (0.986)
  Pallas kernels: 5.66 us -> 5.18 us
    pallas_call x5, Pallas kernels: 5.66 us -> 5.18 us  [call(): pl.pallas_call(kernel, out_shape=out_shape, in_specs=in_specs, out_specs=...]
where the time goes in v5:
time: 36.2 us; the launch traced here: 36 us
  waiting for transfers between devices  16.1 us (44%)
  starting transfers between devices  13 us (36%)
  Pallas kernels  5.18 us (14%)
  local copies, waits for them, and re-layouts  1.72 us (5%)
    ppermute x3, waiting for transfers between devices, gather_all(): lax.ppermute(work, 'orb', exchange(orb, mask))  7.3 us
    pallas_call x5, Pallas kernels, call(): pl.pallas_call(kernel, out_shape=out_shape, in_specs=in_specs, out_specs=...  5.18 us
    ppermute x1, waiting for transfers between devices, halo(): one = lax.ppermute(planes, BOTH, partners(orb, grid, (3, 1)))  4.72 us
    ppermute x3, starting transfers between devices, grid_sum(): return [part] + [lax.ppermute(part, BOTH, pairs) for pairs in sets]  3.93 us
    ppermute x3, starting transfers between devices, gather_all(): lax.ppermute(work, 'orb', exchange(orb, mask))  3.55 us
    ppermute x1, starting transfers between devices, halo(): two = lax.ppermute(planes, BOTH, partners(orb, grid, (1, 3)))  3.02 us
    ppermute x1, starting transfers between devices, halo(): one = lax.ppermute(planes, BOTH, partners(orb, grid, (3, 1)))  2.47 us
    ppermute x3, waiting for transfers between devices, grid_sum(): return [part] + [lax.ppermute(part, BOTH, pairs) for pairs in sets]  2.08 us
  transfers between devices with their start and end apart: 12, of which 8 were waited for; matrix products, arithmetic and copies ran while one was open for 0% of the time, Pallas kernels for 5%

profile of v5, /device:TPU:0, one launch (start us, length us, event | category | flops | bytes accessed | tf_op | source)
XLA Modules:
  0.0 36.0 jit_solution(2071393105872002303)
XLA Ops:
  0.0 3.0 %collective-permute-start.1 = (f32[6,8,1024]{2,1,0:T(8,128)}, f32[6,8,1024]{2,1,0:T(8,128)S(1)}, u32[]{:S(2)}, u32[]{:S(2)}) collective-permute-start(f32[6,8,1024]{2,1,0:T(8,128)} %bitcast.4), channel_id=1, source_target_pairs={{0,1},{1,0},{2,3},{3,2},{4,7},{5,6},{6,5},{7,4},{8,9},{9,8},{10,11... | collective-permute-start | bytes 589832 | tf_op jit(solution)/shard_map/ppermute | solution.py:250
  3.0 2.5 %collective-permute-start = (f32[6,8,1024]{2,1,0:T(8,128)}, f32[6,8,1024]{2,1,0:T(8,128)S(1)}, u32[]{:S(2)}, u32[]{:S(2)}) collective-permute-start(f32[6,8,1024]{2,1,0:T(8,128)} %bitcast.5), channel_id=1, source_target_pairs={{0,3},{1,2},{2,1},{3,0},{4,5},{5,4},{6,7},{7,6},{8,11},{9,10},{10,... | collective-permute-start | bytes 589832 | tf_op jit(solution)/shard_map/ppermute | solution.py:249
  5.5 0.0 copy-start
  5.5 1.0 %copy-done = f32[8,6,1024]{2,0,1:T(8,128)S(1)} copy-done((f32[8,6,1024]{2,0,1:T(8,128)S(1)}, f32[8,6,1024]{2,0,1:T(8,128)}, u32[]{:S(2)}) %copy-start) | copy-done | bytes 196632
  6.5 0.8 %copy-done.1 = f32[6,1024]{1,0:T(8,128)S(1)} copy-done((f32[6,1024]{1,0:T(8,128)S(1)}, f32[6,1024]{1,0:T(8,128)}, u32[]{:S(2)}) %copy-start.1) | copy-done | bytes 24600
  7.2 0.9 %shard_map.28.local_ref = f32[8,6144]{1,0:T(8,128)S(1)} custom-call(f32[6,8,1024]{2,1,0:T(8,128)S(1)} %bitcast.6, f32[6,1024]{1,0:T(8,128)S(1)} %copy-done.1), custom_call_target="tpu_custom_call" | custom-call | flops 1000000000 | bytes 1000000 | tf_op jit(solution)/shard_map/pallas_call | solution.py:214
  8.2 1.5 %collective-permute-done.1.two_ref = f32[6,8,1024]{2,1,0:T(8,128)S(1)} collective-permute-done((f32[6,8,1024]{2,1,0:T(8,128)}, f32[6,8,1024]{2,1,0:T(8,128)S(1)}, u32[]{:S(2)}, u32[]{:S(2)}) %collective-permute-start.1) | collective-permute-done | bytes 196640 | tf_op jit(solution)/shard_map/ppermute | solution.py:250
  9.7 4.7 %collective-permute-done.one_ref = f32[6,8,1024]{2,1,0:T(8,128)S(1)} collective-permute-done((f32[6,8,1024]{2,1,0:T(8,128)}, f32[6,8,1024]{2,1,0:T(8,128)S(1)}, u32[]{:S(2)}, u32[]{:S(2)}) %collective-permute-start) | collective-permute-done | bytes 196640 | tf_op jit(solution)/shard_map/ppermute | solution.py:249
  14.4 0.1 shard_map.29.refs_0_
  14.5 1.6 %collective-permute-start.7 = (f32[8,6144]{1,0:T(8,128)S(1)}, f32[8,6144]{1,0:T(8,128)S(1)}, u32[]{:S(2)}, u32[]{:S(2)}) collective-permute-start(f32[8,6144]{1,0:T(8,128)S(1)} %shard_map.29.refs_0_), channel_id=1, source_target_pairs={{0,16},{4,20},{8,24},{12,28},{16,0},{20,4},{24,8},{28,12},{1,17},{... | collective-permute-start | bytes 589832 | tf_op jit(solution)/shard_map/ppermute | solution.py:271
  16.1 1.5 %collective-permute-start.5 = (f32[8,6144]{1,0:T(8,128)S(1)}, f32[8,6144]{1,0:T(8,128)S(1)}, u32[]{:S(2)}, u32[]{:S(2)}) collective-permute-start(f32[8,6144]{1,0:T(8,128)S(1)} %shard_map.29.refs_0_), channel_id=1, source_target_pairs={{0,8},{4,12},{8,0},{12,4},{16,24},{20,28},{24,16},{28,20},{1,9},{5... | collective-permute-start | bytes 589832 | tf_op jit(solution)/shard_map/ppermute | solution.py:271
  17.6 0.5 %collective-permute-start.2 = (f32[8,6144]{1,0:T(8,128)S(1)}, f32[8,6144]{1,0:T(8,128)S(1)}, u32[]{:S(2)}, u32[]{:S(2)}) collective-permute-start(f32[8,6144]{1,0:T(8,128)S(1)} %shard_map.29.refs_0_), channel_id=1, source_target_pairs={{0,24},{4,28},{8,16},{12,20},{16,8},{20,12},{24,0},{28,4},{1,25},{... | collective-permute-start | bytes 589832 | tf_op jit(solution)/shard_map/ppermute | solution.py:271
  18.1 0.0 collective-permute-start.4
  18.1 3.8 %collective-permute-done.7.refs_4_ = f32[8,6144]{1,0:T(8,128)S(1)} collective-permute-done((f32[8,6144]{1,0:T(8,128)S(1)}, f32[8,6144]{1,0:T(8,128)S(1)}, u32[]{:S(2)}, u32[]{:S(2)}) %collective-permute-start.7) | collective-permute-done | bytes 196640 | tf_op jit(solution)/shard_map/ppermute | solution.py:271
  21.9 0.0 collective-permute-start.8
  21.9 1.4 %collective-permute-done.5.refs_2_ = f32[8,6144]{1,0:T(8,128)S(1)} collective-permute-done((f32[8,6144]{1,0:T(8,128)S(1)}, f32[8,6144]{1,0:T(8,128)S(1)}, u32[]{:S(2)}, u32[]{:S(2)}) %collective-permute-start.5) | collective-permute-done | bytes 196640 | tf_op jit(solution)/shard_map/ppermute | solution.py:271
  23.3 0.0 collective-permute-start.6
  23.3 2.1 %collective-permute-done.2.one_ref = f32[8,6144]{1,0:T(8,128)S(1)} collective-permute-done((f32[8,6144]{1,0:T(8,128)S(1)}, f32[8,6144]{1,0:T(8,128)S(1)}, u32[]{:S(2)}, u32[]{:S(2)}) %collective-permute-start.2) | collective-permute-done | bytes 196640 | tf_op jit(solution)/shard_map/ppermute | solution.py:271
  25.4 0.0 collective-permute-start.3
  25.4 0.0 collective-permute-done.4.refs_1_
  25.4 0.0 collective-permute-done.8.refs_5_
  25.4 0.0 collective-permute-done.6.refs_3_
  25.4 1.0 %shard_map.30 = (f32[64,64]{1,0:T(8,128)S(1)}, bf16[128,6144]{1,0:T(8,128)(2,1)S(1)}) custom-call(s32[1]{0:T(128)} %bitcast.rank_ref, f32[8,6144]{1,0:T(8,128)S(1)} %shard_map.29.refs_0_, f32[8,6144]{1,0:T(8,128)S(1)} %collective-permute-done.4.refs_1_, f32[8,6144]{1,0:T(8,128)S(1)} %collective-permute-done.5.refs_2_, ...), custom_call_target="tpu_custom_call" | custom-call | bytes 1000000 | tf_op jit(solution)/shard_map/pallas_call | solution.py:214
  26.4 0.4 %collective-permute-done.3.two_ref = f32[8,6144]{1,0:T(8,128)S(1)} collective-permute-done((f32[8,6144]{1,0:T(8,128)S(1)}, f32[8,6144]{1,0:T(8,128)S(1)}, u32[]{:S(2)}, u32[]{:S(2)}) %collective-permute-start.3) | collective-permute-done | bytes 196640 | tf_op jit(solution)/shard_map/ppermute | solution.py:272
  26.8 0.9 %shard_map.31 = (f32[64,64]{1,0:T(8,128)S(1)}, bf16[128,6144]{1,0:T(8,128)(2,1)S(1)}) custom-call(s32[1]{0:T(128)} %bitcast.rank_ref, f32[8,6144]{1,0:T(8,128)S(1)} %collective-permute-done.2.one_ref, f32[8,6144]{1,0:T(8,128)S(1)} %collective-permute-done.3.two_ref, f32[64,64]{1,0:T(8,128)S(1)} %get-tuple-element.9.early_ref, ...), custom_call_target="tpu_custom_call", output_to_operand_aliasing={{1}: (4, {})} | custom-call | bytes 1000000 | tf_op jit(solution)/shard_map/pallas_call | solution.py:214
  27.7 0.7 %collective-permute-start.11 = (f32[64,64]{1,0:T(8,128)S(1)}, f32[64,64]{1,0:T(8,128)S(1)}, u32[]{:S(2)}, u32[]{:S(2)}) collective-permute-start(f32[64,64]{1,0:T(8,128)S(1)} %get-tuple-element.11.refs_0_), channel_id=1, source_target_pairs={{0,7},{1,6},{2,5},{3,4},{4,3},{5,2},{6,1},{7,0},{8,15},{9,14},{10,... | collective-permute-start | bytes 49160 | tf_op jit(solution)/shard_map/ppermute | solution.py:262
  28.4 0.5 %collective-permute-start.10 = (f32[64,64]{1,0:T(8,128)S(1)}, f32[64,64]{1,0:T(8,128)S(1)}, u32[]{:S(2)}, u32[]{:S(2)}) collective-permute-start(f32[64,64]{1,0:T(8,128)S(1)} %get-tuple-element.11.refs_0_), channel_id=1, source_target_pairs={{0,5},{1,4},{2,7},{3,6},{4,1},{5,0},{6,3},{7,2},{8,13},{9,12},{10,... | collective-permute-start | bytes 49160 | tf_op jit(solution)/shard_map/ppermute | solution.py:262
  28.9 2.7 %collective-permute-start.9 = (f32[64,64]{1,0:T(8,128)S(1)}, f32[64,64]{1,0:T(8,128)S(1)}, u32[]{:S(2)}, u32[]{:S(2)}) collective-permute-start(f32[64,64]{1,0:T(8,128)S(1)} %get-tuple-element.11.refs_0_), channel_id=1, source_target_pairs={{0,6},{1,7},{2,4},{3,5},{4,2},{5,3},{6,0},{7,1},{8,14},{9,15},{10,... | collective-permute-start | bytes 49160 | tf_op jit(solution)/shard_map/ppermute | solution.py:262
  31.7 1.3 %collective-permute-done.11.refs_3_ = f32[64,64]{1,0:T(8,128)S(1)} collective-permute-done((f32[64,64]{1,0:T(8,128)S(1)}, f32[64,64]{1,0:T(8,128)S(1)}, u32[]{:S(2)}, u32[]{:S(2)}) %collective-permute-start.11) | collective-permute-done | bytes 16416 | tf_op jit(solution)/shard_map/ppermute | solution.py:262
  33.0 0.0 collective-permute-done.10.refs_2_
  33.0 0.8 %collective-permute-done.9.refs_1_ = f32[64,64]{1,0:T(8,128)S(1)} collective-permute-done((f32[64,64]{1,0:T(8,128)S(1)}, f32[64,64]{1,0:T(8,128)S(1)}, u32[]{:S(2)}, u32[]{:S(2)}) %collective-permute-start.9) | collective-permute-done | bytes 16416 | tf_op jit(solution)/shard_map/ppermute | solution.py:262
  33.7 2.3 %shard_map.32 = f32[6,8,1024]{2,1,0:T(8,128)} custom-call(s32[1]{0:T(128)} %bitcast.rank_ref, f32[64,64]{1,0:T(8,128)S(1)} %get-tuple-element.11.refs_0_, f32[64,64]{1,0:T(8,128)S(1)} %collective-permute-done.9.refs_1_, f32[64,64]{1,0:T(8,128)S(1)} %collective-permute-done.10.refs_2_, f32[64,64]{1,0:T(8,128)S(1)} %collective-permute-done.11.refs_3_, ...), custom_call_target="tpu_custom_call" | custom-call | bytes 1000000 | tf_op jit(solution)/shard_map/pallas_call | solution.py:214
  (1 shorter events, 0.0 us)
Async XLA Ops:
  0.0 9.7 %collective-permute-start.1 = (f32[6,8,1024]{2,1,0:T(8,128)}, f32[6,8,1024]{2,1,0:T(8,128)S(1)}, u32[]{:S(2)}, u32[]{:S(2)}) collective-permute-start(f32[6,8,1024]{2,1,0:T(8,128)} %bitcast.4), channel_id=1, source_target_pairs={{0,1},{1,0},{2,3},{3,2},{4,7},{5,6},{6,5},{7,4},{8,9},{9,8},{10,11... | collective-permute-start | bytes 589832 | tf_op jit(solution)/shard_map/ppermute | solution.py:250
  3.0 11.4 %collective-permute-start = (f32[6,8,1024]{2,1,0:T(8,128)}, f32[6,8,1024]{2,1,0:T(8,128)S(1)}, u32[]{:S(2)}, u32[]{:S(2)}) collective-permute-start(f32[6,8,1024]{2,1,0:T(8,128)} %bitcast.5), channel_id=1, source_target_pairs={{0,3},{1,2},{2,1},{3,0},{4,5},{5,4},{6,7},{7,6},{8,11},{9,10},{10,... | collective-permute-start | bytes 589832 | tf_op jit(solution)/shard_map/ppermute | solution.py:249
  5.5 1.0 %copy-start = (f32[8,6,1024]{2,0,1:T(8,128)S(1)}, f32[8,6,1024]{2,0,1:T(8,128)}, u32[]{:S(2)}) copy-start(f32[8,6,1024]{2,0,1:T(8,128)} %param.2) | copy-start | bytes 589828
  6.5 0.8 %copy-start.1 = (f32[6,1024]{1,0:T(8,128)S(1)}, f32[6,1024]{1,0:T(8,128)}, u32[]{:S(2)}) copy-start(f32[6,1024]{1,0:T(8,128)} %pot_ref.1) | copy-start | bytes 73732
  14.5 7.4 %collective-permute-start.7 = (f32[8,6144]{1,0:T(8,128)S(1)}, f32[8,6144]{1,0:T(8,128)S(1)}, u32[]{:S(2)}, u32[]{:S(2)}) collective-permute-start(f32[8,6144]{1,0:T(8,128)S(1)} %shard_map.29.refs_0_), channel_id=1, source_target_pairs={{0,16},{4,20},{8,24},{12,28},{16,0},{20,4},{24,8},{28,12},{1,17},{... | collective-permute-start | bytes 589832 | tf_op jit(solution)/shard_map/ppermute | solution.py:271
  16.1 7.2 %collective-permute-start.5 = (f32[8,6144]{1,0:T(8,128)S(1)}, f32[8,6144]{1,0:T(8,128)S(1)}, u32[]{:S(2)}, u32[]{:S(2)}) collective-permute-start(f32[8,6144]{1,0:T(8,128)S(1)} %shard_map.29.refs_0_), channel_id=1, source_target_pairs={{0,8},{4,12},{8,0},{12,4},{16,24},{20,28},{24,16},{28,20},{1,9},{5... | collective-permute-start | bytes 589832 | tf_op jit(solution)/shard_map/ppermute | solution.py:271
  17.6 7.8 %collective-permute-start.2 = (f32[8,6144]{1,0:T(8,128)S(1)}, f32[8,6144]{1,0:T(8,128)S(1)}, u32[]{:S(2)}, u32[]{:S(2)}) collective-permute-start(f32[8,6144]{1,0:T(8,128)S(1)} %shard_map.29.refs_0_), channel_id=1, source_target_pairs={{0,24},{4,28},{8,16},{12,20},{16,8},{20,12},{24,0},{28,4},{1,25},{... | collective-permute-start | bytes 589832 | tf_op jit(solution)/shard_map/ppermute | solution.py:271
  18.1 7.3 %collective-permute-start.4 = (f32[8,6144]{1,0:T(8,128)S(1)}, f32[8,6144]{1,0:T(8,128)S(1)}, u32[]{:S(2)}, u32[]{:S(2)}) collective-permute-start(f32[8,6144]{1,0:T(8,128)S(1)} %shard_map.29.refs_0_), channel_id=1, source_target_pairs={{0,4},{4,0},{8,12},{12,8},{16,20},{20,16},{24,28},{28,24},{1,5},{5... | collective-permute-start | bytes 589832 | tf_op jit(solution)/shard_map/ppermute | solution.py:272
  21.9 3.5 %collective-permute-start.8 = (f32[8,6144]{1,0:T(8,128)S(1)}, f32[8,6144]{1,0:T(8,128)S(1)}, u32[]{:S(2)}, u32[]{:S(2)}) collective-permute-start(f32[8,6144]{1,0:T(8,128)S(1)} %collective-permute-done.7.refs_4_), channel_id=1, source_target_pairs={{0,4},{4,0},{8,12},{12,8},{16,20},{20,16},{24,28},{28,24},{1,5},{5... | collective-permute-start | bytes 589832 | tf_op jit(solution)/shard_map/ppermute | solution.py:272
  23.3 2.1 %collective-permute-start.6 = (f32[8,6144]{1,0:T(8,128)S(1)}, f32[8,6144]{1,0:T(8,128)S(1)}, u32[]{:S(2)}, u32[]{:S(2)}) collective-permute-start(f32[8,6144]{1,0:T(8,128)S(1)} %collective-permute-done.5.refs_2_), channel_id=1, source_target_pairs={{0,4},{4,0},{8,12},{12,8},{16,20},{20,16},{24,28},{28,24},{1,5},{5... | collective-permute-start | bytes 589832 | tf_op jit(solution)/shard_map/ppermute | solution.py:272
  25.4 1.4 %collective-permute-start.3 = (f32[8,6144]{1,0:T(8,128)S(1)}, f32[8,6144]{1,0:T(8,128)S(1)}, u32[]{:S(2)}, u32[]{:S(2)}) collective-permute-start(f32[8,6144]{1,0:T(8,128)S(1)} %collective-permute-done.2.one_ref), channel_id=1, source_target_pairs={{0,4},{4,0},{8,12},{12,8},{16,20},{20,16},{24,28},{28,24},{1,5},{5... | collective-permute-start | bytes 589832 | tf_op jit(solution)/shard_map/ppermute | solution.py:272
  27.7 5.2 %collective-permute-start.11 = (f32[64,64]{1,0:T(8,128)S(1)}, f32[64,64]{1,0:T(8,128)S(1)}, u32[]{:S(2)}, u32[]{:S(2)}) collective-permute-start(f32[64,64]{1,0:T(8,128)S(1)} %get-tuple-element.11.refs_0_), channel_id=1, source_target_pairs={{0,7},{1,6},{2,5},{3,4},{4,3},{5,2},{6,1},{7,0},{8,15},{9,14},{10,... | collective-permute-start | bytes 49160 | tf_op jit(solution)/shard_map/ppermute | solution.py:262
  28.4 4.5 %collective-permute-start.10 = (f32[64,64]{1,0:T(8,128)S(1)}, f32[64,64]{1,0:T(8,128)S(1)}, u32[]{:S(2)}, u32[]{:S(2)}) collective-permute-start(f32[64,64]{1,0:T(8,128)S(1)} %get-tuple-element.11.refs_0_), channel_id=1, source_target_pairs={{0,5},{1,4},{2,7},{3,6},{4,1},{5,0},{6,3},{7,2},{8,13},{9,12},{10,... | collective-permute-start | bytes 49160 | tf_op jit(solution)/shard_map/ppermute | solution.py:262
  28.9 4.8 %collective-permute-start.9 = (f32[64,64]{1,0:T(8,128)S(1)}, f32[64,64]{1,0:T(8,128)S(1)}, u32[]{:S(2)}, u32[]{:S(2)}) collective-permute-start(f32[64,64]{1,0:T(8,128)S(1)} %get-tuple-element.11.refs_0_), channel_id=1, source_target_pairs={{0,6},{1,7},{2,4},{3,5},{4,2},{5,3},{6,0},{7,1},{8,14},{9,15},{10,... | collective-permute-start | bytes 49160 | tf_op jit(solution)/shard_map/ppermute | solution.py:262

commit v6 on v5

--- a/solution.py
+++ b/solution.py
@@ -115,19 +115,25 @@
     rank = rank_ref[0]
     rows = 2 * one_ref.shape[0]
     total = gram_ref.shape[0]
-    pair = store_pair(rank, LAST, one_ref, two_ref, stack_ref)
-    lines = products(pair, stack_ref[...], scale)
-    repeated = jnp.concatenate([lines] * (total // rows), 0)
-    first = place(rank, LAST, rows)
-    row = lax.broadcasted_iota(jnp.int32, (total, total), 0)
-    column = lax.broadcasted_iota(jnp.int32, (total, total), 1)
-    gram = jnp.where(
-        (column >= first) & (column < first + rows), repeated.T, early_ref[...]
-    )
-    gram_ref[...] = jnp.where((row >= first) & (row < first + rows), repeated, gram)
-
-
-def invert_factor(gram):
+    needed = (rank // 2 ^ LAST // 2) < rank // 2
+
+    @pl.when(needed)
+    def _():
+        pair = store_pair(rank, LAST, one_ref, two_ref, stack_ref)
+        lines = products(pair, stack_ref[...], scale)
+        repeated = jnp.concatenate([lines] * (total // rows), 0)
+        first = place(rank, LAST, rows)
+        row = lax.broadcasted_iota(jnp.int32, (total, total), 0)
+        column = lax.broadcasted_iota(jnp.int32, (total, total), 1)
+        gram = jnp.where((column >= first) & (column < first + rows), repeated.T, early_ref[...])
+        gram_ref[...] = jnp.where((row >= first) & (row < first + rows), repeated, gram)
+
+    @pl.when(jnp.logical_not(needed))
+    def _():
+        gram_ref[...] = early_ref[...]
+
+
+def invert_factor(gram, leading):
     size = gram.shape[0]
     rows = 8
     full = (rows, 2 * size)
@@ -137,7 +143,7 @@
     ).astype(jnp.float32)
     zero = lax.broadcasted_iota(jnp.int32, full, 1).astype(jnp.float32) * 0.0
     whole = jnp.concatenate([gram, ident], 1)
-    tiles = [whole[i : i + rows] for i in range(0, size, rows)]
+    tiles = [whole[i : i + rows] for i in range(0, leading, rows)]
 
     def columns(i, first):
         return [jnp.broadcast_to(tiles[i][:, k : k + 1], full) for k in range(first, first + rows)]
@@ -191,7 +197,16 @@
     gram = parts[0][...]
     for part in parts[1:]:
         gram = gram + part[...]
-    factor_ref[...] = invert_factor(gram)
+    held = 2 * count
+    chip = rank_ref[0] // 2
+    low_chip = 0
+    for top in (2, 4):
+
+        @pl.when((chip >= low_chip) & (chip < top))
+        def _(top=top):
+            factor_ref[: top * held, :] = invert_factor(gram, top * held)
+
+        low_chip = top
     rows = factor_ref[pl.ds(pl.multiple_of(rank_ref[0] * count, count), count), :]
     high = rows.astype(jnp.bfloat16).astype(jnp.float32)
     low = rows - high

time: 36.2 us -> 35.3 us (0.975); the launches traced: 36 us -> 34.6 us
  Pallas kernels: 5.18 us -> 3.77 us
    pallas_call x5, Pallas kernels: 5.18 us -> 3.77 us  [call(): pl.pallas_call(kernel, out_shape=out_shape, in_specs=in_specs, out_specs=...]
  transfers between devices with their start and end apart: 12 -> 12, of which waited for: 8 -> 8; matrix products, arithmetic and copies ran while one was open for 0% -> 0% of each run, Pallas kernels for 5% -> 6%
where the time goes in v6:
time: 35.3 us; the launch traced here: 34.6 us
  waiting for transfers between devices  16.1 us (46%)
  starting transfers between devices  13 us (37%)
  Pallas kernels  3.77 us (11%)
  local copies, waits for them, and re-layouts  1.72 us (5%)
    ppermute x3, waiting for transfers between devices, gather_all(): lax.ppermute(work, 'orb', exchange(orb, mask))  7.3 us
    ppermute x1, waiting for transfers between devices, halo(): one = lax.ppermute(planes, BOTH, partners(orb, grid, (3, 1)))  4.72 us
    ppermute x3, starting transfers between devices, grid_sum(): return [part] + [lax.ppermute(part, BOTH, pairs) for pairs in sets]  3.91 us
    pallas_call x5, Pallas kernels, call(): pl.pallas_call(kernel, out_shape=out_shape, in_specs=in_specs, out_specs=...  3.77 us
    ppermute x3, starting transfers between devices, gather_all(): lax.ppermute(work, 'orb', exchange(orb, mask))  3.55 us
    ppermute x1, starting transfers between devices, halo(): two = lax.ppermute(planes, BOTH, partners(orb, grid, (1, 3)))  3.02 us
    ppermute x1, starting transfers between devices, halo(): one = lax.ppermute(planes, BOTH, partners(orb, grid, (3, 1)))  2.47 us
    ppermute x3, waiting for transfers between devices, grid_sum(): return [part] + [lax.ppermute(part, BOTH, pairs) for pairs in sets]  2.15 us
  transfers between devices with their start and end apart: 12, of which 8 were waited for; matrix products, arithmetic and copies ran while one was open for 0% of the time, Pallas kernels for 6%

profile of v6, /device:TPU:0, one launch (start us, length us, event | category | flops | bytes accessed | tf_op | source)
XLA Modules:
  0.0 34.6 jit_solution(13475543561529916072)
XLA Ops:
  0.0 3.0 %collective-permute-start.1 = (f32[6,8,1024]{2,1,0:T(8,128)}, f32[6,8,1024]{2,1,0:T(8,128)S(1)}, u32[]{:S(2)}, u32[]{:S(2)}) collective-permute-start(f32[6,8,1024]{2,1,0:T(8,128)} %bitcast.4), channel_id=1, source_target_pairs={{0,1},{1,0},{2,3},{3,2},{4,7},{5,6},{6,5},{7,4},{8,9},{9,8},{10,11... | collective-permute-start | bytes 589832 | tf_op jit(solution)/shard_map/ppermute | solution.py:265
  3.0 2.5 %collective-permute-start = (f32[6,8,1024]{2,1,0:T(8,128)}, f32[6,8,1024]{2,1,0:T(8,128)S(1)}, u32[]{:S(2)}, u32[]{:S(2)}) collective-permute-start(f32[6,8,1024]{2,1,0:T(8,128)} %bitcast.5), channel_id=1, source_target_pairs={{0,3},{1,2},{2,1},{3,0},{4,5},{5,4},{6,7},{7,6},{8,11},{9,10},{10,... | collective-permute-start | bytes 589832 | tf_op jit(solution)/shard_map/ppermute | solution.py:264
  5.5 0.0 copy-start
  5.5 1.0 %copy-done = f32[8,6,1024]{2,0,1:T(8,128)S(1)} copy-done((f32[8,6,1024]{2,0,1:T(8,128)S(1)}, f32[8,6,1024]{2,0,1:T(8,128)}, u32[]{:S(2)}) %copy-start) | copy-done | bytes 196632
  6.5 0.0 copy-start.1
  6.5 0.8 %copy-done.1 = f32[6,1024]{1,0:T(8,128)S(1)} copy-done((f32[6,1024]{1,0:T(8,128)S(1)}, f32[6,1024]{1,0:T(8,128)}, u32[]{:S(2)}) %copy-start.1) | copy-done | bytes 24600
  7.2 0.9 %shard_map.28.local_ref = f32[8,6144]{1,0:T(8,128)S(1)} custom-call(f32[6,8,1024]{2,1,0:T(8,128)S(1)} %bitcast.6, f32[6,1024]{1,0:T(8,128)S(1)} %copy-done.1), custom_call_target="tpu_custom_call" | custom-call | flops 1000000000 | bytes 1000000 | tf_op jit(solution)/shard_map/pallas_call | solution.py:229
  8.2 1.5 %collective-permute-done.1.two_ref = f32[6,8,1024]{2,1,0:T(8,128)S(1)} collective-permute-done((f32[6,8,1024]{2,1,0:T(8,128)}, f32[6,8,1024]{2,1,0:T(8,128)S(1)}, u32[]{:S(2)}, u32[]{:S(2)}) %collective-permute-start.1) | collective-permute-done | bytes 196640 | tf_op jit(solution)/shard_map/ppermute | solution.py:265
  9.7 4.7 %collective-permute-done.one_ref = f32[6,8,1024]{2,1,0:T(8,128)S(1)} collective-permute-done((f32[6,8,1024]{2,1,0:T(8,128)}, f32[6,8,1024]{2,1,0:T(8,128)S(1)}, u32[]{:S(2)}, u32[]{:S(2)}) %collective-permute-start) | collective-permute-done | bytes 196640 | tf_op jit(solution)/shard_map/ppermute | solution.py:264
  14.4 0.1 shard_map.29.refs_0_
  14.5 1.6 %collective-permute-start.7 = (f32[8,6144]{1,0:T(8,128)S(1)}, f32[8,6144]{1,0:T(8,128)S(1)}, u32[]{:S(2)}, u32[]{:S(2)}) collective-permute-start(f32[8,6144]{1,0:T(8,128)S(1)} %shard_map.29.refs_0_), channel_id=1, source_target_pairs={{0,16},{4,20},{8,24},{12,28},{16,0},{20,4},{24,8},{28,12},{1,17},{... | collective-permute-start | bytes 589832 | tf_op jit(solution)/shard_map/ppermute | solution.py:286
  16.1 1.5 %collective-permute-start.5 = (f32[8,6144]{1,0:T(8,128)S(1)}, f32[8,6144]{1,0:T(8,128)S(1)}, u32[]{:S(2)}, u32[]{:S(2)}) collective-permute-start(f32[8,6144]{1,0:T(8,128)S(1)} %shard_map.29.refs_0_), channel_id=1, source_target_pairs={{0,8},{4,12},{8,0},{12,4},{16,24},{20,28},{24,16},{28,20},{1,9},{5... | collective-permute-start | bytes 589832 | tf_op jit(solution)/shard_map/ppermute | solution.py:286
  17.6 0.5 %collective-permute-start.2 = (f32[8,6144]{1,0:T(8,128)S(1)}, f32[8,6144]{1,0:T(8,128)S(1)}, u32[]{:S(2)}, u32[]{:S(2)}) collective-permute-start(f32[8,6144]{1,0:T(8,128)S(1)} %shard_map.29.refs_0_), channel_id=1, source_target_pairs={{0,24},{4,28},{8,16},{12,20},{16,8},{20,12},{24,0},{28,4},{1,25},{... | collective-permute-start | bytes 589832 | tf_op jit(solution)/shard_map/ppermute | solution.py:286
  18.1 0.0 collective-permute-start.4
  18.1 3.8 %collective-permute-done.7.refs_4_ = f32[8,6144]{1,0:T(8,128)S(1)} collective-permute-done((f32[8,6144]{1,0:T(8,128)S(1)}, f32[8,6144]{1,0:T(8,128)S(1)}, u32[]{:S(2)}, u32[]{:S(2)}) %collective-permute-start.7) | collective-permute-done | bytes 196640 | tf_op jit(solution)/shard_map/ppermute | solution.py:286
  21.9 0.0 collective-permute-start.8
  21.9 1.4 %collective-permute-done.5.refs_2_ = f32[8,6144]{1,0:T(8,128)S(1)} collective-permute-done((f32[8,6144]{1,0:T(8,128)S(1)}, f32[8,6144]{1,0:T(8,128)S(1)}, u32[]{:S(2)}, u32[]{:S(2)}) %collective-permute-start.5) | collective-permute-done | bytes 196640 | tf_op jit(solution)/shard_map/ppermute | solution.py:286
  23.3 0.0 collective-permute-start.6
  23.3 2.1 %collective-permute-done.2.one_ref = f32[8,6144]{1,0:T(8,128)S(1)} collective-permute-done((f32[8,6144]{1,0:T(8,128)S(1)}, f32[8,6144]{1,0:T(8,128)S(1)}, u32[]{:S(2)}, u32[]{:S(2)}) %collective-permute-start.2) | collective-permute-done | bytes 196640 | tf_op jit(solution)/shard_map/ppermute | solution.py:286
  25.4 0.0 collective-permute-start.3
  25.4 0.0 collective-permute-done.4.refs_1_
  25.4 0.0 collective-permute-done.8.refs_5_
  25.4 0.0 collective-permute-done.6.refs_3_
  25.4 1.0 %shard_map.30 = (f32[64,64]{1,0:T(8,128)S(1)}, bf16[128,6144]{1,0:T(8,128)(2,1)S(1)}) custom-call(s32[1]{0:T(128)} %bitcast.rank_ref, f32[8,6144]{1,0:T(8,128)S(1)} %shard_map.29.refs_0_, f32[8,6144]{1,0:T(8,128)S(1)} %collective-permute-done.4.refs_1_, f32[8,6144]{1,0:T(8,128)S(1)} %collective-permute-done.5.refs_2_, ...), custom_call_target="tpu_custom_call" | custom-call | bytes 1000000 | tf_op jit(solution)/shard_map/pallas_call | solution.py:229
  26.4 0.4 %collective-permute-done.3.two_ref = f32[8,6144]{1,0:T(8,128)S(1)} collective-permute-done((f32[8,6144]{1,0:T(8,128)S(1)}, f32[8,6144]{1,0:T(8,128)S(1)}, u32[]{:S(2)}, u32[]{:S(2)}) %collective-permute-start.3) | collective-permute-done | bytes 196640 | tf_op jit(solution)/shard_map/ppermute | solution.py:287
  26.8 0.7 %collective-permute-start.11 = (f32[64,64]{1,0:T(8,128)S(1)}, f32[64,64]{1,0:T(8,128)S(1)}, u32[]{:S(2)}, u32[]{:S(2)}) collective-permute-start(f32[64,64]{1,0:T(8,128)S(1)} %get-tuple-element.11.refs_0_), channel_id=1, source_target_pairs={{0,7},{1,6},{2,5},{3,4},{4,3},{5,2},{6,1},{7,0},{8,15},{9,14},{10,... | collective-permute-start | bytes 49160 | tf_op jit(solution)/shard_map/ppermute | solution.py:277
  27.5 0.5 %collective-permute-start.10 = (f32[64,64]{1,0:T(8,128)S(1)}, f32[64,64]{1,0:T(8,128)S(1)}, u32[]{:S(2)}, u32[]{:S(2)}) collective-permute-start(f32[64,64]{1,0:T(8,128)S(1)} %get-tuple-element.11.refs_0_), channel_id=1, source_target_pairs={{0,5},{1,4},{2,7},{3,6},{4,1},{5,0},{6,3},{7,2},{8,13},{9,12},{10,... | collective-permute-start | bytes 49160 | tf_op jit(solution)/shard_map/ppermute | solution.py:277
  28.0 2.7 %collective-permute-start.9 = (f32[64,64]{1,0:T(8,128)S(1)}, f32[64,64]{1,0:T(8,128)S(1)}, u32[]{:S(2)}, u32[]{:S(2)}) collective-permute-start(f32[64,64]{1,0:T(8,128)S(1)} %get-tuple-element.11.refs_0_), channel_id=1, source_target_pairs={{0,6},{1,7},{2,4},{3,5},{4,2},{5,3},{6,0},{7,1},{8,14},{9,15},{10,... | collective-permute-start | bytes 49160 | tf_op jit(solution)/shard_map/ppermute | solution.py:277
  30.8 1.2 %collective-permute-done.11.refs_3_ = f32[64,64]{1,0:T(8,128)S(1)} collective-permute-done((f32[64,64]{1,0:T(8,128)S(1)}, f32[64,64]{1,0:T(8,128)S(1)}, u32[]{:S(2)}, u32[]{:S(2)}) %collective-permute-start.11) | collective-permute-done | bytes 16416 | tf_op jit(solution)/shard_map/ppermute | solution.py:277
  32.0 0.0 collective-permute-done.10.refs_2_
  32.0 0.9 %collective-permute-done.9.refs_1_ = f32[64,64]{1,0:T(8,128)S(1)} collective-permute-done((f32[64,64]{1,0:T(8,128)S(1)}, f32[64,64]{1,0:T(8,128)S(1)}, u32[]{:S(2)}, u32[]{:S(2)}) %collective-permute-start.9) | collective-permute-done | bytes 16416 | tf_op jit(solution)/shard_map/ppermute | solution.py:277
  32.9 1.7 %shard_map.32 = f32[6,8,1024]{2,1,0:T(8,128)} custom-call(s32[1]{0:T(128)} %bitcast.rank_ref, f32[64,64]{1,0:T(8,128)S(1)} %get-tuple-element.11.refs_0_, f32[64,64]{1,0:T(8,128)S(1)} %collective-permute-done.9.refs_1_, f32[64,64]{1,0:T(8,128)S(1)} %collective-permute-done.10.refs_2_, f32[64,64]{1,0:T(8,128)S(1)} %collective-permute-done.11.refs_3_, ...), custom_call_target="tpu_custom_call" | custom-call | bytes 1000000 | tf_op jit(solution)/shard_map/pallas_call | solution.py:229
  (1 shorter events, 0.0 us)
Async XLA Ops:
  0.0 9.7 %collective-permute-start.1 = (f32[6,8,1024]{2,1,0:T(8,128)}, f32[6,8,1024]{2,1,0:T(8,128)S(1)}, u32[]{:S(2)}, u32[]{:S(2)}) collective-permute-start(f32[6,8,1024]{2,1,0:T(8,128)} %bitcast.4), channel_id=1, source_target_pairs={{0,1},{1,0},{2,3},{3,2},{4,7},{5,6},{6,5},{7,4},{8,9},{9,8},{10,11... | collective-permute-start | bytes 589832 | tf_op jit(solution)/shard_map/ppermute | solution.py:265
  3.0 11.4 %collective-permute-start = (f32[6,8,1024]{2,1,0:T(8,128)}, f32[6,8,1024]{2,1,0:T(8,128)S(1)}, u32[]{:S(2)}, u32[]{:S(2)}) collective-permute-start(f32[6,8,1024]{2,1,0:T(8,128)} %bitcast.5), channel_id=1, source_target_pairs={{0,3},{1,2},{2,1},{3,0},{4,5},{5,4},{6,7},{7,6},{8,11},{9,10},{10,... | collective-permute-start | bytes 589832 | tf_op jit(solution)/shard_map/ppermute | solution.py:264
  5.5 1.0 %copy-start = (f32[8,6,1024]{2,0,1:T(8,128)S(1)}, f32[8,6,1024]{2,0,1:T(8,128)}, u32[]{:S(2)}) copy-start(f32[8,6,1024]{2,0,1:T(8,128)} %param.2) | copy-start | bytes 589828
  6.5 0.8 %copy-start.1 = (f32[6,1024]{1,0:T(8,128)S(1)}, f32[6,1024]{1,0:T(8,128)}, u32[]{:S(2)}) copy-start(f32[6,1024]{1,0:T(8,128)} %pot_ref.1) | copy-start | bytes 73732
  14.5 7.4 %collective-permute-start.7 = (f32[8,6144]{1,0:T(8,128)S(1)}, f32[8,6144]{1,0:T(8,128)S(1)}, u32[]{:S(2)}, u32[]{:S(2)}) collective-permute-start(f32[8,6144]{1,0:T(8,128)S(1)} %shard_map.29.refs_0_), channel_id=1, source_target_pairs={{0,16},{4,20},{8,24},{12,28},{16,0},{20,4},{24,8},{28,12},{1,17},{... | collective-permute-start | bytes 589832 | tf_op jit(solution)/shard_map/ppermute | solution.py:286
  16.1 7.2 %collective-permute-start.5 = (f32[8,6144]{1,0:T(8,128)S(1)}, f32[8,6144]{1,0:T(8,128)S(1)}, u32[]{:S(2)}, u32[]{:S(2)}) collective-permute-start(f32[8,6144]{1,0:T(8,128)S(1)} %shard_map.29.refs_0_), channel_id=1, source_target_pairs={{0,8},{4,12},{8,0},{12,4},{16,24},{20,28},{24,16},{28,20},{1,9},{5... | collective-permute-start | bytes 589832 | tf_op jit(solution)/shard_map/ppermute | solution.py:286
  17.6 7.8 %collective-permute-start.2 = (f32[8,6144]{1,0:T(8,128)S(1)}, f32[8,6144]{1,0:T(8,128)S(1)}, u32[]{:S(2)}, u32[]{:S(2)}) collective-permute-start(f32[8,6144]{1,0:T(8,128)S(1)} %shard_map.29.refs_0_), channel_id=1, source_target_pairs={{0,24},{4,28},{8,16},{12,20},{16,8},{20,12},{24,0},{28,4},{1,25},{... | collective-permute-start | bytes 589832 | tf_op jit(solution)/shard_map/ppermute | solution.py:286
  18.1 7.3 %collective-permute-start.4 = (f32[8,6144]{1,0:T(8,128)S(1)}, f32[8,6144]{1,0:T(8,128)S(1)}, u32[]{:S(2)}, u32[]{:S(2)}) collective-permute-start(f32[8,6144]{1,0:T(8,128)S(1)} %shard_map.29.refs_0_), channel_id=1, source_target_pairs={{0,4},{4,0},{8,12},{12,8},{16,20},{20,16},{24,28},{28,24},{1,5},{5... | collective-permute-start | bytes 589832 | tf_op jit(solution)/shard_map/ppermute | solution.py:287
  21.9 3.5 %collective-permute-start.8 = (f32[8,6144]{1,0:T(8,128)S(1)}, f32[8,6144]{1,0:T(8,128)S(1)}, u32[]{:S(2)}, u32[]{:S(2)}) collective-permute-start(f32[8,6144]{1,0:T(8,128)S(1)} %collective-permute-done.7.refs_4_), channel_id=1, source_target_pairs={{0,4},{4,0},{8,12},{12,8},{16,20},{20,16},{24,28},{28,24},{1,5},{5... | collective-permute-start | bytes 589832 | tf_op jit(solution)/shard_map/ppermute | solution.py:287
  23.3 2.1 %collective-permute-start.6 = (f32[8,6144]{1,0:T(8,128)S(1)}, f32[8,6144]{1,0:T(8,128)S(1)}, u32[]{:S(2)}, u32[]{:S(2)}) collective-permute-start(f32[8,6144]{1,0:T(8,128)S(1)} %collective-permute-done.5.refs_2_), channel_id=1, source_target_pairs={{0,4},{4,0},{8,12},{12,8},{16,20},{20,16},{24,28},{28,24},{1,5},{5... | collective-permute-start | bytes 589832 | tf_op jit(solution)/shard_map/ppermute | solution.py:287
  25.4 1.4 %collective-permute-start.3 = (f32[8,6144]{1,0:T(8,128)S(1)}, f32[8,6144]{1,0:T(8,128)S(1)}, u32[]{:S(2)}, u32[]{:S(2)}) collective-permute-start(f32[8,6144]{1,0:T(8,128)S(1)} %collective-permute-done.2.one_ref), channel_id=1, source_target_pairs={{0,4},{4,0},{8,12},{12,8},{16,20},{20,16},{24,28},{28,24},{1,5},{5... | collective-permute-start | bytes 589832 | tf_op jit(solution)/shard_map/ppermute | solution.py:287
  26.8 5.1 %collective-permute-start.11 = (f32[64,64]{1,0:T(8,128)S(1)}, f32[64,64]{1,0:T(8,128)S(1)}, u32[]{:S(2)}, u32[]{:S(2)}) collective-permute-start(f32[64,64]{1,0:T(8,128)S(1)} %get-tuple-element.11.refs_0_), channel_id=1, source_target_pairs={{0,7},{1,6},{2,5},{3,4},{4,3},{5,2},{6,1},{7,0},{8,15},{9,14},{10,... | collective-permute-start | bytes 49160 | tf_op jit(solution)/shard_map/ppermute | solution.py:277
  27.5 4.4 %collective-permute-start.10 = (f32[64,64]{1,0:T(8,128)S(1)}, f32[64,64]{1,0:T(8,128)S(1)}, u32[]{:S(2)}, u32[]{:S(2)}) collective-permute-start(f32[64,64]{1,0:T(8,128)S(1)} %get-tuple-element.11.refs_0_), channel_id=1, source_target_pairs={{0,5},{1,4},{2,7},{3,6},{4,1},{5,0},{6,3},{7,2},{8,13},{9,12},{10,... | collective-permute-start | bytes 49160 | tf_op jit(solution)/shard_map/ppermute | solution.py:277
  28.0 4.9 %collective-permute-start.9 = (f32[64,64]{1,0:T(8,128)S(1)}, f32[64,64]{1,0:T(8,128)S(1)}, u32[]{:S(2)}, u32[]{:S(2)}) collective-permute-start(f32[64,64]{1,0:T(8,128)S(1)} %get-tuple-element.11.refs_0_), channel_id=1, source_target_pairs={{0,6},{1,7},{2,4},{3,5},{4,2},{5,3},{6,0},{7,1},{8,14},{9,15},{10,... | collective-permute-start | bytes 49160 | tf_op jit(solution)/shard_map/ppermute | solution.py:277

commit v7 on v6

--- a/solution.py
+++ b/solution.py
@@ -192,7 +192,7 @@
 
 
 def finish_kernel(rank_ref, *refs):
-    parts, (stack_ref, out_ref, factor_ref) = refs[:-3], refs[-3:]
+    parts, (stack_ref, out_ref, factor_ref, held_ref, sems) = refs[:-5], refs[-5:]
     depth, count, plane = out_ref.shape
     gram = parts[0][...]
     for part in parts[1:]:
@@ -200,7 +200,7 @@
     held = 2 * count
     chip = rank_ref[0] // 2
     low_chip = 0
-    for top in (2, 4):
+    for top in (2, 3, 4):
 
         @pl.when((chip >= low_chip) & (chip < top))
         def _(top=top):
@@ -213,19 +213,24 @@
     left = jnp.concatenate(
         [jnp.concatenate([high, high], 1), jnp.concatenate([low, low], 1)], 0
     ).astype(jnp.bfloat16)
+    copies = []
     for p in range(depth):
         both = jnp.dot(
             left, stack_ref[:, p * plane : (p + 1) * plane], preferred_element_type=jnp.float32
         )
-        out_ref[p] = both[:count] + both[count:]
-
-
-def call(kernel, out_shape, inputs, scratch=(), flops=0, aliases=None):
+        held_ref[p] = both[:count] + both[count:]
+        copies.append(pltpu.make_async_copy(held_ref.at[p], out_ref.at[p], sems.at[p]))
+        copies[-1].start()
+    for copy in copies:
+        copy.wait()
+
+
+def call(kernel, out_shape, inputs, scratch=(), flops=0, aliases=None, space=pltpu.VMEM):
     in_specs = [
         pl.BlockSpec(memory_space=pltpu.SMEM if a.dtype == jnp.int32 else pltpu.VMEM)
         for a in inputs
     ]
-    out_specs = jax.tree.map(lambda s: pl.BlockSpec(memory_space=pltpu.VMEM), out_shape)
+    out_specs = jax.tree.map(lambda s: pl.BlockSpec(memory_space=space), out_shape)
     return pl.pallas_call(
         kernel,
         out_shape=out_shape,
@@ -346,7 +351,12 @@
         finish_kernel,
         shape(depth, count, plane),
         [rank.reshape(1), *parts, stack],
-        scratch=[pltpu.VMEM((total, total), jnp.float32)],
+        scratch=[
+            pltpu.VMEM((total, total), jnp.float32),
+            pltpu.VMEM((depth, count, plane), jnp.float32),
+            pltpu.SemaphoreType.DMA((depth,)),
+        ],
+        space=pl.ANY,
     )
     return jnp.transpose(done, (1, 0, 2))
 

time: 35.3 us -> 35.3 us (level)
  no operation moved by 1% of the time
where the time goes in v7:
time: 35.3 us; the launch traced here: 34.6 us
  waiting for transfers between devices  16.1 us (46%)
  starting transfers between devices  13 us (37%)
  Pallas kernels  3.76 us (11%)
  local copies, waits for them, and re-layouts  1.72 us (5%)
    ppermute x3, waiting for transfers between devices, gather_all(): lax.ppermute(work, 'orb', exchange(orb, mask))  7.3 us
    ppermute x1, waiting for transfers between devices, halo(): one = lax.ppermute(planes, BOTH, partners(orb, grid, (3, 1)))  4.72 us
    ppermute x3, starting transfers between devices, grid_sum(): return [part] + [lax.ppermute(part, BOTH, pairs) for pairs in sets]  3.91 us
    pallas_call x5, Pallas kernels, call(): pl.pallas_call(kernel, out_shape=out_shape, in_specs=in_specs, out_specs=...  3.76 us
    ppermute x3, starting transfers between devices, gather_all(): lax.ppermute(work, 'orb', exchange(orb, mask))  3.55 us
    ppermute x1, starting transfers between devices, halo(): two = lax.ppermute(planes, BOTH, partners(orb, grid, (1, 3)))  3.02 us
    ppermute x1, starting transfers between devices, halo(): one = lax.ppermute(planes, BOTH, partners(orb, grid, (3, 1)))  2.47 us
    ppermute x3, waiting for transfers between devices, grid_sum(): return [part] + [lax.ppermute(part, BOTH, pairs) for pairs in sets]  2.15 us
  transfers between devices with their start and end apart: 12, of which 8 were waited for; matrix products, arithmetic and copies ran while one was open for 0% of the time, Pallas kernels for 6%

profile of v7, /device:TPU:0, one launch (start us, length us, event | category | flops | bytes accessed | tf_op | source)
XLA Modules:
  0.0 34.6 jit_solution(18184230999420549314)
XLA Ops:
  0.0 3.0 %collective-permute-start.1 = (f32[6,8,1024]{2,1,0:T(8,128)}, f32[6,8,1024]{2,1,0:T(8,128)S(1)}, u32[]{:S(2)}, u32[]{:S(2)}) collective-permute-start(f32[6,8,1024]{2,1,0:T(8,128)} %bitcast.4), channel_id=1, source_target_pairs={{0,1},{1,0},{2,3},{3,2},{4,7},{5,6},{6,5},{7,4},{8,9},{9,8},{10,11... | collective-permute-start | bytes 589832 | tf_op jit(solution)/shard_map/ppermute | solution.py:270
  3.0 2.5 %collective-permute-start = (f32[6,8,1024]{2,1,0:T(8,128)}, f32[6,8,1024]{2,1,0:T(8,128)S(1)}, u32[]{:S(2)}, u32[]{:S(2)}) collective-permute-start(f32[6,8,1024]{2,1,0:T(8,128)} %bitcast.5), channel_id=1, source_target_pairs={{0,3},{1,2},{2,1},{3,0},{4,5},{5,4},{6,7},{7,6},{8,11},{9,10},{10,... | collective-permute-start | bytes 589832 | tf_op jit(solution)/shard_map/ppermute | solution.py:269
  5.5 0.0 copy-start
  5.5 1.0 %copy-done = f32[8,6,1024]{2,0,1:T(8,128)S(1)} copy-done((f32[8,6,1024]{2,0,1:T(8,128)S(1)}, f32[8,6,1024]{2,0,1:T(8,128)}, u32[]{:S(2)}) %copy-start) | copy-done | bytes 196632
  6.5 0.0 copy-start.1
  6.5 0.8 %copy-done.1 = f32[6,1024]{1,0:T(8,128)S(1)} copy-done((f32[6,1024]{1,0:T(8,128)S(1)}, f32[6,1024]{1,0:T(8,128)}, u32[]{:S(2)}) %copy-start.1) | copy-done | bytes 24600
  7.2 0.9 %shard_map.28.local_ref = f32[8,6144]{1,0:T(8,128)S(1)} custom-call(f32[6,8,1024]{2,1,0:T(8,128)S(1)} %bitcast.6, f32[6,1024]{1,0:T(8,128)S(1)} %copy-done.1), custom_call_target="tpu_custom_call" | custom-call | flops 1000000000 | bytes 1000000 | tf_op jit(solution)/shard_map/pallas_call | solution.py:234
  8.2 1.5 %collective-permute-done.1.two_ref = f32[6,8,1024]{2,1,0:T(8,128)S(1)} collective-permute-done((f32[6,8,1024]{2,1,0:T(8,128)}, f32[6,8,1024]{2,1,0:T(8,128)S(1)}, u32[]{:S(2)}, u32[]{:S(2)}) %collective-permute-start.1) | collective-permute-done | bytes 196640 | tf_op jit(solution)/shard_map/ppermute | solution.py:270
  9.7 4.7 %collective-permute-done.one_ref = f32[6,8,1024]{2,1,0:T(8,128)S(1)} collective-permute-done((f32[6,8,1024]{2,1,0:T(8,128)}, f32[6,8,1024]{2,1,0:T(8,128)S(1)}, u32[]{:S(2)}, u32[]{:S(2)}) %collective-permute-start) | collective-permute-done | bytes 196640 | tf_op jit(solution)/shard_map/ppermute | solution.py:269
  14.4 0.1 shard_map.29.refs_0_
  14.5 1.6 %collective-permute-start.7 = (f32[8,6144]{1,0:T(8,128)S(1)}, f32[8,6144]{1,0:T(8,128)S(1)}, u32[]{:S(2)}, u32[]{:S(2)}) collective-permute-start(f32[8,6144]{1,0:T(8,128)S(1)} %shard_map.29.refs_0_), channel_id=1, source_target_pairs={{0,16},{4,20},{8,24},{12,28},{16,0},{20,4},{24,8},{28,12},{1,17},{... | collective-permute-start | bytes 589832 | tf_op jit(solution)/shard_map/ppermute | solution.py:291
  16.1 1.5 %collective-permute-start.5 = (f32[8,6144]{1,0:T(8,128)S(1)}, f32[8,6144]{1,0:T(8,128)S(1)}, u32[]{:S(2)}, u32[]{:S(2)}) collective-permute-start(f32[8,6144]{1,0:T(8,128)S(1)} %shard_map.29.refs_0_), channel_id=1, source_target_pairs={{0,8},{4,12},{8,0},{12,4},{16,24},{20,28},{24,16},{28,20},{1,9},{5... | collective-permute-start | bytes 589832 | tf_op jit(solution)/shard_map/ppermute | solution.py:291
  17.6 0.5 %collective-permute-start.2 = (f32[8,6144]{1,0:T(8,128)S(1)}, f32[8,6144]{1,0:T(8,128)S(1)}, u32[]{:S(2)}, u32[]{:S(2)}) collective-permute-start(f32[8,6144]{1,0:T(8,128)S(1)} %shard_map.29.refs_0_), channel_id=1, source_target_pairs={{0,24},{4,28},{8,16},{12,20},{16,8},{20,12},{24,0},{28,4},{1,25},{... | collective-permute-start | bytes 589832 | tf_op jit(solution)/shard_map/ppermute | solution.py:291
  18.1 0.0 collective-permute-start.4
  18.1 3.8 %collective-permute-done.7.refs_4_ = f32[8,6144]{1,0:T(8,128)S(1)} collective-permute-done((f32[8,6144]{1,0:T(8,128)S(1)}, f32[8,6144]{1,0:T(8,128)S(1)}, u32[]{:S(2)}, u32[]{:S(2)}) %collective-permute-start.7) | collective-permute-done | bytes 196640 | tf_op jit(solution)/shard_map/ppermute | solution.py:291
  21.9 0.0 collective-permute-start.8
  21.9 1.4 %collective-permute-done.5.refs_2_ = f32[8,6144]{1,0:T(8,128)S(1)} collective-permute-done((f32[8,6144]{1,0:T(8,128)S(1)}, f32[8,6144]{1,0:T(8,128)S(1)}, u32[]{:S(2)}, u32[]{:S(2)}) %collective-permute-start.5) | collective-permute-done | bytes 196640 | tf_op jit(solution)/shard_map/ppermute | solution.py:291
  23.3 0.0 collective-permute-start.6
  23.3 2.1 %collective-permute-done.2.one_ref = f32[8,6144]{1,0:T(8,128)S(1)} collective-permute-done((f32[8,6144]{1,0:T(8,128)S(1)}, f32[8,6144]{1,0:T(8,128)S(1)}, u32[]{:S(2)}, u32[]{:S(2)}) %collective-permute-start.2) | collective-permute-done | bytes 196640 | tf_op jit(solution)/shard_map/ppermute | solution.py:291
  25.4 0.0 collective-permute-start.3
  25.4 0.0 collective-permute-done.4.refs_1_
  25.4 0.0 collective-permute-done.8.refs_5_
  25.4 0.0 collective-permute-done.6.refs_3_
  25.4 1.0 %shard_map.30 = (f32[64,64]{1,0:T(8,128)S(1)}, bf16[128,6144]{1,0:T(8,128)(2,1)S(1)}) custom-call(s32[1]{0:T(128)} %bitcast.rank_ref, f32[8,6144]{1,0:T(8,128)S(1)} %shard_map.29.refs_0_, f32[8,6144]{1,0:T(8,128)S(1)} %collective-permute-done.4.refs_1_, f32[8,6144]{1,0:T(8,128)S(1)} %collective-permute-done.5.refs_2_, ...), custom_call_target="tpu_custom_call" | custom-call | bytes 1000000 | tf_op jit(solution)/shard_map/pallas_call | solution.py:234
  26.4 0.4 %collective-permute-done.3.two_ref = f32[8,6144]{1,0:T(8,128)S(1)} collective-permute-done((f32[8,6144]{1,0:T(8,128)S(1)}, f32[8,6144]{1,0:T(8,128)S(1)}, u32[]{:S(2)}, u32[]{:S(2)}) %collective-permute-start.3) | collective-permute-done | bytes 196640 | tf_op jit(solution)/shard_map/ppermute | solution.py:292
  26.8 0.7 %collective-permute-start.11 = (f32[64,64]{1,0:T(8,128)S(1)}, f32[64,64]{1,0:T(8,128)S(1)}, u32[]{:S(2)}, u32[]{:S(2)}) collective-permute-start(f32[64,64]{1,0:T(8,128)S(1)} %get-tuple-element.11.refs_0_), channel_id=1, source_target_pairs={{0,7},{1,6},{2,5},{3,4},{4,3},{5,2},{6,1},{7,0},{8,15},{9,14},{10,... | collective-permute-start | bytes 49160 | tf_op jit(solution)/shard_map/ppermute | solution.py:282
  27.5 0.5 %collective-permute-start.10 = (f32[64,64]{1,0:T(8,128)S(1)}, f32[64,64]{1,0:T(8,128)S(1)}, u32[]{:S(2)}, u32[]{:S(2)}) collective-permute-start(f32[64,64]{1,0:T(8,128)S(1)} %get-tuple-element.11.refs_0_), channel_id=1, source_target_pairs={{0,5},{1,4},{2,7},{3,6},{4,1},{5,0},{6,3},{7,2},{8,13},{9,12},{10,... | collective-permute-start | bytes 49160 | tf_op jit(solution)/shard_map/ppermute | solution.py:282
  28.0 2.7 %collective-permute-start.9 = (f32[64,64]{1,0:T(8,128)S(1)}, f32[64,64]{1,0:T(8,128)S(1)}, u32[]{:S(2)}, u32[]{:S(2)}) collective-permute-start(f32[64,64]{1,0:T(8,128)S(1)} %get-tuple-element.11.refs_0_), channel_id=1, source_target_pairs={{0,6},{1,7},{2,4},{3,5},{4,2},{5,3},{6,0},{7,1},{8,14},{9,15},{10,... | collective-permute-start | bytes 49160 | tf_op jit(solution)/shard_map/ppermute | solution.py:282
  30.8 1.2 %collective-permute-done.11.refs_3_ = f32[64,64]{1,0:T(8,128)S(1)} collective-permute-done((f32[64,64]{1,0:T(8,128)S(1)}, f32[64,64]{1,0:T(8,128)S(1)}, u32[]{:S(2)}, u32[]{:S(2)}) %collective-permute-start.11) | collective-permute-done | bytes 16416 | tf_op jit(solution)/shard_map/ppermute | solution.py:282
  32.0 0.0 collective-permute-done.10.refs_2_
  32.0 0.9 %collective-permute-done.9.refs_1_ = f32[64,64]{1,0:T(8,128)S(1)} collective-permute-done((f32[64,64]{1,0:T(8,128)S(1)}, f32[64,64]{1,0:T(8,128)S(1)}, u32[]{:S(2)}, u32[]{:S(2)}) %collective-permute-start.9) | collective-permute-done | bytes 16416 | tf_op jit(solution)/shard_map/ppermute | solution.py:282
  32.9 1.7 %shard_map.32 = f32[6,8,1024]{2,1,0:T(8,128)} custom-call(s32[1]{0:T(128)} %bitcast.rank_ref, f32[64,64]{1,0:T(8,128)S(1)} %get-tuple-element.11.refs_0_, f32[64,64]{1,0:T(8,128)S(1)} %collective-permute-done.9.refs_1_, f32[64,64]{1,0:T(8,128)S(1)} %collective-permute-done.10.refs_2_, f32[64,64]{1,0:T(8,128)S(1)} %collective-permute-done.11.refs_3_, ...), custom_call_target="tpu_custom_call" | custom-call | bytes 1000000 | tf_op jit(solution)/shard_map/pallas_call | solution.py:234
  (1 shorter events, 0.0 us)
Async XLA Ops:
  0.0 9.7 %collective-permute-start.1 = (f32[6,8,1024]{2,1,0:T(8,128)}, f32[6,8,1024]{2,1,0:T(8,128)S(1)}, u32[]{:S(2)}, u32[]{:S(2)}) collective-permute-start(f32[6,8,1024]{2,1,0:T(8,128)} %bitcast.4), channel_id=1, source_target_pairs={{0,1},{1,0},{2,3},{3,2},{4,7},{5,6},{6,5},{7,4},{8,9},{9,8},{10,11... | collective-permute-start | bytes 589832 | tf_op jit(solution)/shard_map/ppermute | solution.py:270
  3.0 11.4 %collective-permute-start = (f32[6,8,1024]{2,1,0:T(8,128)}, f32[6,8,1024]{2,1,0:T(8,128)S(1)}, u32[]{:S(2)}, u32[]{:S(2)}) collective-permute-start(f32[6,8,1024]{2,1,0:T(8,128)} %bitcast.5), channel_id=1, source_target_pairs={{0,3},{1,2},{2,1},{3,0},{4,5},{5,4},{6,7},{7,6},{8,11},{9,10},{10,... | collective-permute-start | bytes 589832 | tf_op jit(solution)/shard_map/ppermute | solution.py:269
  5.5 1.0 %copy-start = (f32[8,6,1024]{2,0,1:T(8,128)S(1)}, f32[8,6,1024]{2,0,1:T(8,128)}, u32[]{:S(2)}) copy-start(f32[8,6,1024]{2,0,1:T(8,128)} %param.2) | copy-start | bytes 589828
  6.5 0.8 %copy-start.1 = (f32[6,1024]{1,0:T(8,128)S(1)}, f32[6,1024]{1,0:T(8,128)}, u32[]{:S(2)}) copy-start(f32[6,1024]{1,0:T(8,128)} %pot_ref.1) | copy-start | bytes 73732
  14.5 7.4 %collective-permute-start.7 = (f32[8,6144]{1,0:T(8,128)S(1)}, f32[8,6144]{1,0:T(8,128)S(1)}, u32[]{:S(2)}, u32[]{:S(2)}) collective-permute-start(f32[8,6144]{1,0:T(8,128)S(1)} %shard_map.29.refs_0_), channel_id=1, source_target_pairs={{0,16},{4,20},{8,24},{12,28},{16,0},{20,4},{24,8},{28,12},{1,17},{... | collective-permute-start | bytes 589832 | tf_op jit(solution)/shard_map/ppermute | solution.py:291
  16.1 7.2 %collective-permute-start.5 = (f32[8,6144]{1,0:T(8,128)S(1)}, f32[8,6144]{1,0:T(8,128)S(1)}, u32[]{:S(2)}, u32[]{:S(2)}) collective-permute-start(f32[8,6144]{1,0:T(8,128)S(1)} %shard_map.29.refs_0_), channel_id=1, source_target_pairs={{0,8},{4,12},{8,0},{12,4},{16,24},{20,28},{24,16},{28,20},{1,9},{5... | collective-permute-start | bytes 589832 | tf_op jit(solution)/shard_map/ppermute | solution.py:291
  17.6 7.8 %collective-permute-start.2 = (f32[8,6144]{1,0:T(8,128)S(1)}, f32[8,6144]{1,0:T(8,128)S(1)}, u32[]{:S(2)}, u32[]{:S(2)}) collective-permute-start(f32[8,6144]{1,0:T(8,128)S(1)} %shard_map.29.refs_0_), channel_id=1, source_target_pairs={{0,24},{4,28},{8,16},{12,20},{16,8},{20,12},{24,0},{28,4},{1,25},{... | collective-permute-start | bytes 589832 | tf_op jit(solution)/shard_map/ppermute | solution.py:291
  18.1 7.3 %collective-permute-start.4 = (f32[8,6144]{1,0:T(8,128)S(1)}, f32[8,6144]{1,0:T(8,128)S(1)}, u32[]{:S(2)}, u32[]{:S(2)}) collective-permute-start(f32[8,6144]{1,0:T(8,128)S(1)} %shard_map.29.refs_0_), channel_id=1, source_target_pairs={{0,4},{4,0},{8,12},{12,8},{16,20},{20,16},{24,28},{28,24},{1,5},{5... | collective-permute-start | bytes 589832 | tf_op jit(solution)/shard_map/ppermute | solution.py:292
  21.9 3.5 %collective-permute-start.8 = (f32[8,6144]{1,0:T(8,128)S(1)}, f32[8,6144]{1,0:T(8,128)S(1)}, u32[]{:S(2)}, u32[]{:S(2)}) collective-permute-start(f32[8,6144]{1,0:T(8,128)S(1)} %collective-permute-done.7.refs_4_), channel_id=1, source_target_pairs={{0,4},{4,0},{8,12},{12,8},{16,20},{20,16},{24,28},{28,24},{1,5},{5... | collective-permute-start | bytes 589832 | tf_op jit(solution)/shard_map/ppermute | solution.py:292
  23.3 2.1 %collective-permute-start.6 = (f32[8,6144]{1,0:T(8,128)S(1)}, f32[8,6144]{1,0:T(8,128)S(1)}, u32[]{:S(2)}, u32[]{:S(2)}) collective-permute-start(f32[8,6144]{1,0:T(8,128)S(1)} %collective-permute-done.5.refs_2_), channel_id=1, source_target_pairs={{0,4},{4,0},{8,12},{12,8},{16,20},{20,16},{24,28},{28,24},{1,5},{5... | collective-permute-start | bytes 589832 | tf_op jit(solution)/shard_map/ppermute | solution.py:292
  25.4 1.4 %collective-permute-start.3 = (f32[8,6144]{1,0:T(8,128)S(1)}, f32[8,6144]{1,0:T(8,128)S(1)}, u32[]{:S(2)}, u32[]{:S(2)}) collective-permute-start(f32[8,6144]{1,0:T(8,128)S(1)} %collective-permute-done.2.one_ref), channel_id=1, source_target_pairs={{0,4},{4,0},{8,12},{12,8},{16,20},{20,16},{24,28},{28,24},{1,5},{5... | collective-permute-start | bytes 589832 | tf_op jit(solution)/shard_map/ppermute | solution.py:292
  26.8 5.1 %collective-permute-start.11 = (f32[64,64]{1,0:T(8,128)S(1)}, f32[64,64]{1,0:T(8,128)S(1)}, u32[]{:S(2)}, u32[]{:S(2)}) collective-permute-start(f32[64,64]{1,0:T(8,128)S(1)} %get-tuple-element.11.refs_0_), channel_id=1, source_target_pairs={{0,7},{1,6},{2,5},{3,4},{4,3},{5,2},{6,1},{7,0},{8,15},{9,14},{10,... | collective-permute-start | bytes 49160 | tf_op jit(solution)/shard_map/ppermute | solution.py:282
  27.5 4.4 %collective-permute-start.10 = (f32[64,64]{1,0:T(8,128)S(1)}, f32[64,64]{1,0:T(8,128)S(1)}, u32[]{:S(2)}, u32[]{:S(2)}) collective-permute-start(f32[64,64]{1,0:T(8,128)S(1)} %get-tuple-element.11.refs_0_), channel_id=1, source_target_pairs={{0,5},{1,4},{2,7},{3,6},{4,1},{5,0},{6,3},{7,2},{8,13},{9,12},{10,... | collective-permute-start | bytes 49160 | tf_op jit(solution)/shard_map/ppermute | solution.py:282
  28.0 4.9 %collective-permute-start.9 = (f32[64,64]{1,0:T(8,128)S(1)}, f32[64,64]{1,0:T(8,128)S(1)}, u32[]{:S(2)}, u32[]{:S(2)}) collective-permute-start(f32[64,64]{1,0:T(8,128)S(1)} %get-tuple-element.11.refs_0_), channel_id=1, source_target_pairs={{0,6},{1,7},{2,4},{3,5},{4,2},{5,3},{6,0},{7,1},{8,14},{9,15},{10,... | collective-permute-start | bytes 49160 | tf_op jit(solution)/shard_map/ppermute | solution.py:282

commit v8 on v6

--- a/solution.py
+++ b/solution.py
@@ -111,10 +111,15 @@
     gram_ref[...] = products(whole, whole, scale)
 
 
+def beside(gram):
+    half = gram.shape[0] // 2
+    return jnp.concatenate([gram[:half], gram[half:]], 1)
+
+
 def last_kernel(scale, rank_ref, one_ref, two_ref, early_ref, before_ref, gram_ref, stack_ref):
     rank = rank_ref[0]
     rows = 2 * one_ref.shape[0]
-    total = gram_ref.shape[0]
+    total = early_ref.shape[0]
     needed = (rank // 2 ^ LAST // 2) < rank // 2
 
     @pl.when(needed)
@@ -126,11 +131,12 @@
         row = lax.broadcasted_iota(jnp.int32, (total, total), 0)
         column = lax.broadcasted_iota(jnp.int32, (total, total), 1)
         gram = jnp.where((column >= first) & (column < first + rows), repeated.T, early_ref[...])
-        gram_ref[...] = jnp.where((row >= first) & (row < first + rows), repeated, gram)
+        gram = jnp.where((row >= first) & (row < first + rows), repeated, gram)
+        gram_ref[...] = beside(gram)
 
     @pl.when(jnp.logical_not(needed))
     def _():
-        gram_ref[...] = early_ref[...]
+        gram_ref[...] = beside(early_ref[...])
 
 
 def invert_factor(gram, leading):
@@ -197,6 +203,8 @@
     gram = parts[0][...]
     for part in parts[1:]:
         gram = gram + part[...]
+    size = gram.shape[1] // 2
+    gram = jnp.concatenate([gram[:, :size], gram[:, size:]], 0)
     held = 2 * count
     chip = rank_ref[0] // 2
     low_chip = 0
@@ -291,7 +299,7 @@
     )
     return call(
         functools.partial(last_kernel, scale),
-        outs,
+        (shape(total // 2, 2 * total), outs[1]),
         [rank, *pairs[-1], early, before],
         aliases={4: 1},
     )

time: 35.3 us -> 34.8 us (0.986)
  waiting for transfers between devices: 16.1 us -> 15.6 us
    ppermute x3, waiting for transfers between devices: 2.15 us -> 1.59 us  [grid_sum(): return [part] + [lax.ppermute(part, BOTH, pairs) for pairs in sets]]
where the time goes in v8:
time: 34.8 us; the launch traced here: 34.2 us
  waiting for transfers between devices  15.6 us (45%)
  starting transfers between devices  12.9 us (37%)
  Pallas kernels  3.9 us (11%)
  local copies, waits for them, and re-layouts  1.72 us (5%)
    ppermute x3, waiting for transfers between devices, gather_all(): lax.ppermute(work, 'orb', exchange(orb, mask))  7.3 us
    ppermute x1, waiting for transfers between devices, halo(): one = lax.ppermute(planes, BOTH, partners(orb, grid, (3, 1)))  4.72 us
    pallas_call x5, Pallas kernels, call(): pl.pallas_call(kernel, out_shape=out_shape, in_specs=in_specs, out_specs=...  3.9 us
    ppermute x3, starting transfers between devices, grid_sum(): return [part] + [lax.ppermute(part, BOTH, pairs) for pairs in sets]  3.87 us
    ppermute x3, starting transfers between devices, gather_all(): lax.ppermute(work, 'orb', exchange(orb, mask))  3.55 us
    ppermute x1, starting transfers between devices, halo(): two = lax.ppermute(planes, BOTH, partners(orb, grid, (1, 3)))  3.02 us
    ppermute x1, starting transfers between devices, halo(): one = lax.ppermute(planes, BOTH, partners(orb, grid, (3, 1)))  2.47 us
    unnamed x4, local copies, waits for them, and re-layouts  1.72 us
  transfers between devices with their start and end apart: 12, of which 8 were waited for; matrix products, arithmetic and copies ran while one was open for 0% of the time, Pallas kernels for 6%

profile of v8, /device:TPU:0, one launch (start us, length us, event | category | flops | bytes accessed | tf_op | source)
XLA Modules:
  0.0 34.2 jit_solution(15562217281640706036)
XLA Ops:
  0.0 3.0 %collective-permute-start.1 = (f32[6,8,1024]{2,1,0:T(8,128)}, f32[6,8,1024]{2,1,0:T(8,128)S(1)}, u32[]{:S(2)}, u32[]{:S(2)}) collective-permute-start(f32[6,8,1024]{2,1,0:T(8,128)} %bitcast.4), channel_id=1, source_target_pairs={{0,1},{1,0},{2,3},{3,2},{4,7},{5,6},{6,5},{7,4},{8,9},{9,8},{10,11... | collective-permute-start | bytes 589832 | tf_op jit(solution)/shard_map/ppermute | solution.py:273
  3.0 2.5 %collective-permute-start = (f32[6,8,1024]{2,1,0:T(8,128)}, f32[6,8,1024]{2,1,0:T(8,128)S(1)}, u32[]{:S(2)}, u32[]{:S(2)}) collective-permute-start(f32[6,8,1024]{2,1,0:T(8,128)} %bitcast.5), channel_id=1, source_target_pairs={{0,3},{1,2},{2,1},{3,0},{4,5},{5,4},{6,7},{7,6},{8,11},{9,10},{10,... | collective-permute-start | bytes 589832 | tf_op jit(solution)/shard_map/ppermute | solution.py:272
  5.5 0.0 copy-start
  5.5 1.0 %copy-done = f32[8,6,1024]{2,0,1:T(8,128)S(1)} copy-done((f32[8,6,1024]{2,0,1:T(8,128)S(1)}, f32[8,6,1024]{2,0,1:T(8,128)}, u32[]{:S(2)}) %copy-start) | copy-done | bytes 196632
  6.5 0.8 %copy-done.1 = f32[6,1024]{1,0:T(8,128)S(1)} copy-done((f32[6,1024]{1,0:T(8,128)S(1)}, f32[6,1024]{1,0:T(8,128)}, u32[]{:S(2)}) %copy-start.1) | copy-done | bytes 24600
  7.2 0.9 %shard_map.28.local_ref = f32[8,6144]{1,0:T(8,128)S(1)} custom-call(f32[6,8,1024]{2,1,0:T(8,128)S(1)} %bitcast.6, f32[6,1024]{1,0:T(8,128)S(1)} %copy-done.1), custom_call_target="tpu_custom_call" | custom-call | flops 1000000000 | bytes 1000000 | tf_op jit(solution)/shard_map/pallas_call | solution.py:237
  8.2 1.5 %collective-permute-done.1.two_ref = f32[6,8,1024]{2,1,0:T(8,128)S(1)} collective-permute-done((f32[6,8,1024]{2,1,0:T(8,128)}, f32[6,8,1024]{2,1,0:T(8,128)S(1)}, u32[]{:S(2)}, u32[]{:S(2)}) %collective-permute-start.1) | collective-permute-done | bytes 196640 | tf_op jit(solution)/shard_map/ppermute | solution.py:273
  9.7 4.7 %collective-permute-done.one_ref = f32[6,8,1024]{2,1,0:T(8,128)S(1)} collective-permute-done((f32[6,8,1024]{2,1,0:T(8,128)}, f32[6,8,1024]{2,1,0:T(8,128)S(1)}, u32[]{:S(2)}, u32[]{:S(2)}) %collective-permute-start) | collective-permute-done | bytes 196640 | tf_op jit(solution)/shard_map/ppermute | solution.py:272
  14.4 0.1 shard_map.29.refs_0_
  14.5 1.6 %collective-permute-start.7 = (f32[8,6144]{1,0:T(8,128)S(1)}, f32[8,6144]{1,0:T(8,128)S(1)}, u32[]{:S(2)}, u32[]{:S(2)}) collective-permute-start(f32[8,6144]{1,0:T(8,128)S(1)} %shard_map.29.refs_0_), channel_id=1, source_target_pairs={{0,16},{4,20},{8,24},{12,28},{16,0},{20,4},{24,8},{28,12},{1,17},{... | collective-permute-start | bytes 589832 | tf_op jit(solution)/shard_map/ppermute | solution.py:294
  16.1 1.5 %collective-permute-start.5 = (f32[8,6144]{1,0:T(8,128)S(1)}, f32[8,6144]{1,0:T(8,128)S(1)}, u32[]{:S(2)}, u32[]{:S(2)}) collective-permute-start(f32[8,6144]{1,0:T(8,128)S(1)} %shard_map.29.refs_0_), channel_id=1, source_target_pairs={{0,8},{4,12},{8,0},{12,4},{16,24},{20,28},{24,16},{28,20},{1,9},{5... | collective-permute-start | bytes 589832 | tf_op jit(solution)/shard_map/ppermute | solution.py:294
  17.6 0.5 %collective-permute-start.2 = (f32[8,6144]{1,0:T(8,128)S(1)}, f32[8,6144]{1,0:T(8,128)S(1)}, u32[]{:S(2)}, u32[]{:S(2)}) collective-permute-start(f32[8,6144]{1,0:T(8,128)S(1)} %shard_map.29.refs_0_), channel_id=1, source_target_pairs={{0,24},{4,28},{8,16},{12,20},{16,8},{20,12},{24,0},{28,4},{1,25},{... | collective-permute-start | bytes 589832 | tf_op jit(solution)/shard_map/ppermute | solution.py:294
  18.1 0.0 collective-permute-start.4
  18.1 3.8 %collective-permute-done.7.refs_4_ = f32[8,6144]{1,0:T(8,128)S(1)} collective-permute-done((f32[8,6144]{1,0:T(8,128)S(1)}, f32[8,6144]{1,0:T(8,128)S(1)}, u32[]{:S(2)}, u32[]{:S(2)}) %collective-permute-start.7) | collective-permute-done | bytes 196640 | tf_op jit(solution)/shard_map/ppermute | solution.py:294
  21.9 0.0 collective-permute-start.8
  21.9 1.4 %collective-permute-done.5.refs_2_ = f32[8,6144]{1,0:T(8,128)S(1)} collective-permute-done((f32[8,6144]{1,0:T(8,128)S(1)}, f32[8,6144]{1,0:T(8,128)S(1)}, u32[]{:S(2)}, u32[]{:S(2)}) %collective-permute-start.5) | collective-permute-done | bytes 196640 | tf_op jit(solution)/shard_map/ppermute | solution.py:294
  23.3 0.0 collective-permute-start.6
  23.3 2.1 %collective-permute-done.2.one_ref = f32[8,6144]{1,0:T(8,128)S(1)} collective-permute-done((f32[8,6144]{1,0:T(8,128)S(1)}, f32[8,6144]{1,0:T(8,128)S(1)}, u32[]{:S(2)}, u32[]{:S(2)}) %collective-permute-start.2) | collective-permute-done | bytes 196640 | tf_op jit(solution)/shard_map/ppermute | solution.py:294
  25.4 0.0 collective-permute-start.3
  25.4 0.0 collective-permute-done.4.refs_1_
  25.4 0.0 collective-permute-done.8.refs_5_
  25.4 0.0 collective-permute-done.6.refs_3_
  25.4 1.0 %shard_map.30 = (f32[64,64]{1,0:T(8,128)S(1)}, bf16[128,6144]{1,0:T(8,128)(2,1)S(1)}) custom-call(s32[1]{0:T(128)} %bitcast.rank_ref, f32[8,6144]{1,0:T(8,128)S(1)} %shard_map.29.refs_0_, f32[8,6144]{1,0:T(8,128)S(1)} %collective-permute-done.4.refs_1_, f32[8,6144]{1,0:T(8,128)S(1)} %collective-permute-done.5.refs_2_, ...), custom_call_target="tpu_custom_call" | custom-call | bytes 1000000 | tf_op jit(solution)/shard_map/pallas_call | solution.py:237
  26.4 0.4 %collective-permute-done.3.two_ref = f32[8,6144]{1,0:T(8,128)S(1)} collective-permute-done((f32[8,6144]{1,0:T(8,128)S(1)}, f32[8,6144]{1,0:T(8,128)S(1)}, u32[]{:S(2)}, u32[]{:S(2)}) %collective-permute-start.3) | collective-permute-done | bytes 196640 | tf_op jit(solution)/shard_map/ppermute | solution.py:295
  26.8 0.1 shard_map.31
  26.9 0.6 %collective-permute-start.11 = (f32[32,128]{1,0:T(8,128)S(1)}, f32[32,128]{1,0:T(8,128)S(1)}, u32[]{:S(2)}, u32[]{:S(2)}) collective-permute-start(f32[32,128]{1,0:T(8,128)S(1)} %get-tuple-element.11.refs_0_), channel_id=1, source_target_pairs={{0,7},{1,6},{2,5},{3,4},{4,3},{5,2},{6,1},{7,0},{8,15},{9,14},{10,... | collective-permute-start | bytes 49160 | tf_op jit(solution)/shard_map/ppermute | solution.py:285
  27.5 0.5 %collective-permute-start.10 = (f32[32,128]{1,0:T(8,128)S(1)}, f32[32,128]{1,0:T(8,128)S(1)}, u32[]{:S(2)}, u32[]{:S(2)}) collective-permute-start(f32[32,128]{1,0:T(8,128)S(1)} %get-tuple-element.11.refs_0_), channel_id=1, source_target_pairs={{0,5},{1,4},{2,7},{3,6},{4,1},{5,0},{6,3},{7,2},{8,13},{9,12},{10,... | collective-permute-start | bytes 49160 | tf_op jit(solution)/shard_map/ppermute | solution.py:285
  28.0 2.7 %collective-permute-start.9 = (f32[32,128]{1,0:T(8,128)S(1)}, f32[32,128]{1,0:T(8,128)S(1)}, u32[]{:S(2)}, u32[]{:S(2)}) collective-permute-start(f32[32,128]{1,0:T(8,128)S(1)} %get-tuple-element.11.refs_0_), channel_id=1, source_target_pairs={{0,6},{1,7},{2,4},{3,5},{4,2},{5,3},{6,0},{7,1},{8,14},{9,15},{10,... | collective-permute-start | bytes 49160 | tf_op jit(solution)/shard_map/ppermute | solution.py:285
  30.8 1.1 %collective-permute-done.11.refs_3_ = f32[32,128]{1,0:T(8,128)S(1)} collective-permute-done((f32[32,128]{1,0:T(8,128)S(1)}, f32[32,128]{1,0:T(8,128)S(1)}, u32[]{:S(2)}, u32[]{:S(2)}) %collective-permute-start.11) | collective-permute-done | bytes 16416 | tf_op jit(solution)/shard_map/ppermute | solution.py:285
  31.9 0.0 collective-permute-done.10.refs_2_
  31.9 0.5 %collective-permute-done.9.refs_1_ = f32[32,128]{1,0:T(8,128)S(1)} collective-permute-done((f32[32,128]{1,0:T(8,128)S(1)}, f32[32,128]{1,0:T(8,128)S(1)}, u32[]{:S(2)}, u32[]{:S(2)}) %collective-permute-start.9) | collective-permute-done | bytes 16416 | tf_op jit(solution)/shard_map/ppermute | solution.py:285
  32.4 1.8 %shard_map.32 = f32[6,8,1024]{2,1,0:T(8,128)} custom-call(s32[1]{0:T(128)} %bitcast.rank_ref, f32[32,128]{1,0:T(8,128)S(1)} %get-tuple-element.11.refs_0_, f32[32,128]{1,0:T(8,128)S(1)} %collective-permute-done.9.refs_1_, f32[32,128]{1,0:T(8,128)S(1)} %collective-permute-done.10.refs_2_, f32[32,128]{1,0:T(8,128)S(1)} %collective-permute-done.11.refs_3_, ...), custom_call_target="tpu_custom_call" | custom-call | bytes 1000000 | tf_op jit(solution)/shard_map/pallas_call | solution.py:237
  (1 shorter events, 0.0 us)
Async XLA Ops:
  0.0 9.7 %collective-permute-start.1 = (f32[6,8,1024]{2,1,0:T(8,128)}, f32[6,8,1024]{2,1,0:T(8,128)S(1)}, u32[]{:S(2)}, u32[]{:S(2)}) collective-permute-start(f32[6,8,1024]{2,1,0:T(8,128)} %bitcast.4), channel_id=1, source_target_pairs={{0,1},{1,0},{2,3},{3,2},{4,7},{5,6},{6,5},{7,4},{8,9},{9,8},{10,11... | collective-permute-start | bytes 589832 | tf_op jit(solution)/shard_map/ppermute | solution.py:273
  3.0 11.4 %collective-permute-start = (f32[6,8,1024]{2,1,0:T(8,128)}, f32[6,8,1024]{2,1,0:T(8,128)S(1)}, u32[]{:S(2)}, u32[]{:S(2)}) collective-permute-start(f32[6,8,1024]{2,1,0:T(8,128)} %bitcast.5), channel_id=1, source_target_pairs={{0,3},{1,2},{2,1},{3,0},{4,5},{5,4},{6,7},{7,6},{8,11},{9,10},{10,... | collective-permute-start | bytes 589832 | tf_op jit(solution)/shard_map/ppermute | solution.py:272
  5.5 1.0 %copy-start = (f32[8,6,1024]{2,0,1:T(8,128)S(1)}, f32[8,6,1024]{2,0,1:T(8,128)}, u32[]{:S(2)}) copy-start(f32[8,6,1024]{2,0,1:T(8,128)} %param.2) | copy-start | bytes 589828
  6.5 0.8 %copy-start.1 = (f32[6,1024]{1,0:T(8,128)S(1)}, f32[6,1024]{1,0:T(8,128)}, u32[]{:S(2)}) copy-start(f32[6,1024]{1,0:T(8,128)} %pot_ref.1) | copy-start | bytes 73732
  14.5 7.4 %collective-permute-start.7 = (f32[8,6144]{1,0:T(8,128)S(1)}, f32[8,6144]{1,0:T(8,128)S(1)}, u32[]{:S(2)}, u32[]{:S(2)}) collective-permute-start(f32[8,6144]{1,0:T(8,128)S(1)} %shard_map.29.refs_0_), channel_id=1, source_target_pairs={{0,16},{4,20},{8,24},{12,28},{16,0},{20,4},{24,8},{28,12},{1,17},{... | collective-permute-start | bytes 589832 | tf_op jit(solution)/shard_map/ppermute | solution.py:294
  16.1 7.2 %collective-permute-start.5 = (f32[8,6144]{1,0:T(8,128)S(1)}, f32[8,6144]{1,0:T(8,128)S(1)}, u32[]{:S(2)}, u32[]{:S(2)}) collective-permute-start(f32[8,6144]{1,0:T(8,128)S(1)} %shard_map.29.refs_0_), channel_id=1, source_target_pairs={{0,8},{4,12},{8,0},{12,4},{16,24},{20,28},{24,16},{28,20},{1,9},{5... | collective-permute-start | bytes 589832 | tf_op jit(solution)/shard_map/ppermute | solution.py:294
  17.6 7.8 %collective-permute-start.2 = (f32[8,6144]{1,0:T(8,128)S(1)}, f32[8,6144]{1,0:T(8,128)S(1)}, u32[]{:S(2)}, u32[]{:S(2)}) collective-permute-start(f32[8,6144]{1,0:T(8,128)S(1)} %shard_map.29.refs_0_), channel_id=1, source_target_pairs={{0,24},{4,28},{8,16},{12,20},{16,8},{20,12},{24,0},{28,4},{1,25},{... | collective-permute-start | bytes 589832 | tf_op jit(solution)/shard_map/ppermute | solution.py:294
  18.1 7.3 %collective-permute-start.4 = (f32[8,6144]{1,0:T(8,128)S(1)}, f32[8,6144]{1,0:T(8,128)S(1)}, u32[]{:S(2)}, u32[]{:S(2)}) collective-permute-start(f32[8,6144]{1,0:T(8,128)S(1)} %shard_map.29.refs_0_), channel_id=1, source_target_pairs={{0,4},{4,0},{8,12},{12,8},{16,20},{20,16},{24,28},{28,24},{1,5},{5... | collective-permute-start | bytes 589832 | tf_op jit(solution)/shard_map/ppermute | solution.py:295
  21.9 3.5 %collective-permute-start.8 = (f32[8,6144]{1,0:T(8,128)S(1)}, f32[8,6144]{1,0:T(8,128)S(1)}, u32[]{:S(2)}, u32[]{:S(2)}) collective-permute-start(f32[8,6144]{1,0:T(8,128)S(1)} %collective-permute-done.7.refs_4_), channel_id=1, source_target_pairs={{0,4},{4,0},{8,12},{12,8},{16,20},{20,16},{24,28},{28,24},{1,5},{5... | collective-permute-start | bytes 589832 | tf_op jit(solution)/shard_map/ppermute | solution.py:295
  23.3 2.1 %collective-permute-start.6 = (f32[8,6144]{1,0:T(8,128)S(1)}, f32[8,6144]{1,0:T(8,128)S(1)}, u32[]{:S(2)}, u32[]{:S(2)}) collective-permute-start(f32[8,6144]{1,0:T(8,128)S(1)} %collective-permute-done.5.refs_2_), channel_id=1, source_target_pairs={{0,4},{4,0},{8,12},{12,8},{16,20},{20,16},{24,28},{28,24},{1,5},{5... | collective-permute-start | bytes 589832 | tf_op jit(solution)/shard_map/ppermute | solution.py:295
  25.4 1.4 %collective-permute-start.3 = (f32[8,6144]{1,0:T(8,128)S(1)}, f32[8,6144]{1,0:T(8,128)S(1)}, u32[]{:S(2)}, u32[]{:S(2)}) collective-permute-start(f32[8,6144]{1,0:T(8,128)S(1)} %collective-permute-done.2.one_ref), channel_id=1, source_target_pairs={{0,4},{4,0},{8,12},{12,8},{16,20},{20,16},{24,28},{28,24},{1,5},{5... | collective-permute-start | bytes 589832 | tf_op jit(solution)/shard_map/ppermute | solution.py:295
  26.9 5.0 %collective-permute-start.11 = (f32[32,128]{1,0:T(8,128)S(1)}, f32[32,128]{1,0:T(8,128)S(1)}, u32[]{:S(2)}, u32[]{:S(2)}) collective-permute-start(f32[32,128]{1,0:T(8,128)S(1)} %get-tuple-element.11.refs_0_), channel_id=1, source_target_pairs={{0,7},{1,6},{2,5},{3,4},{4,3},{5,2},{6,1},{7,0},{8,15},{9,14},{10,... | collective-permute-start | bytes 49160 | tf_op jit(solution)/shard_map/ppermute | solution.py:285
  27.5 4.3 %collective-permute-start.10 = (f32[32,128]{1,0:T(8,128)S(1)}, f32[32,128]{1,0:T(8,128)S(1)}, u32[]{:S(2)}, u32[]{:S(2)}) collective-permute-start(f32[32,128]{1,0:T(8,128)S(1)} %get-tuple-element.11.refs_0_), channel_id=1, source_target_pairs={{0,5},{1,4},{2,7},{3,6},{4,1},{5,0},{6,3},{7,2},{8,13},{9,12},{10,... | collective-permute-start | bytes 49160 | tf_op jit(solution)/shard_map/ppermute | solution.py:285
  28.0 4.3 %collective-permute-start.9 = (f32[32,128]{1,0:T(8,128)S(1)}, f32[32,128]{1,0:T(8,128)S(1)}, u32[]{:S(2)}, u32[]{:S(2)}) collective-permute-start(f32[32,128]{1,0:T(8,128)S(1)} %get-tuple-element.11.refs_0_), channel_id=1, source_target_pairs={{0,6},{1,7},{2,4},{3,5},{4,2},{5,3},{6,0},{7,1},{8,14},{9,15},{10,... | collective-permute-start | bytes 49160 | tf_op jit(solution)/shard_map/ppermute | solution.py:285

commit v9 on v8

--- a/solution.py
+++ b/solution.py
@@ -208,7 +208,7 @@
     held = 2 * count
     chip = rank_ref[0] // 2
     low_chip = 0
-    for top in (2, 4):
+    for top in (1, 2, 3, 4):
 
         @pl.when((chip >= low_chip) & (chip < top))
         def _(top=top):

time: 34.8 us -> 34.8 us (level)
  the two profiles are of different devices: /device:TPU:0 before, /device:TPU:23 now
where the time goes in v9:
time: 34.8 us; the launch traced here: 34.6 us
  starting transfers between devices  17.4 us (50%)
  waiting for transfers between devices  10.1 us (29%)
  Pallas kernels  5.34 us (15%)
  local copies, waits for them, and re-layouts  1.72 us (5%)
    ppermute x4, starting transfers between devices, gather_all(): pairs.append([block, lax.ppermute(block, 'orb', exchange(orb, 1))])  10.1 us
    pallas_call x5, Pallas kernels, call(): pl.pallas_call(kernel, out_shape=out_shape, in_specs=in_specs, out_specs=...  5.34 us
    ppermute x3, waiting for transfers between devices, grid_sum(): return [part] + [lax.ppermute(part, BOTH, pairs) for pairs in sets]  4.06 us
    ppermute x1, waiting for transfers between devices, halo(): one = lax.ppermute(planes, BOTH, partners(orb, grid, (3, 1)))  3.64 us
    ppermute x3, starting transfers between devices, grid_sum(): return [part] + [lax.ppermute(part, BOTH, pairs) for pairs in sets]  3.3 us
    ppermute x3, starting transfers between devices, gather_all(): lax.ppermute(work, 'orb', exchange(orb, mask))  2.71 us
    ppermute x1, waiting for transfers between devices, halo(): two = lax.ppermute(planes, BOTH, partners(orb, grid, (1, 3)))  2.34 us
    unnamed x4, local copies, waits for them, and re-layouts  1.72 us
  transfers between devices with their start and end apart: 12, of which 5 were waited for; matrix products, arithmetic and copies ran while one was open for 0% of the time, Pallas kernels for 6%

profile of v9, /device:TPU:23, one launch (start us, length us, event | category | flops | bytes accessed | tf_op | source)
XLA Modules:
  0.0 34.6 jit_solution(5346212692395432860)
XLA Ops:
  0.0 0.2 collective-permute-start.1
  0.2 1.1 %collective-permute-start = (f32[6,8,1024]{2,1,0:T(8,128)}, f32[6,8,1024]{2,1,0:T(8,128)S(1)}, u32[]{:S(2)}, u32[]{:S(2)}) collective-permute-start(f32[6,8,1024]{2,1,0:T(8,128)} %bitcast.5), channel_id=1, source_target_pairs={{0,3},{1,2},{2,1},{3,0},{4,5},{5,4},{6,7},{7,6},{8,11},{9,10},{10,... | collective-permute-start | bytes 589832 | tf_op jit(solution)/shard_map/ppermute | solution.py:272
  1.3 0.0 copy-start
  1.3 1.0 %copy-done = f32[8,6,1024]{2,0,1:T(8,128)S(1)} copy-done((f32[8,6,1024]{2,0,1:T(8,128)S(1)}, f32[8,6,1024]{2,0,1:T(8,128)}, u32[]{:S(2)}) %copy-start) | copy-done | bytes 196632
  2.3 0.8 %copy-done.1 = f32[6,1024]{1,0:T(8,128)S(1)} copy-done((f32[6,1024]{1,0:T(8,128)S(1)}, f32[6,1024]{1,0:T(8,128)}, u32[]{:S(2)}) %copy-start.1) | copy-done | bytes 24600
  3.0 0.9 %shard_map.28.local_ref = f32[8,6144]{1,0:T(8,128)S(1)} custom-call(f32[6,8,1024]{2,1,0:T(8,128)S(1)} %bitcast.6, f32[6,1024]{1,0:T(8,128)S(1)} %copy-done.1), custom_call_target="tpu_custom_call" | custom-call | flops 1000000000 | bytes 1000000 | tf_op jit(solution)/shard_map/pallas_call | solution.py:237
  4.0 2.3 %collective-permute-done.1.two_ref = f32[6,8,1024]{2,1,0:T(8,128)S(1)} collective-permute-done((f32[6,8,1024]{2,1,0:T(8,128)}, f32[6,8,1024]{2,1,0:T(8,128)S(1)}, u32[]{:S(2)}, u32[]{:S(2)}) %collective-permute-start.1) | collective-permute-done | bytes 196640 | tf_op jit(solution)/shard_map/ppermute | solution.py:273
  6.3 3.6 %collective-permute-done.one_ref = f32[6,8,1024]{2,1,0:T(8,128)S(1)} collective-permute-done((f32[6,8,1024]{2,1,0:T(8,128)}, f32[6,8,1024]{2,1,0:T(8,128)S(1)}, u32[]{:S(2)}, u32[]{:S(2)}) %collective-permute-start) | collective-permute-done | bytes 196640 | tf_op jit(solution)/shard_map/ppermute | solution.py:272
  9.9 0.1 shard_map.29.refs_0_
  10.0 0.3 collective-permute-start.7
  10.3 0.3 collective-permute-start.5
  10.6 2.2 %collective-permute-start.2 = (f32[8,6144]{1,0:T(8,128)S(1)}, f32[8,6144]{1,0:T(8,128)S(1)}, u32[]{:S(2)}, u32[]{:S(2)}) collective-permute-start(f32[8,6144]{1,0:T(8,128)S(1)} %shard_map.29.refs_0_), channel_id=1, source_target_pairs={{0,24},{4,28},{8,16},{12,20},{16,8},{20,12},{24,0},{28,4},{1,25},{... | collective-permute-start | bytes 589832 | tf_op jit(solution)/shard_map/ppermute | solution.py:294
  12.8 2.9 %collective-permute-start.4 = (f32[8,6144]{1,0:T(8,128)S(1)}, f32[8,6144]{1,0:T(8,128)S(1)}, u32[]{:S(2)}, u32[]{:S(2)}) collective-permute-start(f32[8,6144]{1,0:T(8,128)S(1)} %shard_map.29.refs_0_), channel_id=1, source_target_pairs={{0,4},{4,0},{8,12},{12,8},{16,20},{20,16},{24,28},{28,24},{1,5},{5... | collective-permute-start | bytes 589832 | tf_op jit(solution)/shard_map/ppermute | solution.py:295
  15.6 0.0 collective-permute-done.7.refs_4_
  15.6 4.2 %collective-permute-start.8 = (f32[8,6144]{1,0:T(8,128)S(1)}, f32[8,6144]{1,0:T(8,128)S(1)}, u32[]{:S(2)}, u32[]{:S(2)}) collective-permute-start(f32[8,6144]{1,0:T(8,128)S(1)} %collective-permute-done.7.refs_4_), channel_id=1, source_target_pairs={{0,4},{4,0},{8,12},{12,8},{16,20},{20,16},{24,28},{28,24},{1,5},{5... | collective-permute-start | bytes 589832 | tf_op jit(solution)/shard_map/ppermute | solution.py:295
  19.8 0.0 collective-permute-done.5.refs_2_
  19.8 0.0 collective-permute-start.6
  19.8 0.0 collective-permute-done.2.one_ref
  19.8 3.0 %collective-permute-start.3 = (f32[8,6144]{1,0:T(8,128)S(1)}, f32[8,6144]{1,0:T(8,128)S(1)}, u32[]{:S(2)}, u32[]{:S(2)}) collective-permute-start(f32[8,6144]{1,0:T(8,128)S(1)} %collective-permute-done.2.one_ref), channel_id=1, source_target_pairs={{0,4},{4,0},{8,12},{12,8},{16,20},{20,16},{24,28},{28,24},{1,5},{5... | collective-permute-start | bytes 589832 | tf_op jit(solution)/shard_map/ppermute | solution.py:295
  22.8 0.0 collective-permute-done.4.refs_1_
  22.8 0.0 collective-permute-done.8.refs_5_
  22.8 0.0 collective-permute-done.6.refs_3_
  22.8 1.0 %shard_map.30 = (f32[64,64]{1,0:T(8,128)S(1)}, bf16[128,6144]{1,0:T(8,128)(2,1)S(1)}) custom-call(s32[1]{0:T(128)} %bitcast.rank_ref, f32[8,6144]{1,0:T(8,128)S(1)} %shard_map.29.refs_0_, f32[8,6144]{1,0:T(8,128)S(1)} %collective-permute-done.4.refs_1_, f32[8,6144]{1,0:T(8,128)S(1)} %collective-permute-done.5.refs_2_, ...), custom_call_target="tpu_custom_call" | custom-call | bytes 1000000 | tf_op jit(solution)/shard_map/pallas_call | solution.py:237
  23.8 0.0 collective-permute-done.3.two_ref
  23.9 0.9 %shard_map.31 = (f32[32,128]{1,0:T(8,128)S(1)}, bf16[128,6144]{1,0:T(8,128)(2,1)S(1)}) custom-call(s32[1]{0:T(128)} %bitcast.rank_ref, f32[8,6144]{1,0:T(8,128)S(1)} %collective-permute-done.2.one_ref, f32[8,6144]{1,0:T(8,128)S(1)} %collective-permute-done.3.two_ref, f32[64,64]{1,0:T(8,128)S(1)} %get-tuple-element.9.early_ref, ...), custom_call_target="tpu_custom_call", output_to_operand_aliasing={{1}: (4, {})} | custom-call | bytes 1000000 | tf_op jit(solution)/shard_map/pallas_call | solution.py:237
  24.8 2.0 %collective-permute-start.11 = (f32[32,128]{1,0:T(8,128)S(1)}, f32[32,128]{1,0:T(8,128)S(1)}, u32[]{:S(2)}, u32[]{:S(2)}) collective-permute-start(f32[32,128]{1,0:T(8,128)S(1)} %get-tuple-element.11.refs_0_), channel_id=1, source_target_pairs={{0,7},{1,6},{2,5},{3,4},{4,3},{5,2},{6,1},{7,0},{8,15},{9,14},{10,... | collective-permute-start | bytes 49160 | tf_op jit(solution)/shard_map/ppermute | solution.py:285
  26.8 1.3 %collective-permute-start.10 = (f32[32,128]{1,0:T(8,128)S(1)}, f32[32,128]{1,0:T(8,128)S(1)}, u32[]{:S(2)}, u32[]{:S(2)}) collective-permute-start(f32[32,128]{1,0:T(8,128)S(1)} %get-tuple-element.11.refs_0_), channel_id=1, source_target_pairs={{0,5},{1,4},{2,7},{3,6},{4,1},{5,0},{6,3},{7,2},{8,13},{9,12},{10,... | collective-permute-start | bytes 49160 | tf_op jit(solution)/shard_map/ppermute | solution.py:285
  28.1 0.0 collective-permute-start.9
  28.1 0.1 collective-permute-done.11.refs_3_
  28.2 1.7 %collective-permute-done.10.refs_2_ = f32[32,128]{1,0:T(8,128)S(1)} collective-permute-done((f32[32,128]{1,0:T(8,128)S(1)}, f32[32,128]{1,0:T(8,128)S(1)}, u32[]{:S(2)}, u32[]{:S(2)}) %collective-permute-start.10) | collective-permute-done | bytes 16416 | tf_op jit(solution)/shard_map/ppermute | solution.py:285
  30.0 2.2 %collective-permute-done.9.refs_1_ = f32[32,128]{1,0:T(8,128)S(1)} collective-permute-done((f32[32,128]{1,0:T(8,128)S(1)}, f32[32,128]{1,0:T(8,128)S(1)}, u32[]{:S(2)}, u32[]{:S(2)}) %collective-permute-start.9) | collective-permute-done | bytes 16416 | tf_op jit(solution)/shard_map/ppermute | solution.py:285
  32.2 2.4 %shard_map.32 = f32[6,8,1024]{2,1,0:T(8,128)} custom-call(s32[1]{0:T(128)} %bitcast.rank_ref, f32[32,128]{1,0:T(8,128)S(1)} %get-tuple-element.11.refs_0_, f32[32,128]{1,0:T(8,128)S(1)} %collective-permute-done.9.refs_1_, f32[32,128]{1,0:T(8,128)S(1)} %collective-permute-done.10.refs_2_, f32[32,128]{1,0:T(8,128)S(1)} %collective-permute-done.11.refs_3_, ...), custom_call_target="tpu_custom_call" | custom-call | bytes 1000000 | tf_op jit(solution)/shard_map/pallas_call | solution.py:237
  (1 shorter events, 0.0 us)
Async XLA Ops:
  0.0 6.3 %collective-permute-start.1 = (f32[6,8,1024]{2,1,0:T(8,128)}, f32[6,8,1024]{2,1,0:T(8,128)S(1)}, u32[]{:S(2)}, u32[]{:S(2)}) collective-permute-start(f32[6,8,1024]{2,1,0:T(8,128)} %bitcast.4), channel_id=1, source_target_pairs={{0,1},{1,0},{2,3},{3,2},{4,7},{5,6},{6,5},{7,4},{8,9},{9,8},{10,11... | collective-permute-start | bytes 589832 | tf_op jit(solution)/shard_map/ppermute | solution.py:273
  0.2 9.8 %collective-permute-start = (f32[6,8,1024]{2,1,0:T(8,128)}, f32[6,8,1024]{2,1,0:T(8,128)S(1)}, u32[]{:S(2)}, u32[]{:S(2)}) collective-permute-start(f32[6,8,1024]{2,1,0:T(8,128)} %bitcast.5), channel_id=1, source_target_pairs={{0,3},{1,2},{2,1},{3,0},{4,5},{5,4},{6,7},{7,6},{8,11},{9,10},{10,... | collective-permute-start | bytes 589832 | tf_op jit(solution)/shard_map/ppermute | solution.py:272
  1.3 1.0 %copy-start = (f32[8,6,1024]{2,0,1:T(8,128)S(1)}, f32[8,6,1024]{2,0,1:T(8,128)}, u32[]{:S(2)}) copy-start(f32[8,6,1024]{2,0,1:T(8,128)} %param.2) | copy-start | bytes 589828
  2.3 0.8 %copy-start.1 = (f32[6,1024]{1,0:T(8,128)S(1)}, f32[6,1024]{1,0:T(8,128)}, u32[]{:S(2)}) copy-start(f32[6,1024]{1,0:T(8,128)} %pot_ref.1) | copy-start | bytes 73732
  10.0 5.6 %collective-permute-start.7 = (f32[8,6144]{1,0:T(8,128)S(1)}, f32[8,6144]{1,0:T(8,128)S(1)}, u32[]{:S(2)}, u32[]{:S(2)}) collective-permute-start(f32[8,6144]{1,0:T(8,128)S(1)} %shard_map.29.refs_0_), channel_id=1, source_target_pairs={{0,16},{4,20},{8,24},{12,28},{16,0},{20,4},{24,8},{28,12},{1,17},{... | collective-permute-start | bytes 589832 | tf_op jit(solution)/shard_map/ppermute | solution.py:294
  10.3 9.5 %collective-permute-start.5 = (f32[8,6144]{1,0:T(8,128)S(1)}, f32[8,6144]{1,0:T(8,128)S(1)}, u32[]{:S(2)}, u32[]{:S(2)}) collective-permute-start(f32[8,6144]{1,0:T(8,128)S(1)} %shard_map.29.refs_0_), channel_id=1, source_target_pairs={{0,8},{4,12},{8,0},{12,4},{16,24},{20,28},{24,16},{28,20},{1,9},{5... | collective-permute-start | bytes 589832 | tf_op jit(solution)/shard_map/ppermute | solution.py:294
  10.6 9.2 %collective-permute-start.2 = (f32[8,6144]{1,0:T(8,128)S(1)}, f32[8,6144]{1,0:T(8,128)S(1)}, u32[]{:S(2)}, u32[]{:S(2)}) collective-permute-start(f32[8,6144]{1,0:T(8,128)S(1)} %shard_map.29.refs_0_), channel_id=1, source_target_pairs={{0,24},{4,28},{8,16},{12,20},{16,8},{20,12},{24,0},{28,4},{1,25},{... | collective-permute-start | bytes 589832 | tf_op jit(solution)/shard_map/ppermute | solution.py:294
  12.8 10.1 %collective-permute-start.4 = (f32[8,6144]{1,0:T(8,128)S(1)}, f32[8,6144]{1,0:T(8,128)S(1)}, u32[]{:S(2)}, u32[]{:S(2)}) collective-permute-start(f32[8,6144]{1,0:T(8,128)S(1)} %shard_map.29.refs_0_), channel_id=1, source_target_pairs={{0,4},{4,0},{8,12},{12,8},{16,20},{20,16},{24,28},{28,24},{1,5},{5... | collective-permute-start | bytes 589832 | tf_op jit(solution)/shard_map/ppermute | solution.py:295
  15.6 7.2 %collective-permute-start.8 = (f32[8,6144]{1,0:T(8,128)S(1)}, f32[8,6144]{1,0:T(8,128)S(1)}, u32[]{:S(2)}, u32[]{:S(2)}) collective-permute-start(f32[8,6144]{1,0:T(8,128)S(1)} %collective-permute-done.7.refs_4_), channel_id=1, source_target_pairs={{0,4},{4,0},{8,12},{12,8},{16,20},{20,16},{24,28},{28,24},{1,5},{5... | collective-permute-start | bytes 589832 | tf_op jit(solution)/shard_map/ppermute | solution.py:295
  19.8 3.0 %collective-permute-start.6 = (f32[8,6144]{1,0:T(8,128)S(1)}, f32[8,6144]{1,0:T(8,128)S(1)}, u32[]{:S(2)}, u32[]{:S(2)}) collective-permute-start(f32[8,6144]{1,0:T(8,128)S(1)} %collective-permute-done.5.refs_2_), channel_id=1, source_target_pairs={{0,4},{4,0},{8,12},{12,8},{16,20},{20,16},{24,28},{28,24},{1,5},{5... | collective-permute-start | bytes 589832 | tf_op jit(solution)/shard_map/ppermute | solution.py:295
  19.8 4.1 %collective-permute-start.3 = (f32[8,6144]{1,0:T(8,128)S(1)}, f32[8,6144]{1,0:T(8,128)S(1)}, u32[]{:S(2)}, u32[]{:S(2)}) collective-permute-start(f32[8,6144]{1,0:T(8,128)S(1)} %collective-permute-done.2.one_ref), channel_id=1, source_target_pairs={{0,4},{4,0},{8,12},{12,8},{16,20},{20,16},{24,28},{28,24},{1,5},{5... | collective-permute-start | bytes 589832 | tf_op jit(solution)/shard_map/ppermute | solution.py:295
  24.8 3.4 %collective-permute-start.11 = (f32[32,128]{1,0:T(8,128)S(1)}, f32[32,128]{1,0:T(8,128)S(1)}, u32[]{:S(2)}, u32[]{:S(2)}) collective-permute-start(f32[32,128]{1,0:T(8,128)S(1)} %get-tuple-element.11.refs_0_), channel_id=1, source_target_pairs={{0,7},{1,6},{2,5},{3,4},{4,3},{5,2},{6,1},{7,0},{8,15},{9,14},{10,... | collective-permute-start | bytes 49160 | tf_op jit(solution)/shard_map/ppermute | solution.py:285
  26.8 3.2 %collective-permute-start.10 = (f32[32,128]{1,0:T(8,128)S(1)}, f32[32,128]{1,0:T(8,128)S(1)}, u32[]{:S(2)}, u32[]{:S(2)}) collective-permute-start(f32[32,128]{1,0:T(8,128)S(1)} %get-tuple-element.11.refs_0_), channel_id=1, source_target_pairs={{0,5},{1,4},{2,7},{3,6},{4,1},{5,0},{6,3},{7,2},{8,13},{9,12},{10,... | collective-permute-start | bytes 49160 | tf_op jit(solution)/shard_map/ppermute | solution.py:285
  28.1 4.1 %collective-permute-start.9 = (f32[32,128]{1,0:T(8,128)S(1)}, f32[32,128]{1,0:T(8,128)S(1)}, u32[]{:S(2)}, u32[]{:S(2)}) collective-permute-start(f32[32,128]{1,0:T(8,128)S(1)} %get-tuple-element.11.refs_0_), channel_id=1, source_target_pairs={{0,6},{1,7},{2,4},{3,5},{4,2},{5,3},{6,0},{7,1},{8,14},{9,15},{10,... | collective-permute-start | bytes 49160 | tf_op jit(solution)/shard_map/ppermute | solution.py:285
